TPU v7x, 32 devices: a whole 2x2x4 slice. The times are simulated.
32 devices in a mesh: tm: 8 (over y, x, core), space: 4 (over z).
Axes of the slice: x: 2, y: 2, z: 4, core: 2. Of those that a mesh axis runs over, the one named last changes fastest.
Arguments:
- clip: bfloat16 [128, 128, 768], P('tm', 'space'), may hold values from -160 to 160
- w_spatial: bfloat16 [4, 768, 768], replicated, may hold values from -4 to 4
- w_temporal: bfloat16 [4, 768, 768], replicated, may hold values from -4 to 4
Outputs:
- result: bfloat16 [128, 128, 768], P('tm', 'space')
All inputs are finite; a program needn't handle non-finite values.
Results may differ from a plain program's by a relative error of at most 0.011.
Values may be sent and summed in bfloat16 or wider, within the bound.
No kernel may reach another device: no remote copies, remote signals or barrier semaphores. Data moves between devices by JAX's collectives and lax.ppermute only.
A program may use at most 128 MiB of HBM per device.

v0:
```python
import math

import jax
import jax.numpy as jnp
from jax import lax
from jax.sharding import PartitionSpec as P

HEAD = 64


def rms_norm(values):
    wide = values.astype(jnp.float32)
    return (wide * lax.rsqrt(jnp.mean(wide * wide, axis=-1, keepdims=True) + 1e-06)).astype(
        jnp.bfloat16
    )


def project_three(normed, weights):
    width = normed.shape[-1]
    flat = normed.reshape(-1, width)
    stacked = jnp.einsum(
        "rd,jde->jre", flat, weights[:3], preferred_element_type=jnp.float32
    ).astype(jnp.bfloat16)
    return (
        stacked[0].reshape(normed.shape),
        stacked[1].reshape(normed.shape),
        stacked[2].reshape(normed.shape),
    )


def out_project(mixed, weight):
    width = mixed.shape[-1]
    return jnp.dot(mixed.reshape(-1, width), weight, preferred_element_type=jnp.float32).reshape(
        mixed.shape
    )


def attend_frame(parts):
    query, key, value = parts
    count, width = query.shape
    heads = width // HEAD
    qh = query.reshape(count, heads, HEAD)
    kh = key.reshape(count, heads, HEAD)
    vh = value.reshape(count, heads, HEAD)
    scores = jnp.einsum("qhd,khd->hqk", qh, kh, preferred_element_type=jnp.float32) * (
        1.0 / math.sqrt(HEAD)
    )
    largest = jnp.max(scores, axis=-1, keepdims=True)
    expo = jnp.exp(scores - largest)
    weights = (expo / jnp.sum(expo, axis=-1, keepdims=True)).astype(jnp.bfloat16)
    mixed = jnp.einsum("hqk,khd->qhd", weights, vh, preferred_element_type=jnp.float32)
    return mixed.astype(jnp.bfloat16).reshape(count, width)


def frame_block(parts):
    inner = (parts[0][0], parts[1][0], parts[2][0])
    return lax.map(attend_frame, inner)[None]


def on_device(clip, w_spatial, w_temporal):
    frames, toks, width = clip.shape
    heads = width // HEAD
    space_count = lax.axis_size("space")
    frame_shape = (space_count, frames // space_count, toks, width)
    normed = rms_norm(clip)
    smix = frame_block(
        project_three(
            lax.all_to_all(
                normed.reshape(frame_shape), "space", split_axis=0, concat_axis=2, tiled=True
            ),
            w_spatial,
        )
    )
    smix = lax.all_to_all(smix, "space", split_axis=2, concat_axis=0, tiled=True).reshape(
        frames, toks, width
    )
    after_space = (clip.astype(jnp.float32) + out_project(smix, w_spatial[3])).astype(jnp.bfloat16)
    tnormed = rms_norm(after_space)
    tq, tk, tv = project_three(tnormed, w_temporal)
    first_frame = lax.axis_index("tm") * frames
    qh = tq.reshape(frames, toks, heads, HEAD)
    query_pos = first_frame + jnp.arange(frames, dtype=jnp.int32)
    running = jnp.full((frames, toks, heads), -1e30, jnp.float32)
    key_piece = lax.all_gather(tk, "tm", axis=0, tiled=True)
    value_piece = lax.all_gather(tv, "tm", axis=0, tiled=True)
    count = key_piece.shape[0]
    kh = key_piece.reshape(count, toks, heads, HEAD)
    vh = value_piece.reshape(count, toks, heads, HEAD)
    scores = jnp.einsum("fphd,gphd->fphg", qh, kh, preferred_element_type=jnp.float32) * (
        1.0 / math.sqrt(HEAD)
    )
    key_pos = jnp.arange(count, dtype=jnp.int32)
    allowed = (key_pos[None, :] <= query_pos[:, None])[:, None, None, :]
    scores = jnp.where(allowed, scores, -1e30)
    newmax = jnp.maximum(running, jnp.max(scores, axis=-1))
    expo = jnp.where(allowed, jnp.exp(scores - newmax[..., None]), 0.0)
    total = jnp.sum(expo, axis=-1)
    acc = jnp.einsum("fphg,gphd->fphd", expo, vh.astype(jnp.float32))
    running, total, acc = (newmax, total, acc)
    tmix = (acc / total[..., None]).reshape(frames, toks, width).astype(jnp.bfloat16)
    return (after_space.astype(jnp.float32) + out_project(tmix, w_temporal[3])).astype(jnp.bfloat16)


def solution(mesh):
    placed = (P("tm", "space", None), P(), P())
    return jax.shard_map(
        on_device, mesh=mesh, in_specs=placed, out_specs=P("tm", "space", None), check_vma=False
    )
```

profile of v0, /device:TPU:0, one launch (start us, length us, event | category | flops | bytes accessed | tf_op | source)
XLA Modules:
  0.0 201.8 jit_solution(4200673567555098672)
XLA Ops:
  6.5 1.4 fusion.17
  7.9 2.2 %fusion.18 = bf16[16,32,768]{2,1,0:T(8,128)(2,1)} fusion(bf16[16,32,768]{2,1,0:T(8,128)(2,1)} %param.5, f32[16,32]{1,0:T(8,128)S(1)} %add_rsqrt_fusion.1), kind=kLoop, calls=%fused_computation.32 | loop fusion | flops 1179648 | bytes 1574912 | tf_op jit(solution)/shard_map/convert_element_type | solution.py:13
  10.1 6.3 %all-to-all-start = ((bf16[4,4,32,768]{3,2,1,0:T(8,128)(2,1)}), bf16[4,4,32,768]{3,2,1,0:T(8,128)(2,1)S(1)}, u32[]{:S(2)}, u32[]{:S(2)}) async-start(bf16[4,4,32,768]{3,2,1,0:T(8,128)(2,1)} %bitcast.5), calls=%async_computation | async-start | bytes 1572864 | tf_op jit(solution)/shard_map/all_to_all | solution.py:68
  16.4 20.1 %all-to-all-done = bf16[4,4,32,768]{3,2,1,0:T(8,128)(2,1)S(1)} async-done(((bf16[4,4,32,768]{3,2,1,0:T(8,128)(2,1)}), bf16[4,4,32,768]{3,2,1,0:T(8,128)(2,1)S(1)}, u32[]{:S(2)}, u32[]{:S(2)}) %all-to-all-start) | async-done | bytes 786464 | tf_op jit(solution)/shard_map/all_to_all | solution.py:68
  36.6 4.0 %convert_bitcast_fusion.1 = bf16[3,512,768]{2,1,0:T(8,128)(2,1)S(1)} fusion(bf16[512,768,1]{1,0,2:T(8,128)(2,1)S(1)} %bitcast.106, bf16[4,768,768]{2,1,0:T(8,128)(2,1)} %param.6), kind=kOutput, calls=%fused_computation.28 | convolution fusion | flops 1813118976 | bytes 6684672 | tf_op jit(solution)/shard_map/rd,jde->jre/dot_general | solution.py:21
  40.8 9.5 %while.10 = (s32[]{:T(128)}, bf16[4,128,768]{1,2,0:T(8,128)(2,1)}, bf16[4,128,768]{2,1,0:T(8,128)(2,1)S(1)}, bf16[4,128,768]{2,1,0:T(8,128)(2,1)S(1)}, bf16[4,128,768]{2,1,0:T(8,128)(2,1)S(1)}, /*index=5*/s32[]{:T(128)}) while((s32[]{:T(128)}, bf16[4,128,768]{1,2,0:T(8,128)(2,1)}, bf16[4,128,768]{2,1,0:T(8,128)(2,1)S(1)}, ...), condition=%wide.region_4.5_spmd, body=%wide.region_1.4_spmd.sunk | while | flops 76973824 | bytes 5517901 | solution.py:57
  41.5 0.4 fusion.65
  42.5 0.7 constant_dynamic-update-slice_fusion.2
  43.9 0.4 fusion.65
  44.8 0.7 constant_dynamic-update-slice_fusion.2
  46.2 0.4 fusion.65
  47.2 0.7 constant_dynamic-update-slice_fusion.2
  48.6 0.4 fusion.65
  49.5 0.7 constant_dynamic-update-slice_fusion.2
  50.2 1.6 copy.29
  51.9 22.1 %all_to_all.30 = bf16[1,4,128,768]{3,1,0,2:T(4,128)(2,1)S(1)} all-to-all(bf16[1,4,128,768]{3,1,0,2:T(4,128)(2,1)S(1)} %bitcast.103), channel_id=1, replica_groups=mesh['tm'=8,'space'=4] {'space'}, dimensions={2} | all-to-all | bytes 1572864 | tf_op jit(solution)/shard_map/all_to_all | solution.py:74
  74.1 2.2 %fusion.20 = (f32[16,32]{1,0:T(8,128)S(1)}, bf16[16,32,768]{2,1,0:T(8,128)(2,1)S(1)}) fusion(bf16[16,32,768]{2,1,0:T(8,128)(2,1)S(1)} %bitcast.105, bf16[4,768,768]{2,1,0:T(8,128)(2,1)} %param.6, bf16[16,32,768]{2,1,0:T(8,128)(2,1)S(1)} %copy-done), kind=kOutput, calls=%fused_computation.34 | convolution fusion | flops 606338560 | bytes 3540992 | tf_op jit(solution)/shard_map/dot_general | solution.py:33
  76.5 0.7 copy-done.1
  77.1 4.0 %convert_bitcast_fusion = bf16[3,512,768]{2,1,0:T(8,128)(2,1)S(1)} fusion(bf16[512,768,1]{1,0,2:T(8,128)(2,1)S(1)} %bitcast.107, bf16[4,768,768]{2,1,0:T(8,128)(2,1)} %param.7), kind=kOutput, calls=%fused_computation.27 | convolution fusion | flops 1813118976 | bytes 6684672 | tf_op jit(solution)/shard_map/rd,jde->jre/dot_general | solution.py:21
  81.1 1.3 fusion.38
  82.7 0.5 all-gather.3.cloned.1.call-update
  83.3 2.2 %reshape_reshape_squeeze.3 = bf16[16,32,12,64]{3,2,1,0:T(8,128)(2,1)} reshape(bf16[1,512,768]{2,1,0:T(8,128)(2,1)S(1)} %get-tuple-element.61) | data formatting | bytes 1572864 | tf_op jit(solution)/shard_map/reshape;reshape;squeeze | solution.py:81
  85.6 41.7 %all-gather.5.cloned.1.call-done = bf16[128,32,768]{2,1,0:T(8,128)(2,1)} async-done(((bf16[16,32,768]{2,1,0:T(8,128)(2,1)}), bf16[128,32,768]{2,1,0:T(8,128)(2,1)}) %all-gather.5.cloned.1.call-update) | async-done | bytes 6291472 | tf_op jit(solution)/shard_map/all_gather | solution.py:84
  127.2 9.0 %copy.33 = bf16[128,32,768]{0,2,1:T(8,128)(2,1)} copy(bf16[128,32,768]{2,1,0:T(8,128)(2,1)} %all-gather.5.cloned.1.call-done) | data formatting | bytes 12582912 | tf_op jit(solution)/shard_map/all_gather | solution.py:84
  136.2 5.7 %fusion.10 = (f32[16,32,12]{0,2,1:T(8,128)S(1)}, f32[32,12,128,16]{2,3,1,0:T(8,128)S(1)}) fusion(pred[16,128]{1,0:T(8,128)(4,1)S(1)} %iota_compare_fusion, bf16[128,32,12,64]{0,3,2,1:T(8,128)(2,1)} %bitcast.89, bf16[16,32,12,64]{3,2,1,0:T(8,128)(2,1)} %reshape_reshape_squeeze.3), kind=kOutput, calls=%fused_computation.20 | convolution fusion | flops 103016448 | bytes 10250240 | tf_op jit(solution)/shard_map/fphd,gphd->fphg/dot_general | solution.py:89
  142.0 2.6 %fusion.11 = f32[16,32,12]{0,2,1:T(8,128)} fusion(f32[32,12,128,16]{2,3,1,0:T(8,128)S(1)} %get-tuple-element.69, f32[16,32,12]{0,2,1:T(8,128)S(1)} %broadcast_maximum_fusion, pred[16,128]{1,0:T(8,128)(4,1)S(1)} %iota_compare_fusion), kind=kLoop, calls=%fused_computation.29 | loop fusion | flops 3926016 | bytes 3196928 | tf_op jit(solution)/shard_map/reduce_sum | solution.py:97
  144.6 30.1 %all-gather.3.cloned.1.call-done = bf16[128,32,768]{2,1,0:T(8,128)(2,1)} async-done(((bf16[16,32,768]{2,1,0:T(8,128)(2,1)}), bf16[128,32,768]{2,1,0:T(8,128)(2,1)}) %all-gather.3.cloned.1.call-update) | async-done | bytes 6291472 | tf_op jit(solution)/shard_map/all_gather | solution.py:85
  174.7 9.0 %copy.32 = bf16[128,32,768]{0,2,1:T(8,128)(2,1)} copy(bf16[128,32,768]{2,1,0:T(8,128)(2,1)} %all-gather.3.cloned.1.call-done) | data formatting | bytes 12582912 | tf_op jit(solution)/shard_map/all_gather | solution.py:85
  183.7 5.5 %fusion.9 = bf16[16,32,12,64]{3,0,2,1:T(8,128)(2,1)S(1)} fusion(f32[16,32,12]{0,2,1:T(8,128)} %fusion.11, bf16[128,32,12,64]{0,3,2,1:T(8,128)(2,1)} %bitcast.94, f32[32,12,128,16]{2,3,1,0:T(8,128)S(1)} %get-tuple-element.69, f32[16,32,12]{0,2,1:T(8,128)S(1)} %broadcast_maximum_fusion, pred[16,128]{1,0:T(8,128)(4,1)S(1)} %iota_compare_fusion), kind=kOutput, calls=%fused_computation.17 | convolution fusion | flops 104595456 | bytes 10274816 | tf_op jit(solution)/shard_map/fphg,gphd->fphd/dot_general | solution.py:98
  189.3 0.5 copy.35
  189.8 2.0 %convert_element_type.60 = bf16[16,32,768]{2,1,0:T(8,128)(2,1)} reshape(bf16[16,32,12,64]{3,2,1,0:T(8,128)(2,1)S(1)} %copy.35) | data formatting | bytes 1572864 | tf_op jit(solution)/shard_map/convert_element_type | solution.py:100
  191.8 3.2 %fusion.22 = bf16[16,32,768]{2,1,0:T(8,128)(2,1)} fusion(bf16[16,32,768]{2,1,0:T(8,128)(2,1)S(1)} %copy-done.2, bf16[16,32,768]{2,1,0:T(8,128)(2,1)} %convert_element_type.60, bf16[4,768,768]{2,1,0:T(8,128)(2,1)} %param.7), kind=kOutput, calls=%fused_computation.36 | convolution fusion | flops 605159424 | bytes 3538944 | tf_op jit(solution)/shard_map/dot_general | solution.py:33
  (47 shorter events, 5.7 us)
Async XLA Ops:
  10.1 26.4 %all-to-all-start = ((bf16[4,4,32,768]{3,2,1,0:T(8,128)(2,1)}), bf16[4,4,32,768]{3,2,1,0:T(8,128)(2,1)S(1)}, u32[]{:S(2)}, u32[]{:S(2)}) async-start(bf16[4,4,32,768]{3,2,1,0:T(8,128)(2,1)} %bitcast.5), calls=%async_computation | async-start | bytes 1572864 | tf_op jit(solution)/shard_map/all_to_all | solution.py:68
  16.4 110.8 %all-gather.5.cloned.1.call-start = ((), (), s32[]{:S(2)}) async-start(), calls=%async_computation.3 | async-start | bytes 7077888 | tf_op jit(solution)/shard_map/all_gather | solution.py:84
  50.2 23.8 %copy-start = (bf16[16,32,768]{2,1,0:T(8,128)(2,1)S(1)}, bf16[16,32,768]{2,1,0:T(8,128)(2,1)}, u32[]{:S(2)}) copy-start(bf16[16,32,768]{2,1,0:T(8,128)(2,1)} %param.5) | copy-start | bytes 2359300
  76.2 0.9 copy-start.1
  82.5 92.2 %all-gather.3.cloned.1.call-start = ((), (), s32[]{:S(2)}) async-start(), calls=%async_computation.2 | async-start | bytes 7077888 | tf_op jit(solution)/shard_map/all_gather | solution.py:85
  189.3 2.6 %copy-start.2 = (bf16[16,32,768]{2,1,0:T(8,128)(2,1)S(1)}, bf16[16,32,768]{2,1,0:T(8,128)(2,1)}, u32[]{:S(2)}) copy-start(bf16[16,32,768]{2,1,0:T(8,128)(2,1)} %copy-done.1) | copy-start | bytes 2359300
Sparse Core Ops, SparseCore 0:
  82.6 44.5 all-gather.4
  129.1 45.5 all-gather.2
where the time goes:
time: 203 us; the launch traced here: 202 us
  waiting for transfers between devices  92.4 us (46%)
  local copies, waits for them, and re-layouts  31.7 us (16%)
  matrix products  29 us (14%)
  blocking collectives  22.1 us (11%)
  between operations  13.6 us (7%)
  starting transfers between devices  6.54 us (3%)
  other arithmetic  6.45 us (3%)
    all_gather x1, waiting for transfers between devices, on_device(): key_piece = lax.all_gather(tk, 'tm', axis=0, tiled=True)  41.7 us
    all_gather x1, waiting for transfers between devices, on_device(): value_piece = lax.all_gather(tv, 'tm', axis=0, tiled=True)  30.1 us
    all_to_all x1, blocking collectives, on_device(): lax.all_to_all(smix, 'space', split_axis=2, concat_axis=0, tiled=True)  22.1 us
    all_to_all x1, waiting for transfers between devices, on_device(): lax.all_to_all(normed.reshape(frame_shape), 'space', split_axis=0, concat...  20.1 us
    all_gather x1, local copies, waits for them, and re-layouts, on_device(): value_piece = lax.all_gather(tv, 'tm', axis=0, tiled=True)  9.04 us
    all_gather x1, local copies, waits for them, and re-layouts, on_device(): key_piece = lax.all_gather(tk, 'tm', axis=0, tiled=True)  8.98 us
    dot_general x2, matrix products, project_three(): jnp.einsum('rd,jde->jre', flat, weights[:3], preferred_element_type=jnp.f...  8.01 us
    all_to_all x1, starting transfers between devices, on_device(): lax.all_to_all(normed.reshape(frame_shape), 'space', split_axis=0, concat...  6.32 us
  transfers between devices with their start and end apart: 3, of which 3 were waited for; matrix products, arithmetic and copies ran while one was open for 10% of the time, Pallas kernels for 0%

commit v1 on v0

v1 whole, which is shorter than its diff:
```python
import math

import jax
import jax.numpy as jnp
from jax import lax
from jax.experimental import pallas as pl
from jax.experimental.pallas import tpu as pltpu
from jax.sharding import PartitionSpec as P

HEAD = 64
PAIR = 2 * HEAD
SCALE = math.log2(math.e) / math.sqrt(HEAD)
F32, BF16 = jnp.float32, jnp.bfloat16
VMEM = pl.BlockSpec(memory_space=pltpu.VMEM)


def dot(a, b):
    return jnp.dot(a, b, preferred_element_type=F32)


def rms_norm(values):
    wide = values.astype(F32)
    return (wide * lax.rsqrt(jnp.mean(wide * wide, axis=-1, keepdims=True) + 1e-06)).astype(BF16)


def halves(rows):
    first = lax.broadcasted_iota(jnp.int32, (rows, PAIR), 1) < HEAD
    one, zero = jnp.ones((rows, PAIR), F32), jnp.zeros((rows, PAIR), F32)
    return jnp.where(first, one, zero).astype(BF16), jnp.where(first, zero, one).astype(BF16)


def attend_pair(query, key, value, masks, allowed):
    rows = query.shape[0]
    low, high = masks
    both = jnp.concatenate([query * low, query * high], axis=0)
    scores = lax.dot_general(both, key, (((1,), (1,)), ((), ())), preferred_element_type=F32)
    if allowed is not None:
        scores = jnp.where(allowed, scores, -1e30)
    largest = jnp.max(scores, axis=-1, keepdims=True)
    expo = jnp.exp2((scores - largest) * SCALE).astype(BF16)
    side = jnp.concatenate([expo[:rows], expo[rows:]], axis=1)
    right = jnp.concatenate(
        [
            jnp.concatenate([value * low, low], axis=1),
            jnp.concatenate([value * high, high], axis=1),
        ],
        axis=0,
    )
    mixed = dot(side, right)
    return (mixed[:, :PAIR] / mixed[:, PAIR:]).astype(BF16)


def space_kernel(clip_ref, w_ref, out_ref, qkv_ref, mix_ref, wide_ref, send_ref):
    count, frames, toks, width = clip_ref.shape
    rows = count * toks
    groups = out_ref.shape[0]
    share = rows // groups
    masks = halves(rows)
    clip = [clip_ref[:, f].reshape(rows, width) for f in range(frames)]
    normed = jnp.concatenate([rms_norm(c) for c in clip], axis=0)
    for j in range(3):
        qkv_ref[j] = dot(normed, w_ref[j]).astype(BF16)
    for f in range(frames):
        at = pl.ds(f * rows, rows)
        for p in range(width // PAIR):
            cols = pl.ds(p * PAIR, PAIR)
            mix_ref[at, cols] = attend_pair(
                qkv_ref[0, at, cols], qkv_ref[1, at, cols], qkv_ref[2, at, cols], masks, None
            )
    out = dot(mix_ref[...], w_ref[3])
    for f in range(frames):
        after = out[f * rows : (f + 1) * rows] + clip[f].astype(F32)
        for p in range(width // PAIR):
            wide_ref[p, pl.ds(f * rows, rows), :] = after[:, p * PAIR : (p + 1) * PAIR]
    for p in range(width // PAIR):
        for f in range(frames):
            for t in range(share):
                send_ref[p, pl.ds(f * share + t, groups, stride=frames * share), :] = wide_ref[
                    p, pl.ds(f * rows + t, groups, stride=share), :
                ]
        out_ref[:, :, pl.ds(p * PAIR, PAIR)] = (
            send_ref[p].astype(BF16).reshape(groups, frames * share, PAIR)
        )


def time_kernel(x_ref, w_ref, out_ref, qkv_ref, mix_ref, wide_ref, *, toks):
    space, tm, block, width = x_ref.shape
    rows = space * tm * block
    frames = rows // toks
    pairs = width // PAIR
    masks = halves(frames)
    x = jnp.concatenate([x_ref[s, m] for m in range(tm) for s in range(space)], axis=0)
    normed = rms_norm(x)
    for j in range(3):
        out = dot(normed, w_ref[j])
        for p in range(pairs):
            qkv_ref[j, p] = out[:, p * PAIR : (p + 1) * PAIR]
    order = lax.broadcasted_iota(jnp.int32, (2 * frames, frames), 0) % frames
    allowed = lax.broadcasted_iota(jnp.int32, (2 * frames, frames), 1) <= order
    for t in range(toks):
        at = pl.ds(t, frames, stride=toks)
        for p in range(pairs):
            mix_ref[pl.ds(t * frames, frames), pl.ds(p * PAIR, PAIR)] = attend_pair(
                qkv_ref[0, p, at, :].astype(BF16),
                qkv_ref[1, p, at, :].astype(BF16),
                qkv_ref[2, p, at, :].astype(BF16),
                masks,
                allowed,
            )
    out = dot(mix_ref[...], w_ref[3])
    for p in range(pairs):
        cols = slice(p * PAIR, (p + 1) * PAIR)
        for t in range(toks):
            wide_ref[p, pl.ds(t, frames, stride=toks), :] = out[t * frames : (t + 1) * frames, cols]
        out_ref[:, pl.ds(p * PAIR, PAIR)] = (wide_ref[p] + x[:, cols].astype(F32)).astype(BF16)


def place_kernel(x_ref, out_ref, wide_ref, flat_ref):
    sources, block, width = x_ref.shape
    frames, toks, _ = out_ref.shape
    share = block // frames
    for p in range(width // PAIR):
        cols = pl.ds(p * PAIR, PAIR)
        wide_ref[p] = x_ref[:, :, cols].astype(F32).reshape(sources * block, PAIR)
        for s in range(sources):
            for t in range(share):
                flat_ref[p, pl.ds(s * share + t, frames, stride=toks), :] = wide_ref[
                    p, pl.ds(s * block + t, frames, stride=share), :
                ]
        out_ref[:, :, cols] = flat_ref[p].astype(BF16).reshape(frames, toks, PAIR)


def params():
    return pltpu.CompilerParams(vmem_limit_bytes=56 * 1024 * 1024)


def on_device(clip, w_spatial, w_temporal):
    frames, toks, width = clip.shape
    rows = frames * toks
    tm, space = lax.axis_size("tm"), lax.axis_size("space")
    share = toks // tm
    lanes = pltpu.VMEM((width // PAIR, rows, PAIR), F32)
    parts = lax.all_to_all(
        clip.reshape(space, rows // space, width), "space", split_axis=0, concat_axis=0, tiled=True
    ).reshape(space, frames // space, toks, width)
    after = pl.pallas_call(
        space_kernel,
        out_shape=jax.ShapeDtypeStruct((space * tm, rows // (space * tm), width), BF16),
        in_specs=[VMEM, VMEM],
        out_specs=VMEM,
        scratch_shapes=[
            pltpu.VMEM((3, rows, width), BF16),
            pltpu.VMEM((rows, width), BF16),
            lanes,
            lanes,
        ],
        compiler_params=params(),
        name="spatial",
    )(parts, w_spatial)
    after = lax.all_to_all(
        after, ("space", "tm"), split_axis=0, concat_axis=0, tiled=True
    )
    result = pl.pallas_call(
        lambda *refs: time_kernel(*refs, toks=share),
        out_shape=jax.ShapeDtypeStruct((rows, width), BF16),
        in_specs=[VMEM, VMEM],
        out_specs=VMEM,
        scratch_shapes=[
            pltpu.VMEM((3, width // PAIR, rows, PAIR), F32),
            pltpu.VMEM((rows, width), BF16),
            lanes,
        ],
        compiler_params=params(),
        name="temporal",
    )(after.reshape(space, tm, rows // (space * tm), width), w_temporal)
    result = lax.all_to_all(
        result.reshape(tm, rows // tm, width), "tm", split_axis=0, concat_axis=0, tiled=True
    )
    return pl.pallas_call(
        place_kernel,
        out_shape=jax.ShapeDtypeStruct((frames, toks, width), BF16),
        in_specs=[VMEM],
        out_specs=VMEM,
        scratch_shapes=[lanes, lanes],
        compiler_params=params(),
        name="place",
    )(result)


def solution(mesh):
    placed = (P("tm", "space", None), P(), P())
    return jax.shard_map(
        on_device, mesh=mesh, in_specs=placed, out_specs=P("tm", "space", None), check_vma=False
    )
```

time: 203 us -> 89.1 us (0.44)
  waiting for transfers between devices: 92.4 us -> 0 us
  blocking collectives: 22.1 us -> 67.7 us
  local copies, waits for them, and re-layouts: 31.7 us -> 0 us
  matrix products: 29 us -> 0 us
  Pallas kernels: 0 us -> 21 us
  between operations: 13.6 us -> 0.01 us
  starting transfers between devices: 6.54 us -> 0 us
  other arithmetic: 6.45 us -> 0 us
    all_gather x2 -> x0, waiting for transfers between devices: 71.8 us -> none  [the longest x1 41.7 us: on_device(): key_piece = lax.all_gather(tk, 'tm', axis=0, tiled=True)]
    all_to_all x1 -> x3, blocking collectives: 22.1 us -> 67.7 us  [the longest x1 26.5 us: on_device(): lax.all_to_all(clip.reshape(space, rows // space, width), 'space', split_...]
    dot_general x14 -> x0, matrix products: 27.2 us -> none  [the longest x2 8.01 us: project_three(): jnp.einsum('rd,jde->jre', flat, weights[:3], preferred_element_type=jnp.f...]
    pallas_call x0 -> x3, Pallas kernels: none -> 21 us  [the longest x1 8.87 us: on_device(): pl.pallas_call(space_kernel, out_shape=jax.ShapeDtypeStruct((space * tm,...]
    all_to_all x1 -> x0, waiting for transfers between devices: 20.1 us -> none  [on_device(): lax.all_to_all(normed.reshape(frame_shape), 'space', split_axis=0, concat...]
    all_gather x2 -> x0, local copies, waits for them, and re-layouts: 18 us -> none  [the longest x1 9.04 us: on_device(): value_piece = lax.all_gather(tv, 'tm', axis=0, tiled=True)]
    all_to_all x1 -> x0, starting transfers between devices: 6.32 us -> none  [on_device(): lax.all_to_all(normed.reshape(frame_shape), 'space', split_axis=0, concat...]
    reduce_sum x2 -> x0, other arithmetic: 3.93 us -> none  [the longest x1 2.58 us: on_device(): total = jnp.sum(expo, axis=-1)]
  transfers between devices with their start and end apart: 3 -> 0, of which waited for: 3 -> 0; matrix products, arithmetic and copies ran while one was open for 10% -> 0% of each run, Pallas kernels for 0% -> 0%
where the time goes in v1:
time: 89.1 us; the launch traced here: 88.7 us
  blocking collectives  67.7 us (76%)
  Pallas kernels  21 us (24%)
    all_to_all x1, blocking collectives, on_device(): lax.all_to_all(clip.reshape(space, rows // space, width), 'space', split_...  26.5 us
    all_to_all x1, blocking collectives, on_device(): lax.all_to_all(after, ('space', 'tm'), split_axis=0, concat_axis=0, tiled...  24.4 us
    all_to_all x1, blocking collectives, on_device(): lax.all_to_all(result.reshape(tm, rows // tm, width), 'tm', split_axis=0,...  16.7 us
    pallas_call x1, Pallas kernels, on_device(): pl.pallas_call(space_kernel, out_shape=jax.ShapeDtypeStruct((space * tm,...  8.87 us
    pallas_call x1, Pallas kernels, on_device(): pl.pallas_call(lambda *refs: time_kernel(*refs, toks=share), out_shape=ja...  8.58 us
    pallas_call x1, Pallas kernels, on_device(): pl.pallas_call(place_kernel, out_shape=jax.ShapeDtypeStruct((frames, toks...  3.51 us

profile of v1, /device:TPU:0, one launch (start us, length us, event | category | flops | bytes accessed | tf_op | source)
XLA Modules:
  0.0 88.7 jit_solution(9768316156176954181)
XLA Ops:
  0.0 26.5 %all_to_all.15 = bf16[4,128,768]{2,1,0:T(8,128)(2,1)} all-to-all(bf16[4,128,768]{2,1,0:T(8,128)(2,1)} %bitcast.7), channel_id=1, replica_groups=mesh['tm'=8,'space'=4] {'space'}, dimensions={0} | all-to-all | bytes 1572864 | tf_op jit(solution)/shard_map/all_to_all | solution.py:143
  26.5 8.9 %spatial.1 = bf16[32,16,768]{2,1,0:T(8,128)(2,1)} custom-call(bf16[4,4,32,768]{3,2,1,0:T(8,128)(2,1)} %bitcast.6, bf16[4,768,768]{2,1,0:T(8,128)(2,1)} %w_ref.1), custom_call_target="tpu_custom_call" | custom-call | tf_op jit(solution)/shard_map/spatial/pallas_call | solution.py:146
  35.4 24.4 %all_to_all.16 = bf16[32,16,768]{2,1,0:T(8,128)(2,1)} all-to-all(bf16[32,16,768]{2,1,0:T(8,128)(2,1)} %spatial.1), channel_id=1, replica_groups=mesh['tm'=8,'space'=4] {'space','tm'}, dimensions={0} | all-to-all | bytes 1572864 | tf_op jit(solution)/shard_map/all_to_all | solution.py:160
  59.8 8.6 %temporal.1 = bf16[512,768]{1,0:T(8,128)(2,1)} custom-call(bf16[4,8,16,768]{3,2,1,0:T(8,128)(2,1)} %bitcast.4, bf16[4,768,768]{2,1,0:T(8,128)(2,1)} %refs_1_.1), custom_call_target="tpu_custom_call" | custom-call | tf_op jit(solution)/shard_map/temporal/pallas_call | solution.py:163
  68.4 16.7 %all_to_all.17.x_ref = bf16[8,64,768]{2,1,0:T(8,128)(2,1)} all-to-all(bf16[8,64,768]{2,1,0:T(8,128)(2,1)} %bitcast.5), channel_id=1, replica_groups=mesh['tm'=8,'space'=4] {'tm'}, dimensions={0} | all-to-all | bytes 1572864 | tf_op jit(solution)/shard_map/all_to_all | solution.py:176
  85.2 3.5 %place.1 = bf16[16,32,768]{2,1,0:T(8,128)(2,1)} custom-call(bf16[8,64,768]{2,1,0:T(8,128)(2,1)} %all_to_all.17.x_ref), custom_call_target="tpu_custom_call" | custom-call | tf_op jit(solution)/shard_map/place/pallas_call | solution.py:179

commit v2 on v1

v2 whole, which is shorter than its diff:
```python
import functools
import math

import jax
import jax.numpy as jnp
from jax import lax
from jax.experimental import pallas as pl
from jax.experimental.pallas import tpu as pltpu
from jax.sharding import PartitionSpec as P

HEAD = 64
PAIR = 2 * HEAD
SCALE = math.log2(math.e) / math.sqrt(HEAD)
F32, BF16 = jnp.float32, jnp.bfloat16
MIB = 1024 * 1024


def dot(a, b):
    return jnp.dot(a, b, preferred_element_type=F32)


def rms_norm(values):
    wide = values.astype(F32)
    return (wide * lax.rsqrt(jnp.mean(wide * wide, axis=-1, keepdims=True) + 1e-06)).astype(BF16)


def halves(rows):
    first = lax.broadcasted_iota(jnp.int32, (rows, PAIR), 1) < HEAD
    one, zero = jnp.ones((rows, PAIR), F32), jnp.zeros((rows, PAIR), F32)
    return jnp.where(first, one, zero).astype(BF16), jnp.where(first, zero, one).astype(BF16)


def reorder(values, source):
    rows = values.shape[0]
    wanted = source(lax.broadcasted_iota(jnp.int32, (rows, 1), 0))
    place = lax.broadcasted_iota(jnp.int32, (rows, rows), 1)
    chosen = jnp.where(place == wanted, 1.0, 0.0).astype(BF16)
    return dot(chosen, values).astype(BF16)


def digits(number, *sizes):
    found = []
    for size in reversed(sizes):
        found.append(number & (size - 1))
        number = number >> (size.bit_length() - 1)
    return found[::-1]


def attend_pair(query, key, value, masks, allowed):
    rows = query.shape[0]
    low, high = masks
    both = jnp.concatenate([query * low, query * high], axis=0)
    scores = lax.dot_general(both, key, (((1,), (1,)), ((), ())), preferred_element_type=F32)
    if allowed is not None:
        scores = jnp.where(allowed, scores, -1e30)
    largest = jnp.max(scores, axis=-1, keepdims=True)
    expo = jnp.exp2((scores - largest) * SCALE).astype(BF16)
    side = jnp.concatenate([expo[:rows], expo[rows:]], axis=1)
    right = jnp.concatenate(
        [
            jnp.concatenate([value * low, low], axis=1),
            jnp.concatenate([value * high, high], axis=1),
        ],
        axis=0,
    )
    mixed = dot(side, right)
    return (mixed[:, :PAIR] / mixed[:, PAIR:]).astype(BF16)


def split_kernel(clip_ref, *refs):
    *out_refs, sems = refs
    me = lax.axis_index("space")
    copies = [
        pltpu.make_async_copy(clip_ref.at[me ^ k], out_ref, sems.at[k])
        for k, out_ref in enumerate(out_refs)
    ]
    for copy in copies:
        copy.start()
    for copy in copies:
        copy.wait()


def project_kernel(*refs):
    *clip_refs, w_ref, out_ref = refs
    frames, toks, width = clip_refs[0].shape
    normed = rms_norm(jnp.concatenate([c[...].reshape(-1, width) for c in clip_refs], axis=0))
    for j in range(3):
        out = dot(normed, w_ref[j]).astype(BF16)
        out_ref[j] = out.reshape(len(clip_refs), frames, toks, width)


def space_kernel(*refs, count, groups):
    clip_refs, qkv_refs, (w_ref, out_ref, mix_ref) = refs[:count], refs[count:-3], refs[-3:]
    frames, toks, width = clip_refs[0].shape
    rows = count * toks
    share = toks // groups
    block = frames * share
    masks = halves(rows)

    def part(j, f, cols):
        return jnp.concatenate(
            [ref[j, s, f, :, cols] for ref in qkv_refs for s in range(ref.shape[1])], axis=0
        )

    for f in range(frames):
        for p in range(width // PAIR):
            cols = pl.ds(p * PAIR, PAIR)
            mixed = attend_pair(part(0, f, cols), part(1, f, cols), part(2, f, cols), masks, None)
            mix_ref[pl.ds(f * rows, rows), cols] = mixed
    clip = jnp.concatenate([c[f] for f in range(frames) for c in clip_refs], axis=0)
    after = (dot(mix_ref[...], w_ref[3]) + clip.astype(F32)).astype(BF16)

    def source(row):
        k, g, f, t = digits(row, count, groups, frames, share)
        return f * rows + k * toks + g * share + t

    after = reorder(after, source).reshape(count, groups, block, width)
    me = lax.axis_index("space")
    for k in range(count):
        out_ref[pl.ds((me ^ k) * groups, groups)] = after[k]


def time_kernel(x_ref, w_ref, *refs, toks):
    *out_refs, qkv_ref, mix_ref, done_ref = refs
    groups = len(out_refs)
    space, _, block, width = x_ref.shape
    rows = space * groups * block
    frames = rows // toks
    per = block // toks
    masks = halves(frames)

    def source(row):
        t, m, s, i = digits(row, toks, groups, space, per)
        return ((s * groups + m) * per + i) * toks + t

    x = reorder(x_ref[...].reshape(rows, width), source)
    normed = rms_norm(x)
    for j in range(3):
        qkv_ref[j] = dot(normed, w_ref[j]).astype(BF16)
    order = lax.broadcasted_iota(jnp.int32, (2 * frames, frames), 0) & (frames - 1)
    allowed = lax.broadcasted_iota(jnp.int32, (2 * frames, frames), 1) <= order
    for t in range(toks):
        at = pl.ds(t * frames, frames)
        for p in range(width // PAIR):
            cols = pl.ds(p * PAIR, PAIR)
            mix_ref[at, cols] = attend_pair(
                qkv_ref[0, at, cols], qkv_ref[1, at, cols], qkv_ref[2, at, cols], masks, allowed
            )
    done_ref[...] = (dot(mix_ref[...], w_ref[3]) + x.astype(F32)).astype(BF16)
    me = lax.axis_index("tm")
    own = frames // groups
    for k, out_ref in enumerate(out_refs):
        for t in range(toks):
            at = pl.multiple_of(t * frames + (me ^ k) * own, own)
            out_ref[pl.ds(t * own, own), :] = done_ref[pl.ds(at, own), :]


def place_kernel(*refs):
    *in_refs, out_ref = refs
    frames, toks, width = out_ref.shape
    groups = len(in_refs)
    share = toks // groups
    me = lax.axis_index("tm")

    def source(row):
        f, g, t = digits(row, frames, groups, share)
        return ((g ^ me) * share + t) * frames + f

    rows = jnp.concatenate([in_ref[...] for in_ref in in_refs], axis=0)
    out_ref[...] = reorder(rows, source).reshape(out_ref.shape)


def call(kernel, name, outs, *args, scratch=(), flops=0, hbm=0, vmem=20):
    like = [jax.ShapeDtypeStruct(shape, BF16) for shape in outs]
    size = 2 * sum(math.prod(a.shape) for a in (*args, *like))
    within = pl.BlockSpec(memory_space=pltpu.VMEM)
    return pl.pallas_call(
        kernel,
        out_shape=like,
        in_specs=[pl.BlockSpec(memory_space=pl.ANY)] * hbm + [within] * (len(args) - hbm),
        out_specs=[within] * len(outs),
        scratch_shapes=scratch,
        compiler_params=pltpu.CompilerParams(vmem_limit_bytes=vmem * MIB),
        cost_estimate=pl.CostEstimate(flops=flops, bytes_accessed=size, transcendentals=0),
        name=name,
    )(*args)


def exchange(pieces, axis, order):
    count = lax.axis_size(axis)
    got = {0: pieces[0]}
    for k in order:
        got[k] = lax.ppermute(pieces[k], axis, [(i, i ^ k) for i in range(count)])
    return [got[k] for k in range(count)]


def on_device(clip, w_spatial, w_temporal):
    frames, toks, width = clip.shape
    rows = frames * toks
    tm, space = lax.axis_size("tm"), lax.axis_size("space")
    share = toks // tm
    per = frames // space
    block = per * share
    piece = (per, toks, width)
    cost = 2 * rows * width * width

    parts = call(
        split_kernel,
        "split",
        [piece] * space,
        clip.reshape(space, *piece),
        scratch=[pltpu.SemaphoreType.DMA((space,))],
        hbm=1,
        vmem=60,
    )
    parts = exchange(parts, "space", reversed(range(1, space)))
    groups = [parts[:1], parts[1:2], parts[2:]]
    qkv = [
        call(
            project_kernel,
            "project",
            [(3, len(group), *piece)],
            *group,
            w_spatial,
            flops=3 * cost * len(group) // space,
        )[0]
        for group in groups
        if group
    ]
    after = call(
        functools.partial(space_kernel, count=space, groups=tm),
        "spatial",
        [(space * tm, block, width)],
        *parts,
        *qkv,
        w_spatial,
        scratch=[pltpu.VMEM((rows, width), BF16)],
        flops=2 * cost,
    )[0]
    after = lax.all_to_all(after, ("space", "tm"), split_axis=0, concat_axis=0, tiled=True)
    result = call(
        functools.partial(time_kernel, toks=share),
        "temporal",
        [(rows // tm, width)] * tm,
        after.reshape(space, tm, block, width),
        w_temporal,
        scratch=[
            pltpu.VMEM((3, rows, width), BF16),
            pltpu.VMEM((rows, width), BF16),
            pltpu.VMEM((rows, width), BF16),
        ],
        flops=5 * cost,
    )
    order = sorted(range(1, tm), key=lambda k: (-(k >> 1).bit_count(), k & 1, k))
    result = exchange(result, "tm", order)
    return call(place_kernel, "place", [(frames, toks, width)], *result)[0]


def solution(mesh):
    placed = (P("tm", "space", None), P(), P())
    return jax.shard_map(
        on_device, mesh=mesh, in_specs=placed, out_specs=P("tm", "space", None), check_vma=False
    )
```

time: 89.1 us -> 72.6 us (0.81)
  blocking collectives: 67.7 us -> 27 us
  waiting for transfers between devices: 0 us -> 15.9 us
  starting transfers between devices: 0 us -> 12.6 us
  Pallas kernels: 21 us -> 13.5 us
  local copies, waits for them, and re-layouts: 0 us -> 3.28 us
    all_to_all x2 -> x0, blocking collectives: 43.3 us -> none  [the longest x1 26.5 us: on_device(): lax.all_to_all(clip.reshape(space, rows // space, width), 'space', split_...]
    ppermute x0 -> x10, waiting for transfers between devices: none -> 15.9 us  [exchange(): got[k] = lax.ppermute(pieces[k], axis, [(i, i ^ k) for i in range(count)])]
    ppermute x0 -> x10, starting transfers between devices: none -> 12.6 us  [exchange(): got[k] = lax.ppermute(pieces[k], axis, [(i, i ^ k) for i in range(count)])]
    pallas_call x3 -> x7, Pallas kernels: 21 us -> 13.5 us  [call(): pl.pallas_call(kernel, out_shape=like, in_specs=[pl.BlockSpec(memory_spac...]
    unnamed x0 -> x10, local copies, waits for them, and re-layouts: none -> 3.28 us
    all_to_all x1, blocking collectives: 24.4 us -> 27 us  [on_device(): lax.all_to_all(after, ('space', 'tm'), split_axis=0, concat_axis=0, tiled...]
  transfers between devices with their start and end apart: 0 -> 10, of which waited for: 0 -> 4; matrix products, arithmetic and copies ran while one was open for 0% -> 0% of each run, Pallas kernels for 0% -> 2%
where the time goes in v2:
time: 72.6 us; the launch traced here: 72.4 us
  blocking collectives  27 us (37%)
  waiting for transfers between devices  15.9 us (22%)
  Pallas kernels  13.5 us (19%)
  starting transfers between devices  12.6 us (17%)
  local copies, waits for them, and re-layouts  3.28 us (5%)
    all_to_all x1, blocking collectives, on_device(): lax.all_to_all(after, ('space', 'tm'), split_axis=0, concat_axis=0, tiled...  27 us
    ppermute x10, waiting for transfers between devices, exchange(): got[k] = lax.ppermute(pieces[k], axis, [(i, i ^ k) for i in range(count)])  15.9 us
    pallas_call x7, Pallas kernels, call(): pl.pallas_call(kernel, out_shape=like, in_specs=[pl.BlockSpec(memory_spac...  13.5 us
    ppermute x10, starting transfers between devices, exchange(): got[k] = lax.ppermute(pieces[k], axis, [(i, i ^ k) for i in range(count)])  12.6 us
    unnamed x10, local copies, waits for them, and re-layouts  3.28 us
  transfers between devices with their start and end apart: 10, of which 4 were waited for; matrix products, arithmetic and copies ran while one was open for 0% of the time, Pallas kernels for 2%

profile of v2, /device:TPU:0, one launch (start us, length us, event | category | flops | bytes accessed | tf_op | source)
XLA Modules:
  0.0 72.4 jit_solution(4767847506237653929)
XLA Ops:
  0.0 2.1 %split.1 = (bf16[4,32,768]{2,1,0:T(8,128)(2,1)}, bf16[4,32,768]{2,1,0:T(8,128)(2,1)}, bf16[4,32,768]{2,1,0:T(8,128)(2,1)}, bf16[4,32,768]{2,1,0:T(8,128)(2,1)}) custom-call(bf16[4,4,32,768]{3,2,1,0:T(8,128)(2,1)} %bitcast.5), custom_call_target="tpu_custom_call" | custom-call | bytes 1572864 | tf_op jit(solution)/shard_map/split/pallas_call | solution.py:177
  2.1 3.1 %collective-permute-start = (bf16[4,32,768]{2,1,0:T(8,128)(2,1)}, bf16[4,32,768]{2,1,0:T(8,128)(2,1)S(1)}, u32[]{:S(2)}, u32[]{:S(2)}) collective-permute-start(bf16[4,32,768]{2,1,0:T(8,128)(2,1)} %get-tuple-element.18), channel_id=1, source_target_pairs={{0,1},{1,0},{2,3},{3,2},{4,5},{5,4},{6,7},{7,6},{8,9},{9,8},{10,11... | collective-permute-start | bytes 589832 | tf_op jit(solution)/shard_map/ppermute | solution.py:193
  5.2 2.6 %collective-permute-start.1 = (bf16[4,32,768]{2,1,0:T(8,128)(2,1)}, bf16[4,32,768]{2,1,0:T(8,128)(2,1)S(1)}, u32[]{:S(2)}, u32[]{:S(2)}) collective-permute-start(bf16[4,32,768]{2,1,0:T(8,128)(2,1)} %get-tuple-element.19), channel_id=1, source_target_pairs={{0,2},{1,3},{2,0},{3,1},{4,6},{5,7},{6,4},{7,5},{8,10},{9,11},{10,... | collective-permute-start | bytes 589832 | tf_op jit(solution)/shard_map/ppermute | solution.py:193
  7.8 0.0 collective-permute-start.2
  7.8 2.3 %copy-done = bf16[4,768,768]{2,1,0:T(8,128)(2,1)S(1)} copy-done((bf16[4,768,768]{2,1,0:T(8,128)(2,1)S(1)}, bf16[4,768,768]{2,1,0:T(8,128)(2,1)}, u32[]{:S(2)}) %copy-start) | copy-done | bytes 4718616
  10.2 0.9 %copy-done.2 = bf16[4,32,768]{2,1,0:T(8,128)(2,1)S(1)} copy-done((bf16[4,32,768]{2,1,0:T(8,128)(2,1)S(1)}, bf16[4,32,768]{2,1,0:T(8,128)(2,1)}, u32[]{:S(2)}) %copy-start.2) | copy-done | bytes 196632
  11.1 0.7 project.3.refs_4_
  11.8 2.0 %collective-permute-done.refs_0_.refs_1_ = bf16[4,32,768]{2,1,0:T(8,128)(2,1)S(1)} collective-permute-done((bf16[4,32,768]{2,1,0:T(8,128)(2,1)}, bf16[4,32,768]{2,1,0:T(8,128)(2,1)S(1)}, u32[]{:S(2)}, u32[]{:S(2)}) %collective-permute-start) | collective-permute-done | bytes 196640 | tf_op jit(solution)/shard_map/ppermute | solution.py:193
  13.8 0.0 copy-done.1
  13.8 0.7 project.4.refs_5_
  14.5 8.1 %collective-permute-done.1.refs_0_.refs_2_ = bf16[4,32,768]{2,1,0:T(8,128)(2,1)S(1)} collective-permute-done((bf16[4,32,768]{2,1,0:T(8,128)(2,1)}, bf16[4,32,768]{2,1,0:T(8,128)(2,1)S(1)}, u32[]{:S(2)}, u32[]{:S(2)}) %collective-permute-start.1) | collective-permute-done | bytes 196640 | tf_op jit(solution)/shard_map/ppermute | solution.py:193
  22.6 0.0 collective-permute-done.2.refs_1_.refs_3_
  22.6 1.2 %project.5.refs_6_ = bf16[3,2,4,32,768]{4,3,2,1,0:T(8,128)(2,1)S(1)} custom-call(bf16[4,32,768]{2,1,0:T(8,128)(2,1)S(1)} %collective-permute-done.1.refs_0_.refs_2_, bf16[4,32,768]{2,1,0:T(8,128)(2,1)S(1)} %collective-permute-done.2.refs_1_.refs_3_, bf16[4,768,768]{2,1,0:T(8,128)(2,1)S(1)} %copy-done.1), custom_call_target="tpu_custom_call" | custom-call | flops 905969664 | bytes 6291456 | tf_op jit(solution)/shard_map/project/pallas_call | solution.py:177
  23.8 0.0 slice-start.1
  23.8 2.3 %spatial.1 = bf16[32,16,768]{2,1,0:T(8,128)(2,1)S(1)} custom-call(bf16[4,32,768]{2,1,0:T(8,128)(2,1)S(1)} %copy-done.2, bf16[4,32,768]{2,1,0:T(8,128)(2,1)S(1)} %collective-permute-done.refs_0_.refs_1_, bf16[4,32,768]{2,1,0:T(8,128)(2,1)S(1)} %collective-permute-done.1.refs_0_.refs_2_, bf16[4,32,768]{2,1,0:T(8,128)(2,1)S(1)} %collective-permute-done.2.refs_1_.refs_3_, ...), custom_call_target="tpu_custom_call" | custom-call | flops 1207959552 | bytes 8650752 | tf_op jit(solution)/shard_map/spatial/pallas_call | solution.py:177
  26.1 27.0 %all_to_all.5 = bf16[32,16,768]{2,1,0:T(8,128)(2,1)S(1)} all-to-all(bf16[32,16,768]{2,1,0:T(8,128)(2,1)S(1)} %spatial.1), channel_id=1, replica_groups=mesh['tm'=8,'space'=4] {'space','tm'}, dimensions={0} | all-to-all | bytes 1572864 | tf_op jit(solution)/shard_map/all_to_all | solution.py:240
  53.2 5.0 %temporal.1 = (bf16[64,768]{1,0:T(8,128)(2,1)S(1)}, bf16[64,768]{1,0:T(8,128)(2,1)S(1)}, bf16[64,768]{1,0:T(8,128)(2,1)S(1)}, bf16[64,768]{1,0:T(8,128)(2,1)S(1)...) custom-call(bf16[4,8,16,768]{3,2,1,0:T(8,128)(2,1)S(1)} %bitcast.2, ...), custom_call_target="tpu_custom_call" | custom-call | flops 3019898880 | bytes 6291456 | tf_op jit(solution)/shard_map/temporal/pallas_call | solution.py:177
  58.2 0.1 collective-permute-start.3
  58.3 1.6 %collective-permute-start.4 = (bf16[64,768]{1,0:T(8,128)(2,1)S(1)}, bf16[64,768]{1,0:T(8,128)(2,1)S(1)}, u32[]{:S(2)}, u32[]{:S(2)}) collective-permute-start(bf16[64,768]{1,0:T(8,128)(2,1)S(1)} %get-tuple-element.23), channel_id=1, source_target_pairs={{0,8},{4,12},{8,0},{12,4},{16,24},{20,28},{24,16},{28,20},{1,9},{5... | collective-permute-start | bytes 294920 | tf_op jit(solution)/shard_map/ppermute | solution.py:193
  59.9 0.3 collective-permute-start.5
  60.1 1.5 %collective-permute-start.6 = (bf16[64,768]{1,0:T(8,128)(2,1)S(1)}, bf16[64,768]{1,0:T(8,128)(2,1)S(1)}, u32[]{:S(2)}, u32[]{:S(2)}) collective-permute-start(bf16[64,768]{1,0:T(8,128)(2,1)S(1)} %get-tuple-element.25), channel_id=1, source_target_pairs={{0,16},{4,20},{8,24},{12,28},{16,0},{20,4},{24,8},{28,12},{1,17},{... | collective-permute-start | bytes 294920 | tf_op jit(solution)/shard_map/ppermute | solution.py:193
  61.6 0.2 collective-permute-start.7
  61.8 0.0 collective-permute-done.3.refs_1_
  61.8 2.4 %collective-permute-start.8 = (bf16[64,768]{1,0:T(8,128)(2,1)S(1)}, bf16[64,768]{1,0:T(8,128)(2,1)S(1)}, u32[]{:S(2)}, u32[]{:S(2)}) collective-permute-start(bf16[64,768]{1,0:T(8,128)(2,1)S(1)} %get-tuple-element.27), channel_id=1, source_target_pairs={{0,24},{4,28},{8,16},{12,20},{16,8},{20,12},{24,0},{28,4},{1,25},{... | collective-permute-start | bytes 294920 | tf_op jit(solution)/shard_map/ppermute | solution.py:193
  64.2 0.0 collective-permute-done.4.refs_2_
  64.2 0.9 %collective-permute-start.9 = (bf16[64,768]{1,0:T(8,128)(2,1)S(1)}, bf16[64,768]{1,0:T(8,128)(2,1)S(1)}, u32[]{:S(2)}, u32[]{:S(2)}) collective-permute-start(bf16[64,768]{1,0:T(8,128)(2,1)S(1)} %get-tuple-element.28), channel_id=1, source_target_pairs={{0,28},{4,24},{8,20},{12,16},{16,12},{20,8},{24,4},{28,0},{1,29},{... | collective-permute-start | bytes 294920 | tf_op jit(solution)/shard_map/ppermute | solution.py:193
  65.1 0.0 collective-permute-done.5.refs_3_
  65.1 0.6 collective-permute-done.6.refs_4_
  65.7 5.2 %collective-permute-done.7.refs_5_ = bf16[64,768]{1,0:T(8,128)(2,1)S(1)} collective-permute-done((bf16[64,768]{1,0:T(8,128)(2,1)S(1)}, bf16[64,768]{1,0:T(8,128)(2,1)S(1)}, u32[]{:S(2)}, u32[]{:S(2)}) %collective-permute-start.7) | collective-permute-done | bytes 98336 | tf_op jit(solution)/shard_map/ppermute | solution.py:193
  70.9 0.0 collective-permute-done.8.refs_6_
  70.9 0.0 collective-permute-done.9.refs_7_
  70.9 1.5 %place.1 = bf16[16,32,768]{2,1,0:T(8,128)(2,1)} custom-call(bf16[64,768]{1,0:T(8,128)(2,1)S(1)} %get-tuple-element.21.refs_0_, bf16[64,768]{1,0:T(8,128)(2,1)S(1)} %collective-permute-done.3.refs_1_, bf16[64,768]{1,0:T(8,128)(2,1)S(1)} %collective-permute-done.4.refs_2_, bf16[64,768]{1,0:T(8,128)(2,1)S(1)} %collective-permute-done.5.refs_3_, ...), custom_call_target="tpu_custom_call" | custom-call | bytes 1572864 | tf_op jit(solution)/shard_map/place/pallas_call | solution.py:177
  (7 shorter events, 0.0 us)
Async XLA Ops:
  2.1 11.6 %collective-permute-start = (bf16[4,32,768]{2,1,0:T(8,128)(2,1)}, bf16[4,32,768]{2,1,0:T(8,128)(2,1)S(1)}, u32[]{:S(2)}, u32[]{:S(2)}) collective-permute-start(bf16[4,32,768]{2,1,0:T(8,128)(2,1)} %get-tuple-element.18), channel_id=1, source_target_pairs={{0,1},{1,0},{2,3},{3,2},{4,5},{5,4},{6,7},{7,6},{8,9},{9,8},{10,11... | collective-permute-start | bytes 589832 | tf_op jit(solution)/shard_map/ppermute | solution.py:193
  5.2 17.4 %collective-permute-start.1 = (bf16[4,32,768]{2,1,0:T(8,128)(2,1)}, bf16[4,32,768]{2,1,0:T(8,128)(2,1)S(1)}, u32[]{:S(2)}, u32[]{:S(2)}) collective-permute-start(bf16[4,32,768]{2,1,0:T(8,128)(2,1)} %get-tuple-element.19), channel_id=1, source_target_pairs={{0,2},{1,3},{2,0},{3,1},{4,6},{5,7},{6,4},{7,5},{8,10},{9,11},{10,... | collective-permute-start | bytes 589832 | tf_op jit(solution)/shard_map/ppermute | solution.py:193
  7.8 14.8 %collective-permute-start.2 = (bf16[4,32,768]{2,1,0:T(8,128)(2,1)}, bf16[4,32,768]{2,1,0:T(8,128)(2,1)S(1)}, u32[]{:S(2)}, u32[]{:S(2)}) collective-permute-start(bf16[4,32,768]{2,1,0:T(8,128)(2,1)} %get-tuple-element.20), channel_id=1, source_target_pairs={{0,3},{1,2},{2,1},{3,0},{4,7},{5,6},{6,5},{7,4},{8,11},{9,10},{10,... | collective-permute-start | bytes 589832 | tf_op jit(solution)/shard_map/ppermute | solution.py:193
  7.8 2.3 %copy-start = (bf16[4,768,768]{2,1,0:T(8,128)(2,1)S(1)}, bf16[4,768,768]{2,1,0:T(8,128)(2,1)}, u32[]{:S(2)}) copy-start(bf16[4,768,768]{2,1,0:T(8,128)(2,1)} %refs_7_.1) | copy-start | bytes 14155780
  10.1 0.9 %copy-start.2 = (bf16[4,32,768]{2,1,0:T(8,128)(2,1)S(1)}, bf16[4,32,768]{2,1,0:T(8,128)(2,1)}, u32[]{:S(2)}) copy-start(bf16[4,32,768]{2,1,0:T(8,128)(2,1)} %get-tuple-element.17.refs_0_) | copy-start | bytes 589828
  11.1 2.7 %copy-start.1 = (bf16[4,768,768]{2,1,0:T(8,128)(2,1)S(1)}, bf16[4,768,768]{2,1,0:T(8,128)(2,1)}, u32[]{:S(2)}) copy-start(bf16[4,768,768]{2,1,0:T(8,128)(2,1)} %refs_7_.1) | copy-start | bytes 14155780
  22.6 30.6 %slice-start = ((s8[4718592]{0:T(1024)(128)(4,1)}), s8[4194304]{0:T(1024)(128)(4,1)S(1)}, s32[]{:S(2)}) async-start(s8[4718592]{0:T(1024)(128)(4,1)} %bitcast.3), calls=%async_computation.1 | async-start | bytes 8388608
  23.8 29.4 %slice-start.1 = ((s8[4718592]{0:T(1024)(128)(4,1)}), s8[524288]{0:T(1024)(128)(4,1)S(1)}, s32[]{:S(2)}) async-start(s8[4718592]{0:T(1024)(128)(4,1)} %bitcast.3), calls=%async_computation.2 | async-start | bytes 1048576
  58.2 3.6 %collective-permute-start.3 = (bf16[64,768]{1,0:T(8,128)(2,1)S(1)}, bf16[64,768]{1,0:T(8,128)(2,1)S(1)}, u32[]{:S(2)}, u32[]{:S(2)}) collective-permute-start(bf16[64,768]{1,0:T(8,128)(2,1)S(1)} %get-tuple-element.22), channel_id=1, source_target_pairs={{0,4},{4,0},{8,12},{12,8},{16,20},{20,16},{24,28},{28,24},{1,5},{5... | collective-permute-start | bytes 294920 | tf_op jit(solution)/shard_map/ppermute | solution.py:193
  58.3 5.9 %collective-permute-start.4 = (bf16[64,768]{1,0:T(8,128)(2,1)S(1)}, bf16[64,768]{1,0:T(8,128)(2,1)S(1)}, u32[]{:S(2)}, u32[]{:S(2)}) collective-permute-start(bf16[64,768]{1,0:T(8,128)(2,1)S(1)} %get-tuple-element.23), channel_id=1, source_target_pairs={{0,8},{4,12},{8,0},{12,4},{16,24},{20,28},{24,16},{28,20},{1,9},{5... | collective-permute-start | bytes 294920 | tf_op jit(solution)/shard_map/ppermute | solution.py:193
  59.9 5.3 %collective-permute-start.5 = (bf16[64,768]{1,0:T(8,128)(2,1)S(1)}, bf16[64,768]{1,0:T(8,128)(2,1)S(1)}, u32[]{:S(2)}, u32[]{:S(2)}) collective-permute-start(bf16[64,768]{1,0:T(8,128)(2,1)S(1)} %get-tuple-element.24), channel_id=1, source_target_pairs={{0,12},{4,8},{8,4},{12,0},{16,28},{20,24},{24,20},{28,16},{1,13},{... | collective-permute-start | bytes 294920 | tf_op jit(solution)/shard_map/ppermute | solution.py:193
  60.1 5.6 %collective-permute-start.6 = (bf16[64,768]{1,0:T(8,128)(2,1)S(1)}, bf16[64,768]{1,0:T(8,128)(2,1)S(1)}, u32[]{:S(2)}, u32[]{:S(2)}) collective-permute-start(bf16[64,768]{1,0:T(8,128)(2,1)S(1)} %get-tuple-element.25), channel_id=1, source_target_pairs={{0,16},{4,20},{8,24},{12,28},{16,0},{20,4},{24,8},{28,12},{1,17},{... | collective-permute-start | bytes 294920 | tf_op jit(solution)/shard_map/ppermute | solution.py:193
  61.6 9.3 %collective-permute-start.7 = (bf16[64,768]{1,0:T(8,128)(2,1)S(1)}, bf16[64,768]{1,0:T(8,128)(2,1)S(1)}, u32[]{:S(2)}, u32[]{:S(2)}) collective-permute-start(bf16[64,768]{1,0:T(8,128)(2,1)S(1)} %get-tuple-element.26), channel_id=1, source_target_pairs={{0,20},{4,16},{8,28},{12,24},{16,4},{20,0},{24,12},{28,8},{1,21},{... | collective-permute-start | bytes 294920 | tf_op jit(solution)/shard_map/ppermute | solution.py:193
  61.8 9.1 %collective-permute-start.8 = (bf16[64,768]{1,0:T(8,128)(2,1)S(1)}, bf16[64,768]{1,0:T(8,128)(2,1)S(1)}, u32[]{:S(2)}, u32[]{:S(2)}) collective-permute-start(bf16[64,768]{1,0:T(8,128)(2,1)S(1)} %get-tuple-element.27), channel_id=1, source_target_pairs={{0,24},{4,28},{8,16},{12,20},{16,8},{20,12},{24,0},{28,4},{1,25},{... | collective-permute-start | bytes 294920 | tf_op jit(solution)/shard_map/ppermute | solution.py:193
  64.2 6.7 %collective-permute-start.9 = (bf16[64,768]{1,0:T(8,128)(2,1)S(1)}, bf16[64,768]{1,0:T(8,128)(2,1)S(1)}, u32[]{:S(2)}, u32[]{:S(2)}) collective-permute-start(bf16[64,768]{1,0:T(8,128)(2,1)S(1)} %get-tuple-element.28), channel_id=1, source_target_pairs={{0,28},{4,24},{8,20},{12,16},{16,12},{20,8},{24,4},{28,0},{1,29},{... | collective-permute-start | bytes 294920 | tf_op jit(solution)/shard_map/ppermute | solution.py:193

commit v3 on v2

v3 whole, which is shorter than its diff:
```python
import functools
import math

import jax
import jax.numpy as jnp
from jax import lax
from jax.experimental import pallas as pl
from jax.experimental.pallas import tpu as pltpu
from jax.sharding import PartitionSpec as P

HEAD = 64
PAIR = 2 * HEAD
SCALE = math.log2(math.e) / math.sqrt(HEAD)
F32, BF16 = jnp.float32, jnp.bfloat16
MIB = 1024 * 1024


def dot(a, b):
    return jnp.dot(a, b, preferred_element_type=F32)


def rms_norm(values):
    wide = values.astype(F32)
    return (wide * lax.rsqrt(jnp.mean(wide * wide, axis=-1, keepdims=True) + 1e-06)).astype(BF16)


def halves(rows):
    first = lax.broadcasted_iota(jnp.int32, (rows, PAIR), 1) < HEAD
    one, zero = jnp.ones((rows, PAIR), F32), jnp.zeros((rows, PAIR), F32)
    return jnp.where(first, one, zero).astype(BF16), jnp.where(first, zero, one).astype(BF16)


def reorder(values, source, rows=None, first=0):
    rows = rows or values.shape[0]
    wanted = source(lax.broadcasted_iota(jnp.int32, (rows, 1), 0) + first)
    place = lax.broadcasted_iota(jnp.int32, (rows, values.shape[0]), 1)
    chosen = jnp.where(place == wanted, 1.0, 0.0).astype(BF16)
    return dot(chosen, values).astype(BF16)


def digits(number, *sizes):
    found = []
    for size in reversed(sizes):
        found.append(number & (size - 1))
        number = number >> (size.bit_length() - 1)
    return found[::-1]


def group_of(width):
    return 2 * PAIR if width % (2 * PAIR) == 0 else PAIR


def attend(query, key, value, masks, allowed):
    rows, width = query.shape
    low, high = masks
    pairs = [slice(p, p + PAIR) for p in range(0, width, PAIR)]
    both = jnp.concatenate(
        [jnp.concatenate([query[:, p] * m for p in pairs], axis=1) for m in masks], axis=0
    )
    nothing = jnp.zeros((rows, PAIR), BF16)
    keys = jnp.concatenate(
        [
            jnp.concatenate([key[:, p] if p == q else nothing for p in pairs], axis=1)
            for q in pairs
        ],
        axis=0,
    )
    scores = lax.dot_general(both, keys, (((1,), (1,)), ((), ())), preferred_element_type=F32)
    out = []
    for i, p in enumerate(pairs):
        part = scores[:, i * rows : (i + 1) * rows]
        if allowed is not None:
            part = jnp.where(allowed, part, -1e30)
        largest = jnp.max(part, axis=-1, keepdims=True)
        expo = jnp.exp2((part - largest) * SCALE).astype(BF16)
        side = jnp.concatenate([expo[:rows], expo[rows:]], axis=1)
        right = jnp.concatenate(
            [jnp.concatenate([value[:, p] * m, m], axis=1) for m in masks], axis=0
        )
        mixed = dot(side, right)
        out.append((mixed[:, :PAIR] / mixed[:, PAIR:]).astype(BF16))
    return jnp.concatenate(out, axis=1)


def own_or_whole(clip_ref, frame):
    if len(clip_ref.shape) == 4:
        return clip_ref[lax.axis_index("space"), frame]
    return clip_ref[frame]


def project_kernel(*refs):
    *clip_refs, w_ref, out_ref = refs
    project(clip_refs, w_ref, out_ref)


def project(clip_refs, w_ref, out_ref):
    frames, toks, width = out_ref.shape[2:]
    clip = [own_or_whole(c, slice(None)).reshape(-1, width) for c in clip_refs]
    normed = rms_norm(jnp.concatenate(clip, axis=0))
    for j in range(3):
        out = dot(normed, w_ref[j]).astype(BF16)
        out_ref[j] = out.reshape(len(clip_refs), frames, toks, width)


def space_kernel(*refs, distances, groups):
    count = len(distances)
    clip_refs, refs = refs[:count], refs[count:]
    *qkv_refs, w_ref, out_ref, mix_ref, last_ref = refs
    project(clip_refs[count - last_ref.shape[1] :], w_ref, last_ref)
    qkv_refs = [*qkv_refs, last_ref]
    frames, toks, width = clip_refs[0].shape[1:]
    rows = count * toks
    share = toks // groups
    block = frames * share
    masks = halves(rows)
    group = group_of(width)

    def part(j, f, cols):
        return jnp.concatenate(
            [ref[j, s, f, :, cols] for ref in qkv_refs for s in range(ref.shape[1])], axis=0
        )

    for f in range(frames):
        for p in range(0, width, group):
            cols = pl.ds(p, group)
            mixed = attend(part(0, f, cols), part(1, f, cols), part(2, f, cols), masks, None)
            mix_ref[pl.ds(f * rows, rows), cols] = mixed
    clip = jnp.concatenate(
        [own_or_whole(c, f) for f in range(frames) for c in clip_refs], axis=0
    )
    after = (dot(mix_ref[...], w_ref[3]) + clip.astype(F32)).astype(BF16)

    def source(row):
        k, g, f, t = digits(row, count, groups, frames, share)
        return f * rows + k * toks + g * share + t

    after = reorder(after, source).reshape(count, groups, block, width)
    me = lax.axis_index("space")
    for i, k in enumerate(distances):
        out_ref[pl.ds((me ^ k) * groups, groups)] = after[i]


def time_kernel(x_ref, w_ref, *refs, toks, last):
    *out_refs, qkv_ref, mix_ref, done_ref = refs
    space, groups, block, width = x_ref.shape
    rows = space * groups * block
    frames = rows // toks
    per = block // toks
    masks = halves(frames)
    group = group_of(width)

    def source(row):
        t, m, s, i = digits(row, toks, groups, space, per)
        return ((s * groups + m) * per + i) * toks + t

    x = reorder(x_ref[...].reshape(rows, width), source)
    normed = rms_norm(x)
    for j in range(3):
        qkv_ref[j] = dot(normed, w_ref[j]).astype(BF16)
    order = lax.broadcasted_iota(jnp.int32, (2 * frames, frames), 0) & (frames - 1)
    allowed = lax.broadcasted_iota(jnp.int32, (2 * frames, frames), 1) <= order
    for t in range(toks):
        at = pl.ds(t * frames, frames)
        for p in range(0, width, group):
            cols = pl.ds(p, group)
            mix_ref[at, cols] = attend(
                qkv_ref[0, at, cols], qkv_ref[1, at, cols], qkv_ref[2, at, cols], masks, allowed
            )
    done_ref[...] = (dot(mix_ref[...], w_ref[3]) + x.astype(F32)).astype(BF16)
    me = lax.axis_index("tm")
    own = frames // groups
    for k in range(groups):
        for t in range(toks):
            at = pl.multiple_of(t * frames + (me ^ k) * own, own)
            block = done_ref[pl.ds(at, own), :]
            if k // 2 == last:
                out_refs[groups // 2 - 1 + k % 2][pl.ds(t * own, own), :] = block
            else:
                out_refs[k // 2 - (k // 2 > last)][k % 2, pl.ds(t * own, own), :] = block


def place_kernel(*refs, order, groups, toks):
    *in_refs, out_ref = refs
    frames, _, width = in_refs[-1].shape[0] * groups // toks, 0, in_refs[-1].shape[1]
    steps = frames // out_ref.shape[0]
    share = toks // groups
    far = groups // 2
    me = lax.axis_index("tm")
    first = pl.program_id(0) * (frames // steps * toks)

    def source(row):
        f, g, t = digits(row, frames, groups, share)
        return ((g ^ me) * share + t) * frames + f

    pairs = {k: (in_refs[i].at[0], in_refs[far - 1 + i]) for i, k in enumerate(order[:-1])}
    pairs[order[-1]] = in_refs[-2:]
    rows = jnp.concatenate([part[...] for k in range(far) for part in pairs[k]], axis=0)
    done = reorder(rows, source, frames // steps * toks, first)
    out_ref[...] = done.reshape(out_ref.shape)


def call(kernel, name, outs, *args, scratch=(), flops=0, **blocks):
    like = [jax.ShapeDtypeStruct(shape, BF16) for shape in outs]
    size = 2 * sum(math.prod(a.shape) for a in (*args, *like))
    within = pl.BlockSpec(memory_space=pltpu.VMEM)
    return pl.pallas_call(
        kernel,
        out_shape=like,
        in_specs=[within] * len(args),
        out_specs=blocks.pop("out_specs", [within] * len(outs)),
        scratch_shapes=scratch,
        compiler_params=pltpu.CompilerParams(vmem_limit_bytes=20 * MIB),
        cost_estimate=pl.CostEstimate(flops=flops, bytes_accessed=size, transcendentals=0),
        name=name,
        **blocks,
    )(*args)


def exchange(pieces, axis, order, unit=1):
    count = lax.axis_size(axis)
    got = {0: pieces[0]}
    for k in order:
        got[k] = lax.ppermute(pieces[k], axis, [(i, i ^ (k * unit)) for i in range(count)])
    return [got[k] for k in range(len(pieces))]


def on_device(clip, w_spatial, w_temporal):
    frames, toks, width = clip.shape
    rows = frames * toks
    tm, space = lax.axis_size("tm"), lax.axis_size("space")
    share = toks // tm
    per = frames // space
    block = per * share
    piece = (per, toks, width)
    cost = 2 * rows * width * width

    blocks = clip.reshape(space, *piece)
    me = lax.axis_index("space")
    parts = [blocks] + [
        lax.dynamic_index_in_dim(blocks, me ^ k, 0, keepdims=False) for k in range(1, space)
    ]
    parts = exchange(parts, "space", sorted(range(1, space), key=lambda k: (k == 1, k)))
    groups = [[0], [2], [1], [*range(3, space)]] if space > 3 else [[*range(space)]]
    qkv = [
        call(
            project_kernel,
            "project",
            [(3, len(group), *piece)],
            *[parts[k] for k in group],
            w_spatial,
            flops=3 * cost * len(group) // space,
        )[0]
        for group in groups[:-1]
    ]
    after = call(
        functools.partial(space_kernel, distances=sum(groups, []), groups=tm),
        "spatial",
        [(space * tm, block, width)],
        *[parts[k] for k in sum(groups, [])],
        *qkv,
        w_spatial,
        scratch=[
            pltpu.VMEM((rows, width), BF16),
            pltpu.VMEM((3, len(groups[-1]), *piece), BF16),
        ],
        flops=2 * cost,
    )[0]
    after = lax.all_to_all(after, ("space", "tm"), split_axis=0, concat_axis=0, tiled=True)
    order = [0, *sorted(range(1, tm // 2), key=lambda k: (-k.bit_count(), k))]
    result = call(
        functools.partial(time_kernel, toks=share, last=order[-1]),
        "temporal",
        [(2, rows // tm, width)] * (tm // 2 - 1) + [(rows // tm, width)] * 2,
        after.reshape(space, tm, block, width),
        w_temporal,
        scratch=[
            pltpu.VMEM((3, rows, width), BF16),
            pltpu.VMEM((rows, width), BF16),
            pltpu.VMEM((rows, width), BF16),
        ],
        flops=5 * cost,
    )
    last = order[-1]
    direct = [
        lax.ppermute(part, "tm", [(i, i ^ (2 * last + s)) for i in range(tm)])
        for s, part in enumerate(result[-2:])
    ]
    whole = dict(zip([k for k in range(tm // 2) if k != last], result))
    whole = {
        k: lax.ppermute(part, "tm", [(i, i ^ (2 * k)) for i in range(tm)]) if k else part
        for k, part in whole.items()
    }
    beside = {
        k: lax.ppermute(part[1], "tm", [(i, i ^ 1) for i in range(tm)])
        for k, part in whole.items()
    }
    steps = 2 if frames % 2 == 0 else 1
    return call(
        functools.partial(place_kernel, order=order, groups=tm, toks=toks),
        "place",
        [(frames, toks, width)],
        *[whole[k] for k in order[:-1]],
        *[beside[k] for k in order[:-1]],
        *direct,
        grid=(steps,),
        out_specs=[pl.BlockSpec((frames // steps, toks, width), lambda i: (i, 0, 0))],
    )[0]


def solution(mesh):
    placed = (P("tm", "space", None), P(), P())
    return jax.shard_map(
        on_device, mesh=mesh, in_specs=placed, out_specs=P("tm", "space", None), check_vma=False
    )
```

time: 72.6 us -> 71.2 us (0.981)
  starting transfers between devices: 12.6 us -> 10.8 us
  Pallas kernels: 13.5 us -> 11.8 us
  local copies, waits for them, and re-layouts: 3.28 us -> 4.66 us
  blocking collectives: 27 us -> 28.3 us
    ppermute x10, starting transfers between devices: 12.6 us -> 10.8 us  [the longest x3 5.68 us: exchange(): lax.ppermute(pieces[k], axis, [(i, i ^ k * unit) for i in range(count)])]
    pallas_call x7 -> x6, Pallas kernels: 13.5 us -> 11.8 us  [call(): pl.pallas_call(kernel, out_shape=like, in_specs=[within] * len(args), out...]
    all_to_all x1, blocking collectives: 27 us -> 28.3 us  [on_device(): lax.all_to_all(after, ('space', 'tm'), split_axis=0, concat_axis=0, tiled...]
    squeeze x0 -> x4, local copies, waits for them, and re-layouts: none -> 1.18 us  [the longest x1 1.15 us: on_device(): lax.dynamic_index_in_dim(blocks, me ^ k, 0, keepdims=False)]
  transfers between devices with their start and end apart: 10 -> 10, of which waited for: 4 -> 5; matrix products, arithmetic and copies ran while one was open for 0% -> 0% of each run, Pallas kernels for 2% -> 3%
where the time goes in v3:
time: 71.2 us; the launch traced here: 71 us
  blocking collectives  28.3 us (40%)
  waiting for transfers between devices  15.4 us (22%)
  Pallas kernels  11.8 us (17%)
  starting transfers between devices  10.8 us (15%)
  local copies, waits for them, and re-layouts  4.66 us (7%)
    all_to_all x1, blocking collectives, on_device(): lax.all_to_all(after, ('space', 'tm'), split_axis=0, concat_axis=0, tiled...  28.3 us
    pallas_call x6, Pallas kernels, call(): pl.pallas_call(kernel, out_shape=like, in_specs=[within] * len(args), out...  11.8 us
    ppermute x3, waiting for transfers between devices, exchange(): lax.ppermute(pieces[k], axis, [(i, i ^ k * unit) for i in range(count)])  7.31 us
    ppermute x2, waiting for transfers between devices, on_device(): lax.ppermute(part, 'tm', [(i, i ^ 2 * k) for i in range(tm)])  6.8 us
    ppermute x3, starting transfers between devices, exchange(): lax.ppermute(pieces[k], axis, [(i, i ^ k * unit) for i in range(count)])  5.68 us
    unnamed x10, local copies, waits for them, and re-layouts  3.49 us
    ppermute x2, starting transfers between devices, on_device(): lax.ppermute(part, 'tm', [(i, i ^ 2 * k) for i in range(tm)])  3.03 us
    ppermute x2, starting transfers between devices, on_device(): lax.ppermute(part, 'tm', [(i, i ^ 2 * last + s) for i in range(tm)])  1.86 us
  transfers between devices with their start and end apart: 10, of which 5 were waited for; matrix products, arithmetic and copies ran while one was open for 0% of the time, Pallas kernels for 3%

profile of v3, /device:TPU:0, one launch (start us, length us, event | category | flops | bytes accessed | tf_op | source)
XLA Modules:
  0.0 71.0 jit_solution(11884577214953325712)
XLA Ops:
  0.0 1.2 %dynamic-slice_bitcast_fusion = (bf16[4,32,768]{2,1,0:T(8,128)(2,1)S(1)}, bf16[4,32,768]{2,1,0:T(8,128)(2,1)S(1)}, bf16[4,32,768]{2,1,0:T(8,128)(2,1)S(1)}) fusion(bf16[4,4,32,768]{3,2,1,0:T(8,128)(2,1)} %bitcast.14, s32[]{:T(128)S(6)} %select_n.12, s32[]{:T(128)S(6)} %select_n.11, s32[]{:T(128)S(6)} %select_n.10), kind=kLoop, calls=%fused_computation | loop fusion | bytes 1179660 | tf_op jit(solution)/shard_map/jit(dynamic_index_in_dim)/squeeze | solution.py:240
  1.2 4.1 %collective-permute-start = (bf16[4,32,768]{2,1,0:T(8,128)(2,1)S(1)}, bf16[4,32,768]{2,1,0:T(8,128)(2,1)S(1)}, u32[]{:S(2)}, u32[]{:S(2)}) collective-permute-start(bf16[4,32,768]{2,1,0:T(8,128)(2,1)S(1)} %get-tuple-element.17), channel_id=1, source_target_pairs={{0,2},{1,3},{2,0},{3,1},{4,6},{5,7},{6,4},{7,5},{8,10},{9,11},{10,... | collective-permute-start | bytes 589832 | tf_op jit(solution)/shard_map/ppermute | solution.py:223
  5.3 1.6 %collective-permute-start.1 = (bf16[4,32,768]{2,1,0:T(8,128)(2,1)S(1)}, bf16[4,32,768]{2,1,0:T(8,128)(2,1)S(1)}, u32[]{:S(2)}, u32[]{:S(2)}) collective-permute-start(bf16[4,32,768]{2,1,0:T(8,128)(2,1)S(1)} %get-tuple-element.16), channel_id=1, source_target_pairs={{0,1},{1,0},{2,3},{3,2},{4,5},{5,4},{6,7},{7,6},{8,9},{9,8},{10,11... | collective-permute-start | bytes 589832 | tf_op jit(solution)/shard_map/ppermute | solution.py:223
  6.8 0.0 collective-permute-start.2
  6.8 2.3 %copy-done = bf16[4,768,768]{2,1,0:T(8,128)(2,1)S(1)} copy-done((bf16[4,768,768]{2,1,0:T(8,128)(2,1)S(1)}, bf16[4,768,768]{2,1,0:T(8,128)(2,1)}, u32[]{:S(2)}) %copy-start) | copy-done | bytes 4718616
  9.2 1.1 %copy-done.2 = bf16[16,32,768]{2,1,0:T(8,128)(2,1)S(1)} copy-done((bf16[16,32,768]{2,1,0:T(8,128)(2,1)S(1)}, bf16[16,32,768]{2,1,0:T(8,128)(2,1)}, u32[]{:S(2)}) %copy-start.2) | copy-done | bytes 786456
  10.3 0.7 %project.3.refs_4_ = bf16[3,1,4,32,768]{4,3,2,1,0:T(8,128)(2,1)S(1)} custom-call(bf16[4,4,32,768]{3,2,1,0:T(8,128)(2,1)S(1)} %bitcast.15, bf16[4,768,768]{2,1,0:T(8,128)(2,1)S(1)} %copy-done), custom_call_target="tpu_custom_call" | custom-call | flops 452984832 | bytes 6094848 | tf_op jit(solution)/shard_map/project/pallas_call | solution.py:206
  11.0 5.1 %collective-permute-done.refs_0_.refs_1_ = bf16[4,32,768]{2,1,0:T(8,128)(2,1)S(1)} collective-permute-done((bf16[4,32,768]{2,1,0:T(8,128)(2,1)S(1)}, bf16[4,32,768]{2,1,0:T(8,128)(2,1)S(1)}, u32[]{:S(2)}, u32[]{:S(2)}) %collective-permute-start) | collective-permute-done | bytes 196640 | tf_op jit(solution)/shard_map/ppermute | solution.py:223
  16.1 0.7 project.4.refs_5_
  16.8 0.0 collective-permute-done.1.refs_0_.refs_2_
  16.8 0.0 slice-start
  16.8 0.7 project.5.refs_6_
  17.6 0.0 slice-start.1
  17.6 2.2 %collective-permute-done.2.refs_3_ = bf16[4,32,768]{2,1,0:T(8,128)(2,1)S(1)} collective-permute-done((bf16[4,32,768]{2,1,0:T(8,128)(2,1)S(1)}, bf16[4,32,768]{2,1,0:T(8,128)(2,1)S(1)}, u32[]{:S(2)}, u32[]{:S(2)}) %collective-permute-start.2) | collective-permute-done | bytes 196640 | tf_op jit(solution)/shard_map/ppermute | solution.py:223
  19.8 3.2 %spatial.1 = bf16[32,16,768]{2,1,0:T(8,128)(2,1)S(1)} custom-call(bf16[4,4,32,768]{3,2,1,0:T(8,128)(2,1)S(1)} %bitcast.16, bf16[4,32,768]{2,1,0:T(8,128)(2,1)S(1)} %collective-permute-done.refs_0_.refs_1_, bf16[4,32,768]{2,1,0:T(8,128)(2,1)S(1)} %collective-permute-done.1.refs_0_.refs_2_, bf16[4,32,768]{2,1,0:T(8,128)(2,1)S(1)} %collective-permute-done.2.refs_3_, ...), custom_call_target="tpu_custom_call" | custom-call | flops 1207959552 | bytes 8650752 | tf_op jit(solution)/shard_map/spatial/pallas_call | solution.py:206
  23.0 28.3 %all_to_all.5 = bf16[32,16,768]{2,1,0:T(8,128)(2,1)S(1)} all-to-all(bf16[32,16,768]{2,1,0:T(8,128)(2,1)S(1)} %spatial.1), channel_id=1, replica_groups=mesh['tm'=8,'space'=4] {'space','tm'}, dimensions={0} | all-to-all | bytes 1572864 | tf_op jit(solution)/shard_map/all_to_all | solution.py:268
  51.3 5.0 %temporal.1 = (bf16[2,64,768]{2,1,0:T(8,128)(2,1)S(1)}, bf16[2,64,768]{2,1,0:T(8,128)(2,1)S(1)}, bf16[2,64,768]{2,1,0:T(8,128)(2,1)S(1)}, bf16[64,768]{1,0:T(8,128)(2,1)S(1)}, bf16[64,768]{1,0:T(8,128)(2,1)S(1)}) custom-call(bf16[4,8,16,768]{3,2,1,0:T(8,128)(2,1)S(1)} %bitcast.17, bf16[4,768,768]{2,1,0:T(8,128)(2,1)S(1)} %bitcast.19), custom_call_target="tpu_custom_call" | custom-call | flops 3019898880 | bytes 6291456 | tf_op jit(solution)/shard_map/temporal/pallas_call | solution.py:206
  56.3 2.5 %collective-permute-start.3 = (bf16[2,64,768]{2,1,0:T(8,128)(2,1)S(1)}, bf16[2,64,768]{2,1,0:T(8,128)(2,1)S(1)}, u32[]{:S(2)}, u32[]{:S(2)}) collective-permute-start(bf16[2,64,768]{2,1,0:T(8,128)(2,1)S(1)} %get-tuple-element.11), channel_id=1, source_target_pairs={{0,24},{4,28},{8,16},{12,20},{16,8},{20,12},{24,0},{28,4},{1,25},{... | collective-permute-start | bytes 589832 | tf_op jit(solution)/shard_map/ppermute | solution.py:290
  58.7 0.1 collective-permute-start.5
  58.8 0.6 collective-permute-start.8
  59.4 1.3 %collective-permute-start.9 = (bf16[64,768]{1,0:T(8,128)(2,1)S(1)}, bf16[64,768]{1,0:T(8,128)(2,1)S(1)}, u32[]{:S(2)}, u32[]{:S(2)}) collective-permute-start(bf16[64,768]{1,0:T(8,128)(2,1)S(1)} %get-tuple-element.14), channel_id=1, source_target_pairs={{0,20},{4,16},{8,28},{12,24},{16,4},{20,0},{24,12},{28,8},{1,21},{... | collective-permute-start | bytes 294920 | tf_op jit(solution)/shard_map/ppermute | solution.py:285
  60.7 0.6 collective-permute-start.4
  61.2 2.8 %collective-permute-done.3.refs_1_ = bf16[2,64,768]{2,1,0:T(8,128)(2,1)S(1)} collective-permute-done((bf16[2,64,768]{2,1,0:T(8,128)(2,1)S(1)}, bf16[2,64,768]{2,1,0:T(8,128)(2,1)S(1)}, u32[]{:S(2)}, u32[]{:S(2)}) %collective-permute-start.3) | collective-permute-done | bytes 196640 | tf_op jit(solution)/shard_map/ppermute | solution.py:290
  64.0 0.1 collective-permute-start.6
  64.1 4.0 %collective-permute-done.4.refs_2_ = bf16[2,64,768]{2,1,0:T(8,128)(2,1)S(1)} collective-permute-done((bf16[2,64,768]{2,1,0:T(8,128)(2,1)S(1)}, bf16[2,64,768]{2,1,0:T(8,128)(2,1)S(1)}, u32[]{:S(2)}, u32[]{:S(2)}) %collective-permute-start.4) | collective-permute-done | bytes 196640 | tf_op jit(solution)/shard_map/ppermute | solution.py:290
  68.1 0.1 collective-permute-start.7
  68.2 0.0 collective-permute-done.5.refs_3_
  68.2 0.0 collective-permute-done.8.refs_6_
  68.2 0.0 collective-permute-done.9.refs_7_
  68.2 0.0 collective-permute-done.6.refs_4_
  68.3 1.2 %collective-permute-done.7.refs_5_ = bf16[64,768]{1,0:T(8,128)(2,1)S(1)} collective-permute-done((bf16[64,768]{1,0:T(8,128)(2,1)S(1)}, bf16[64,768]{1,0:T(8,128)(2,1)S(1)}, u32[]{:S(2)}, u32[]{:S(2)}) %collective-permute-start.7) | collective-permute-done | bytes 98336 | tf_op jit(solution)/shard_map/ppermute | solution.py:294
  69.5 1.5 %place.1 = bf16[16,32,768]{2,1,0:T(8,128)(2,1)} custom-call(bf16[2,64,768]{2,1,0:T(8,128)(2,1)S(1)} %get-tuple-element.10.refs_0_, bf16[2,64,768]{2,1,0:T(8,128)(2,1)S(1)} %collective-permute-done.3.refs_1_, bf16[2,64,768]{2,1,0:T(8,128)(2,1)S(1)} %collective-permute-done.4.refs_2_, bf16[64,768]{1,0:T(8,128)(2,1)S(1)} %collective-permute-done.5.refs_3_, ...), custom_call_target="tpu_custom_call" | custom-call | bytes 1867776 | tf_op jit(solution)/shard_map/place/pallas_call | solution.py:206
  (10 shorter events, 0.0 us)
Async XLA Ops:
  1.2 15.0 %collective-permute-start = (bf16[4,32,768]{2,1,0:T(8,128)(2,1)S(1)}, bf16[4,32,768]{2,1,0:T(8,128)(2,1)S(1)}, u32[]{:S(2)}, u32[]{:S(2)}) collective-permute-start(bf16[4,32,768]{2,1,0:T(8,128)(2,1)S(1)} %get-tuple-element.17), channel_id=1, source_target_pairs={{0,2},{1,3},{2,0},{3,1},{4,6},{5,7},{6,4},{7,5},{8,10},{9,11},{10,... | collective-permute-start | bytes 589832 | tf_op jit(solution)/shard_map/ppermute | solution.py:223
  5.3 11.6 %collective-permute-start.1 = (bf16[4,32,768]{2,1,0:T(8,128)(2,1)S(1)}, bf16[4,32,768]{2,1,0:T(8,128)(2,1)S(1)}, u32[]{:S(2)}, u32[]{:S(2)}) collective-permute-start(bf16[4,32,768]{2,1,0:T(8,128)(2,1)S(1)} %get-tuple-element.16), channel_id=1, source_target_pairs={{0,1},{1,0},{2,3},{3,2},{4,5},{5,4},{6,7},{7,6},{8,9},{9,8},{10,11... | collective-permute-start | bytes 589832 | tf_op jit(solution)/shard_map/ppermute | solution.py:223
  6.8 13.0 %collective-permute-start.2 = (bf16[4,32,768]{2,1,0:T(8,128)(2,1)S(1)}, bf16[4,32,768]{2,1,0:T(8,128)(2,1)S(1)}, u32[]{:S(2)}, u32[]{:S(2)}) collective-permute-start(bf16[4,32,768]{2,1,0:T(8,128)(2,1)S(1)} %get-tuple-element.15), channel_id=1, source_target_pairs={{0,3},{1,2},{2,1},{3,0},{4,7},{5,6},{6,5},{7,4},{8,11},{9,10},{10,... | collective-permute-start | bytes 589832 | tf_op jit(solution)/shard_map/ppermute | solution.py:223
  6.8 2.3 %copy-start = (bf16[4,768,768]{2,1,0:T(8,128)(2,1)S(1)}, bf16[4,768,768]{2,1,0:T(8,128)(2,1)}, u32[]{:S(2)}) copy-start(bf16[4,768,768]{2,1,0:T(8,128)(2,1)} %refs_7_.1) | copy-start | bytes 14155780
  9.2 1.1 %copy-start.2 = (bf16[16,32,768]{2,1,0:T(8,128)(2,1)S(1)}, bf16[16,32,768]{2,1,0:T(8,128)(2,1)}, u32[]{:S(2)}) copy-start(bf16[16,32,768]{2,1,0:T(8,128)(2,1)} %param.3) | copy-start | bytes 2359300
  10.3 5.8 %copy-start.1 = (bf16[4,768,768]{2,1,0:T(8,128)(2,1)S(1)}, bf16[4,768,768]{2,1,0:T(8,128)(2,1)}, u32[]{:S(2)}) copy-start(bf16[4,768,768]{2,1,0:T(8,128)(2,1)} %refs_7_.1) | copy-start | bytes 14155780
  16.8 34.5 %slice-start = ((s8[4718592]{0:T(1024)(128)(4,1)}), s8[4194304]{0:T(1024)(128)(4,1)S(1)}, s32[]{:S(2)}) async-start(s8[4718592]{0:T(1024)(128)(4,1)} %bitcast.18), calls=%async_computation.1 | async-start | bytes 8388608
  17.6 33.7 %slice-start.1 = ((s8[4718592]{0:T(1024)(128)(4,1)}), s8[524288]{0:T(1024)(128)(4,1)S(1)}, s32[]{:S(2)}) async-start(s8[4718592]{0:T(1024)(128)(4,1)} %bitcast.18), calls=%async_computation.2 | async-start | bytes 1048576
  56.3 7.7 %collective-permute-start.3 = (bf16[2,64,768]{2,1,0:T(8,128)(2,1)S(1)}, bf16[2,64,768]{2,1,0:T(8,128)(2,1)S(1)}, u32[]{:S(2)}, u32[]{:S(2)}) collective-permute-start(bf16[2,64,768]{2,1,0:T(8,128)(2,1)S(1)} %get-tuple-element.11), channel_id=1, source_target_pairs={{0,24},{4,28},{8,16},{12,20},{16,8},{20,12},{24,0},{28,4},{1,25},{... | collective-permute-start | bytes 589832 | tf_op jit(solution)/shard_map/ppermute | solution.py:290
  58.7 9.5 %collective-permute-start.5 = (bf16[64,768]{1,0:T(8,128)(2,1)S(1)}, bf16[64,768]{1,0:T(8,128)(2,1)S(1)}, u32[]{:S(2)}, u32[]{:S(2)}) collective-permute-start(bf16[64,768]{1,0:T(8,128)(2,1)S(1)} %slice_bitcast_fusion.2), channel_id=1, source_target_pairs={{0,4},{4,0},{8,12},{12,8},{16,20},{20,16},{24,28},{28,24},{1,5},{5... | collective-permute-start | bytes 294920 | tf_op jit(solution)/shard_map/ppermute | solution.py:294
  58.8 9.4 %collective-permute-start.8 = (bf16[64,768]{1,0:T(8,128)(2,1)S(1)}, bf16[64,768]{1,0:T(8,128)(2,1)S(1)}, u32[]{:S(2)}, u32[]{:S(2)}) collective-permute-start(bf16[64,768]{1,0:T(8,128)(2,1)S(1)} %get-tuple-element.13), channel_id=1, source_target_pairs={{0,16},{4,20},{8,24},{12,28},{16,0},{20,4},{24,8},{28,12},{1,17},{... | collective-permute-start | bytes 294920 | tf_op jit(solution)/shard_map/ppermute | solution.py:285
  59.4 8.8 %collective-permute-start.9 = (bf16[64,768]{1,0:T(8,128)(2,1)S(1)}, bf16[64,768]{1,0:T(8,128)(2,1)S(1)}, u32[]{:S(2)}, u32[]{:S(2)}) collective-permute-start(bf16[64,768]{1,0:T(8,128)(2,1)S(1)} %get-tuple-element.14), channel_id=1, source_target_pairs={{0,20},{4,16},{8,28},{12,24},{16,4},{20,0},{24,12},{28,8},{1,21},{... | collective-permute-start | bytes 294920 | tf_op jit(solution)/shard_map/ppermute | solution.py:285
  60.7 7.5 %collective-permute-start.4 = (bf16[2,64,768]{2,1,0:T(8,128)(2,1)S(1)}, bf16[2,64,768]{2,1,0:T(8,128)(2,1)S(1)}, u32[]{:S(2)}, u32[]{:S(2)}) collective-permute-start(bf16[2,64,768]{2,1,0:T(8,128)(2,1)S(1)} %get-tuple-element.12), channel_id=1, source_target_pairs={{0,8},{4,12},{8,0},{12,4},{16,24},{20,28},{24,16},{28,20},{1,9},{5... | collective-permute-start | bytes 589832 | tf_op jit(solution)/shard_map/ppermute | solution.py:290
  64.0 4.2 %collective-permute-start.6 = (bf16[64,768]{1,0:T(8,128)(2,1)S(1)}, bf16[64,768]{1,0:T(8,128)(2,1)S(1)}, u32[]{:S(2)}, u32[]{:S(2)}) collective-permute-start(bf16[64,768]{1,0:T(8,128)(2,1)S(1)} %slice_bitcast_fusion.1), channel_id=1, source_target_pairs={{0,4},{4,0},{8,12},{12,8},{16,20},{20,16},{24,28},{28,24},{1,5},{5... | collective-permute-start | bytes 294920 | tf_op jit(solution)/shard_map/ppermute | solution.py:294
  68.1 1.4 %collective-permute-start.7 = (bf16[64,768]{1,0:T(8,128)(2,1)S(1)}, bf16[64,768]{1,0:T(8,128)(2,1)S(1)}, u32[]{:S(2)}, u32[]{:S(2)}) collective-permute-start(bf16[64,768]{1,0:T(8,128)(2,1)S(1)} %slice_bitcast_fusion), channel_id=1, source_target_pairs={{0,4},{4,0},{8,12},{12,8},{16,20},{20,16},{24,28},{28,24},{1,5},{5... | collective-permute-start | bytes 294920 | tf_op jit(solution)/shard_map/ppermute | solution.py:294

commit v4 on v3

--- a/solution.py
+++ b/solution.py
@@ -30,20 +30,42 @@
     return jnp.where(first, one, zero).astype(BF16), jnp.where(first, zero, one).astype(BF16)
 
 
-def reorder(values, source, rows=None, first=0):
-    rows = rows or values.shape[0]
-    wanted = source(lax.broadcasted_iota(jnp.int32, (rows, 1), 0) + first)
-    place = lax.broadcasted_iota(jnp.int32, (rows, values.shape[0]), 1)
-    chosen = jnp.where(place == wanted, 1.0, 0.0).astype(BF16)
-    return dot(chosen, values).astype(BF16)
-
-
 def digits(number, *sizes):
     found = []
     for size in reversed(sizes):
         found.append(number & (size - 1))
         number = number >> (size.bit_length() - 1)
     return found[::-1]
+
+
+def orders(rows, *, count, groups, share):
+    toks, frames = groups * share, rows // (groups * share)
+    per = frames // count
+
+    def leave_space(row):
+        k, g, f, t = digits(row, count, groups, per, share)
+        return f * count * toks + k * toks + g * share + t
+
+    def enter_time(row):
+        t, m, s, i = digits(row, share, groups, count, per)
+        return ((s * groups + m) * per + i) * share + t
+
+    def leave_time(row, me):
+        f, g, t = digits(row, frames, groups, share)
+        return ((g ^ me) * share + t) * frames + f
+
+    return leave_space, enter_time, leave_time
+
+
+def table_kernel(_, *out_refs, **sizes):
+    rows = out_refs[0].shape[0]
+    leave_space, enter_time, leave_time = orders(rows, **sizes)
+    me = lax.axis_index("tm")
+    row = lax.broadcasted_iota(jnp.int32, (rows, 1), 0)
+    place = lax.broadcasted_iota(jnp.int32, (rows, rows), 1)
+    wanted = [leave_space(row), enter_time(row), leave_time(row, me)]
+    for out_ref, source in zip(out_refs, wanted):
+        out_ref[...] = jnp.where(place == source, 1.0, 0.0).astype(BF16)
 
 
 def group_of(width):
@@ -105,7 +127,7 @@
 def space_kernel(*refs, distances, groups):
     count = len(distances)
     clip_refs, refs = refs[:count], refs[count:]
-    *qkv_refs, w_ref, out_ref, mix_ref, last_ref = refs
+    *qkv_refs, w_ref, order_ref, out_ref, mix_ref, last_ref = refs
     project(clip_refs[count - last_ref.shape[1] :], w_ref, last_ref)
     qkv_refs = [*qkv_refs, last_ref]
     frames, toks, width = clip_refs[0].shape[1:]
@@ -129,31 +151,21 @@
         [own_or_whole(c, f) for f in range(frames) for c in clip_refs], axis=0
     )
     after = (dot(mix_ref[...], w_ref[3]) + clip.astype(F32)).astype(BF16)
-
-    def source(row):
-        k, g, f, t = digits(row, count, groups, frames, share)
-        return f * rows + k * toks + g * share + t
-
-    after = reorder(after, source).reshape(count, groups, block, width)
+    after = dot(order_ref[...], after).astype(BF16).reshape(count, groups, block, width)
     me = lax.axis_index("space")
     for i, k in enumerate(distances):
         out_ref[pl.ds((me ^ k) * groups, groups)] = after[i]
 
 
-def time_kernel(x_ref, w_ref, *refs, toks, last):
+def time_kernel(x_ref, w_ref, order_ref, *refs, toks, both, direct):
     *out_refs, qkv_ref, mix_ref, done_ref = refs
     space, groups, block, width = x_ref.shape
     rows = space * groups * block
     frames = rows // toks
-    per = block // toks
     masks = halves(frames)
     group = group_of(width)
 
-    def source(row):
-        t, m, s, i = digits(row, toks, groups, space, per)
-        return ((s * groups + m) * per + i) * toks + t
-
-    x = reorder(x_ref[...].reshape(rows, width), source)
+    x = dot(order_ref[...], x_ref[...].reshape(rows, width)).astype(BF16)
     normed = rms_norm(x)
     for j in range(3):
         qkv_ref[j] = dot(normed, w_ref[j]).astype(BF16)
@@ -173,30 +185,30 @@
         for t in range(toks):
             at = pl.multiple_of(t * frames + (me ^ k) * own, own)
             block = done_ref[pl.ds(at, own), :]
-            if k // 2 == last:
-                out_refs[groups // 2 - 1 + k % 2][pl.ds(t * own, own), :] = block
+            if k // 2 in both:
+                out_refs[both.index(k // 2)][k % 2, pl.ds(t * own, own), :] = block
             else:
-                out_refs[k // 2 - (k // 2 > last)][k % 2, pl.ds(t * own, own), :] = block
-
-
-def place_kernel(*refs, order, groups, toks):
-    *in_refs, out_ref = refs
-    frames, _, width = in_refs[-1].shape[0] * groups // toks, 0, in_refs[-1].shape[1]
-    steps = frames // out_ref.shape[0]
-    share = toks // groups
-    far = groups // 2
-    me = lax.axis_index("tm")
-    first = pl.program_id(0) * (frames // steps * toks)
-
-    def source(row):
-        f, g, t = digits(row, frames, groups, share)
-        return ((g ^ me) * share + t) * frames + f
-
-    pairs = {k: (in_refs[i].at[0], in_refs[far - 1 + i]) for i, k in enumerate(order[:-1])}
-    pairs[order[-1]] = in_refs[-2:]
-    rows = jnp.concatenate([part[...] for k in range(far) for part in pairs[k]], axis=0)
-    done = reorder(rows, source, frames // steps * toks, first)
-    out_ref[...] = done.reshape(out_ref.shape)
+                out_refs[len(both) + direct.index(k)][pl.ds(t * own, own), :] = block
+
+
+def place_kernel(*refs, both, direct):
+    *in_refs, order_ref, out_ref, done_ref, sems = refs
+    frames, toks, width = out_ref.shape
+    parts = {2 * k: in_refs[i].at[0] for i, k in enumerate(both)}
+    parts |= {2 * k + 1: in_refs[len(both) + i] for i, k in enumerate(both)}
+    parts |= {k: in_refs[2 * len(both) + i] for i, k in enumerate(direct)}
+    rows = jnp.concatenate([parts[k][...] for k in range(len(parts))], axis=0)
+    steps = sems.shape[0]
+    some = frames // steps
+    copies = []
+    for step in range(steps):
+        at = pl.ds(step * some, some)
+        done = dot(order_ref[pl.ds(step * some * toks, some * toks), :], rows).astype(BF16)
+        done_ref[at] = done.reshape(some, toks, width)
+        copies.append(pltpu.make_async_copy(done_ref.at[at], out_ref.at[at], sems.at[step]))
+        copies[-1].start()
+    for copy in copies:
+        copy.wait()
 
 
 def call(kernel, name, outs, *args, scratch=(), flops=0, **blocks):
@@ -236,9 +248,13 @@
 
     blocks = clip.reshape(space, *piece)
     me = lax.axis_index("space")
-    parts = [blocks] + [
-        lax.dynamic_index_in_dim(blocks, me ^ k, 0, keepdims=False) for k in range(1, space)
-    ]
+    near = sorted(range(1, space), key=lambda k: (k == 1, k))
+    parts = {0: blocks}
+    held = blocks
+    for k in near:
+        parts[k] = lax.dynamic_index_in_dim(held, me ^ k, 0, keepdims=False)
+        held = lax.optimization_barrier((blocks, parts[k]))[0]
+    parts = [parts[k] for k in range(space)]
     parts = exchange(parts, "space", sorted(range(1, space), key=lambda k: (k == 1, k)))
     groups = [[0], [2], [1], [*range(3, space)]] if space > 3 else [[*range(space)]]
     qkv = [
@@ -252,6 +268,14 @@
         )[0]
         for group in groups[:-1]
     ]
+    leave_space, enter_time, leave_time = call(
+        functools.partial(
+            table_kernel, count=space, groups=tm, share=share
+        ),
+        "orders",
+        [(rows, rows)] * 3,
+        qkv[0] if qkv else parts[0],
+    )
     after = call(
         functools.partial(space_kernel, distances=sum(groups, []), groups=tm),
         "spatial",
@@ -259,6 +283,7 @@
         *[parts[k] for k in sum(groups, [])],
         *qkv,
         w_spatial,
+        leave_space,
         scratch=[
             pltpu.VMEM((rows, width), BF16),
             pltpu.VMEM((3, len(groups[-1]), *piece), BF16),
@@ -266,13 +291,15 @@
         flops=2 * cost,
     )[0]
     after = lax.all_to_all(after, ("space", "tm"), split_axis=0, concat_axis=0, tiled=True)
-    order = [0, *sorted(range(1, tm // 2), key=lambda k: (-k.bit_count(), k))]
+    both = [k for k in range(tm // 2) if k.bit_count() != 1]
+    direct = [2 * k + s for s in range(2) for k in reversed(range(tm // 2)) if k not in both]
     result = call(
-        functools.partial(time_kernel, toks=share, last=order[-1]),
+        functools.partial(time_kernel, toks=share, both=both, direct=direct),
         "temporal",
-        [(2, rows // tm, width)] * (tm // 2 - 1) + [(rows // tm, width)] * 2,
+        [(2, rows // tm, width)] * len(both) + [(rows // tm, width)] * len(direct),
         after.reshape(space, tm, block, width),
         w_temporal,
+        enter_time,
         scratch=[
             pltpu.VMEM((3, rows, width), BF16),
             pltpu.VMEM((rows, width), BF16),
@@ -280,30 +307,27 @@
         ],
         flops=5 * cost,
     )
-    last = order[-1]
-    direct = [
-        lax.ppermute(part, "tm", [(i, i ^ (2 * last + s)) for i in range(tm)])
-        for s, part in enumerate(result[-2:])
-    ]
-    whole = dict(zip([k for k in range(tm // 2) if k != last], result))
-    whole = {
-        k: lax.ppermute(part, "tm", [(i, i ^ (2 * k)) for i in range(tm)]) if k else part
-        for k, part in whole.items()
-    }
-    beside = {
-        k: lax.ppermute(part[1], "tm", [(i, i ^ 1) for i in range(tm)])
-        for k, part in whole.items()
-    }
-    steps = 2 if frames % 2 == 0 else 1
+
+    def over_tm(part, distance):
+        return lax.ppermute(part, "tm", [(i, i ^ distance) for i in range(tm)])
+
+    whole = [over_tm(part, 2 * k) if k else part for k, part in zip(both, result)]
+    beside = [over_tm(part[1], 1) for part in whole]
+    near = [over_tm(part, k) for k, part in zip(direct, result[len(both) :])]
+    steps = 4 if frames % 4 == 0 else 1
     return call(
-        functools.partial(place_kernel, order=order, groups=tm, toks=toks),
+        functools.partial(place_kernel, both=both, direct=direct),
         "place",
         [(frames, toks, width)],
-        *[whole[k] for k in order[:-1]],
-        *[beside[k] for k in order[:-1]],
-        *direct,
-        grid=(steps,),
-        out_specs=[pl.BlockSpec((frames // steps, toks, width), lambda i: (i, 0, 0))],
+        *whole,
+        *beside,
+        *near,
+        leave_time,
+        out_specs=[pl.BlockSpec(memory_space=pl.ANY)],
+        scratch=[
+            pltpu.VMEM((frames, toks, width), BF16),
+            pltpu.SemaphoreType.DMA((steps,)),
+        ],
     )[0]
 
 

time: 71.2 us -> 70.4 us (0.989)
  waiting for transfers between devices: 15.4 us -> 12.4 us
  starting transfers between devices: 10.8 us -> 12.6 us
  blocking collectives: 28.3 us -> 26.6 us
  local copies, waits for them, and re-layouts: 4.66 us -> 6.33 us
    ppermute x7, waiting for transfers between devices: 8.05 us -> 5.9 us  [over_tm(): return lax.ppermute(part, 'tm', [(i, i ^ distance) for i in range(tm)])]
    ppermute x7, starting transfers between devices: 5.1 us -> 6.88 us  [over_tm(): return lax.ppermute(part, 'tm', [(i, i ^ distance) for i in range(tm)])]
    all_to_all x1, blocking collectives: 28.3 us -> 26.6 us  [on_device(): lax.all_to_all(after, ('space', 'tm'), split_axis=0, concat_axis=0, tiled...]
    squeeze x4 -> x5, local copies, waits for them, and re-layouts: 1.18 us -> 2.84 us  [the longest x3 2.82 us: on_device(): parts[k] = lax.dynamic_index_in_dim(held, me ^ k, 0, keepdims=False)]
    ppermute x3, waiting for transfers between devices: 7.31 us -> 6.53 us  [exchange(): lax.ppermute(pieces[k], axis, [(i, i ^ k * unit) for i in range(count)])]
    pallas_call x6 -> x7, Pallas kernels: 11.8 us -> 12 us  [call(): pl.pallas_call(kernel, out_shape=like, in_specs=[within] * len(args), out...]
    unnamed x10 -> x12, local copies, waits for them, and re-layouts: 3.49 us -> 3.49 us
  transfers between devices with their start and end apart: 10 -> 10, of which waited for: 5 -> 5; matrix products, arithmetic and copies ran while one was open for 0% -> 3% of each run, Pallas kernels for 3% -> 4%
where the time goes in v4:
time: 70.4 us; the launch traced here: 70.1 us
  blocking collectives  26.6 us (38%)
  starting transfers between devices  12.6 us (18%)
  waiting for transfers between devices  12.4 us (18%)
  Pallas kernels  12 us (17%)
  local copies, waits for them, and re-layouts  6.33 us (9%)
    all_to_all x1, blocking collectives, on_device(): lax.all_to_all(after, ('space', 'tm'), split_axis=0, concat_axis=0, tiled...  26.6 us
    pallas_call x7, Pallas kernels, call(): pl.pallas_call(kernel, out_shape=like, in_specs=[within] * len(args), out...  12 us
    ppermute x7, starting transfers between devices, over_tm(): return lax.ppermute(part, 'tm', [(i, i ^ distance) for i in range(tm)])  6.88 us
    ppermute x3, waiting for transfers between devices, exchange(): lax.ppermute(pieces[k], axis, [(i, i ^ k * unit) for i in range(count)])  6.53 us
    ppermute x7, waiting for transfers between devices, over_tm(): return lax.ppermute(part, 'tm', [(i, i ^ distance) for i in range(tm)])  5.9 us
    ppermute x3, starting transfers between devices, exchange(): lax.ppermute(pieces[k], axis, [(i, i ^ k * unit) for i in range(count)])  5.75 us
    unnamed x12, local copies, waits for them, and re-layouts  3.49 us
    squeeze x3, local copies, waits for them, and re-layouts, on_device(): parts[k] = lax.dynamic_index_in_dim(held, me ^ k, 0, keepdims=False)  2.82 us
  transfers between devices with their start and end apart: 10, of which 5 were waited for; matrix products, arithmetic and copies ran while one was open for 3% of the time, Pallas kernels for 4%

profile of v4, /device:TPU:0, one launch (start us, length us, event | category | flops | bytes accessed | tf_op | source)
XLA Modules:
  0.0 70.1 jit_solution(5547529449481693893)
XLA Ops:
  0.0 0.9 %dynamic-slice_bitcast_fusion.2 = bf16[4,32,768]{2,1,0:T(8,128)(2,1)S(1)} fusion(bf16[4,4,32,768]{3,2,1,0:T(8,128)(2,1)} %bitcast.12, s32[]{:T(128)S(6)} %select_n.10), kind=kLoop, calls=%fused_computation.2 | loop fusion | bytes 393220 | tf_op jit(solution)/shard_map/jit(dynamic_index_in_dim)/squeeze | solution.py:255
  0.9 4.1 %collective-permute-start = (bf16[4,32,768]{2,1,0:T(8,128)(2,1)S(1)}, bf16[4,32,768]{2,1,0:T(8,128)(2,1)S(1)}, u32[]{:S(2)}, u32[]{:S(2)}) collective-permute-start(bf16[4,32,768]{2,1,0:T(8,128)(2,1)S(1)} %dynamic-slice_bitcast_fusion.2), channel_id=1, source_target_pairs={{0,2},{1,3},{2,0},{3,1},{4,6},{5,7},{6,4},{7,5},{8,10},{9,11},{10,... | collective-permute-start | bytes 589832 | tf_op jit(solution)/shard_map/ppermute | solution.py:235
  5.0 0.9 %dynamic-slice_bitcast_fusion.1 = bf16[4,32,768]{2,1,0:T(8,128)(2,1)S(1)} fusion(bf16[4,4,32,768]{3,2,1,0:T(8,128)(2,1)} %bitcast.13, s32[]{:T(128)S(6)} %select_n.11), kind=kLoop, calls=%fused_computation.1 | loop fusion | bytes 393220 | tf_op jit(solution)/shard_map/jit(dynamic_index_in_dim)/squeeze | solution.py:255
  6.0 0.9 %dynamic-slice_bitcast_fusion = bf16[4,32,768]{2,1,0:T(8,128)(2,1)S(1)} fusion(bf16[4,4,32,768]{3,2,1,0:T(8,128)(2,1)} %bitcast.14, s32[]{:T(128)S(6)} %select_n.12), kind=kLoop, calls=%fused_computation | loop fusion | bytes 393220 | tf_op jit(solution)/shard_map/jit(dynamic_index_in_dim)/squeeze | solution.py:255
  6.9 1.6 %collective-permute-start.1 = (bf16[4,32,768]{2,1,0:T(8,128)(2,1)S(1)}, bf16[4,32,768]{2,1,0:T(8,128)(2,1)S(1)}, u32[]{:S(2)}, u32[]{:S(2)}) collective-permute-start(bf16[4,32,768]{2,1,0:T(8,128)(2,1)S(1)} %dynamic-slice_bitcast_fusion), channel_id=1, source_target_pairs={{0,1},{1,0},{2,3},{3,2},{4,5},{5,4},{6,7},{7,6},{8,9},{9,8},{10,11... | collective-permute-start | bytes 589832 | tf_op jit(solution)/shard_map/ppermute | solution.py:235
  8.6 0.0 collective-permute-start.2
  8.6 2.3 %copy-done = bf16[4,768,768]{2,1,0:T(8,128)(2,1)S(1)} copy-done((bf16[4,768,768]{2,1,0:T(8,128)(2,1)S(1)}, bf16[4,768,768]{2,1,0:T(8,128)(2,1)}, u32[]{:S(2)}) %copy-start) | copy-done | bytes 4718616
  10.9 1.1 %copy-done.2 = bf16[16,32,768]{2,1,0:T(8,128)(2,1)S(1)} copy-done((bf16[16,32,768]{2,1,0:T(8,128)(2,1)S(1)}, bf16[16,32,768]{2,1,0:T(8,128)(2,1)}, u32[]{:S(2)}) %copy-start.2) | copy-done | bytes 786456
  12.1 0.7 %project.3._.refs_4_ = bf16[3,1,4,32,768]{4,3,2,1,0:T(8,128)(2,1)S(1)} custom-call(bf16[4,4,32,768]{3,2,1,0:T(8,128)(2,1)S(1)} %bitcast.15, bf16[4,768,768]{2,1,0:T(8,128)(2,1)S(1)} %copy-done), custom_call_target="tpu_custom_call" | custom-call | flops 452984832 | bytes 6094848 | tf_op jit(solution)/shard_map/project/pallas_call | solution.py:218
  12.8 0.6 orders.1
  13.4 0.0 copy-start.3
  13.4 2.5 %collective-permute-done.refs_0_.refs_1_ = bf16[4,32,768]{2,1,0:T(8,128)(2,1)S(1)} collective-permute-done((bf16[4,32,768]{2,1,0:T(8,128)(2,1)S(1)}, bf16[4,32,768]{2,1,0:T(8,128)(2,1)S(1)}, u32[]{:S(2)}, u32[]{:S(2)}) %collective-permute-start) | collective-permute-done | bytes 196640 | tf_op jit(solution)/shard_map/ppermute | solution.py:235
  15.9 0.7 project.4.refs_5_
  16.6 4.0 %collective-permute-done.1.refs_0_.refs_2_ = bf16[4,32,768]{2,1,0:T(8,128)(2,1)S(1)} collective-permute-done((bf16[4,32,768]{2,1,0:T(8,128)(2,1)S(1)}, bf16[4,32,768]{2,1,0:T(8,128)(2,1)S(1)}, u32[]{:S(2)}, u32[]{:S(2)}) %collective-permute-start.1) | collective-permute-done | bytes 196640 | tf_op jit(solution)/shard_map/ppermute | solution.py:235
  20.6 0.7 project.5.refs_6_
  21.3 0.0 collective-permute-done.2.refs_3_
  21.4 0.0 slice-start.1
  21.4 3.1 %spatial.1 = bf16[32,16,768]{2,1,0:T(8,128)(2,1)S(1)} custom-call(bf16[4,4,32,768]{3,2,1,0:T(8,128)(2,1)S(1)} %bitcast.16, bf16[4,32,768]{2,1,0:T(8,128)(2,1)S(1)} %collective-permute-done.refs_0_.refs_1_, bf16[4,32,768]{2,1,0:T(8,128)(2,1)S(1)} %collective-permute-done.1.refs_0_.refs_2_, bf16[4,32,768]{2,1,0:T(8,128)(2,1)S(1)} %collective-permute-done.2.refs_3_, ...), custom_call_target="tpu_custom_call" | custom-call | flops 1207959552 | bytes 9175040 | tf_op jit(solution)/shard_map/spatial/pallas_call | solution.py:218
  24.5 26.6 %all_to_all.5 = bf16[32,16,768]{2,1,0:T(8,128)(2,1)S(1)} all-to-all(bf16[32,16,768]{2,1,0:T(8,128)(2,1)S(1)} %spatial.1), channel_id=1, replica_groups=mesh['tm'=8,'space'=4] {'space','tm'}, dimensions={0} | all-to-all | bytes 1572864 | tf_op jit(solution)/shard_map/all_to_all | solution.py:293
  51.1 4.9 %temporal.1 = (bf16[2,64,768]{2,1,0:T(8,128)(2,1)S(1)}, bf16[2,64,768]{2,1,0:T(8,128)(2,1)S(1)}, bf16[64,768]{1,0:T(8,128)(2,1)S(1)}, bf16[64,768]{1,0:T(8,128)(...) custom-call(bf16[4,8,16,768]{3,2,1,0:T(8,128)(2,1)S(1)} %bitcast.17, ...), custom_call_target="tpu_custom_call" | custom-call | flops 3019898880 | bytes 6815744 | tf_op jit(solution)/shard_map/temporal/pallas_call | solution.py:218
  56.0 2.5 %collective-permute-start.3 = (bf16[2,64,768]{2,1,0:T(8,128)(2,1)S(1)}, bf16[2,64,768]{2,1,0:T(8,128)(2,1)S(1)}, u32[]{:S(2)}, u32[]{:S(2)}) collective-permute-start(bf16[2,64,768]{2,1,0:T(8,128)(2,1)S(1)} %get-tuple-element.21), channel_id=1, source_target_pairs={{0,24},{4,28},{8,16},{12,20},{16,8},{20,12},{24,0},{28,4},{1,25},{... | collective-permute-start | bytes 589832 | tf_op jit(solution)/shard_map/ppermute | solution.py:312
  58.5 0.1 collective-permute-start.4
  58.5 0.6 collective-permute-start.6
  59.1 0.6 collective-permute-start.7
  59.7 1.0 %collective-permute-start.8 = (bf16[64,768]{1,0:T(8,128)(2,1)S(1)}, bf16[64,768]{1,0:T(8,128)(2,1)S(1)}, u32[]{:S(2)}, u32[]{:S(2)}) collective-permute-start(bf16[64,768]{1,0:T(8,128)(2,1)S(1)} %get-tuple-element.24), channel_id=1, source_target_pairs={{0,20},{4,16},{8,28},{12,24},{16,4},{20,0},{24,12},{28,8},{1,21},{... | collective-permute-start | bytes 294920 | tf_op jit(solution)/shard_map/ppermute | solution.py:312
  60.7 3.5 %collective-permute-done.3.refs_1_ = bf16[2,64,768]{2,1,0:T(8,128)(2,1)S(1)} collective-permute-done((bf16[2,64,768]{2,1,0:T(8,128)(2,1)S(1)}, bf16[2,64,768]{2,1,0:T(8,128)(2,1)S(1)}, u32[]{:S(2)}, u32[]{:S(2)}) %collective-permute-start.3) | collective-permute-done | bytes 196640 | tf_op jit(solution)/shard_map/ppermute | solution.py:312
  64.2 0.2 collective-permute-start.9
  64.4 0.0 collective-permute-done.4.refs_2_
  64.4 2.0 %collective-permute-start.5 = (bf16[64,768]{1,0:T(8,128)(2,1)S(1)}, bf16[64,768]{1,0:T(8,128)(2,1)S(1)}, u32[]{:S(2)}, u32[]{:S(2)}) collective-permute-start(bf16[64,768]{1,0:T(8,128)(2,1)S(1)} %slice_bitcast_fusion), channel_id=1, source_target_pairs={{0,4},{4,0},{8,12},{12,8},{16,20},{20,16},{24,28},{28,24},{1,5},{5... | collective-permute-start | bytes 294920 | tf_op jit(solution)/shard_map/ppermute | solution.py:312
  66.4 1.3 %collective-permute-done.8.refs_6_ = bf16[64,768]{1,0:T(8,128)(2,1)S(1)} collective-permute-done((bf16[64,768]{1,0:T(8,128)(2,1)S(1)}, bf16[64,768]{1,0:T(8,128)(2,1)S(1)}, u32[]{:S(2)}, u32[]{:S(2)}) %collective-permute-start.8) | collective-permute-done | bytes 98336 | tf_op jit(solution)/shard_map/ppermute | solution.py:312
  67.7 1.1 %collective-permute-done.9.refs_7_ = bf16[64,768]{1,0:T(8,128)(2,1)S(1)} collective-permute-done((bf16[64,768]{1,0:T(8,128)(2,1)S(1)}, bf16[64,768]{1,0:T(8,128)(2,1)S(1)}, u32[]{:S(2)}, u32[]{:S(2)}) %collective-permute-start.9) | collective-permute-done | bytes 98336 | tf_op jit(solution)/shard_map/ppermute | solution.py:312
  68.8 1.3 %place.1 = bf16[16,32,768]{2,1,0:T(8,128)(2,1)} custom-call(bf16[2,64,768]{2,1,0:T(8,128)(2,1)S(1)} %get-tuple-element.20.refs_0_, bf16[2,64,768]{2,1,0:T(8,128)(2,1)S(1)} %collective-permute-done.3.refs_1_, bf16[64,768]{1,0:T(8,128)(2,1)S(1)} %collective-permute-done.4.refs_2_, bf16[64,768]{1,0:T(8,128)(2,1)S(1)} %collective-permute-done.5.refs_3_, ...), custom_call_target="tpu_custom_call" | custom-call | bytes 2293760 | tf_op jit(solution)/shard_map/place/pallas_call | solution.py:218
  (14 shorter events, 0.0 us)
Async XLA Ops:
  0.9 15.0 %collective-permute-start = (bf16[4,32,768]{2,1,0:T(8,128)(2,1)S(1)}, bf16[4,32,768]{2,1,0:T(8,128)(2,1)S(1)}, u32[]{:S(2)}, u32[]{:S(2)}) collective-permute-start(bf16[4,32,768]{2,1,0:T(8,128)(2,1)S(1)} %dynamic-slice_bitcast_fusion.2), channel_id=1, source_target_pairs={{0,2},{1,3},{2,0},{3,1},{4,6},{5,7},{6,4},{7,5},{8,10},{9,11},{10,... | collective-permute-start | bytes 589832 | tf_op jit(solution)/shard_map/ppermute | solution.py:235
  6.9 13.7 %collective-permute-start.1 = (bf16[4,32,768]{2,1,0:T(8,128)(2,1)S(1)}, bf16[4,32,768]{2,1,0:T(8,128)(2,1)S(1)}, u32[]{:S(2)}, u32[]{:S(2)}) collective-permute-start(bf16[4,32,768]{2,1,0:T(8,128)(2,1)S(1)} %dynamic-slice_bitcast_fusion), channel_id=1, source_target_pairs={{0,1},{1,0},{2,3},{3,2},{4,5},{5,4},{6,7},{7,6},{8,9},{9,8},{10,11... | collective-permute-start | bytes 589832 | tf_op jit(solution)/shard_map/ppermute | solution.py:235
  8.6 12.8 %collective-permute-start.2 = (bf16[4,32,768]{2,1,0:T(8,128)(2,1)S(1)}, bf16[4,32,768]{2,1,0:T(8,128)(2,1)S(1)}, u32[]{:S(2)}, u32[]{:S(2)}) collective-permute-start(bf16[4,32,768]{2,1,0:T(8,128)(2,1)S(1)} %dynamic-slice_bitcast_fusion.1), channel_id=1, source_target_pairs={{0,3},{1,2},{2,1},{3,0},{4,7},{5,6},{6,5},{7,4},{8,11},{9,10},{10,... | collective-permute-start | bytes 589832 | tf_op jit(solution)/shard_map/ppermute | solution.py:235
  8.6 2.3 %copy-start = (bf16[4,768,768]{2,1,0:T(8,128)(2,1)S(1)}, bf16[4,768,768]{2,1,0:T(8,128)(2,1)}, u32[]{:S(2)}) copy-start(bf16[4,768,768]{2,1,0:T(8,128)(2,1)} %refs_7_.1) | copy-start | bytes 14155780
  10.9 1.1 %copy-start.2 = (bf16[16,32,768]{2,1,0:T(8,128)(2,1)S(1)}, bf16[16,32,768]{2,1,0:T(8,128)(2,1)}, u32[]{:S(2)}) copy-start(bf16[16,32,768]{2,1,0:T(8,128)(2,1)} %param.3) | copy-start | bytes 2359300
  12.1 3.8 %copy-start.1 = (bf16[4,768,768]{2,1,0:T(8,128)(2,1)S(1)}, bf16[4,768,768]{2,1,0:T(8,128)(2,1)}, u32[]{:S(2)}) copy-start(bf16[4,768,768]{2,1,0:T(8,128)(2,1)} %refs_7_.1) | copy-start | bytes 14155780
  13.4 8.0 %copy-start.3 = (bf16[16,32,768]{2,1,0:T(8,128)(2,1)S(1)}, bf16[16,32,768]{2,1,0:T(8,128)(2,1)}, u32[]{:S(2)}) copy-start(bf16[16,32,768]{2,1,0:T(8,128)(2,1)} %param.3) | copy-start | bytes 2359300
  20.6 30.5 %slice-start = ((s8[4718592]{0:T(1024)(128)(4,1)}), s8[4194304]{0:T(1024)(128)(4,1)S(1)}, s32[]{:S(2)}) async-start(s8[4718592]{0:T(1024)(128)(4,1)} %bitcast.18), calls=%async_computation.1 | async-start | bytes 8388608
  21.4 29.7 %slice-start.1 = ((s8[4718592]{0:T(1024)(128)(4,1)}), s8[524288]{0:T(1024)(128)(4,1)S(1)}, s32[]{:S(2)}) async-start(s8[4718592]{0:T(1024)(128)(4,1)} %bitcast.18), calls=%async_computation.2 | async-start | bytes 1048576
  56.0 8.2 %collective-permute-start.3 = (bf16[2,64,768]{2,1,0:T(8,128)(2,1)S(1)}, bf16[2,64,768]{2,1,0:T(8,128)(2,1)S(1)}, u32[]{:S(2)}, u32[]{:S(2)}) collective-permute-start(bf16[2,64,768]{2,1,0:T(8,128)(2,1)S(1)} %get-tuple-element.21), channel_id=1, source_target_pairs={{0,24},{4,28},{8,16},{12,20},{16,8},{20,12},{24,0},{28,4},{1,25},{... | collective-permute-start | bytes 589832 | tf_op jit(solution)/shard_map/ppermute | solution.py:312
  58.5 5.9 %collective-permute-start.4 = (bf16[64,768]{1,0:T(8,128)(2,1)S(1)}, bf16[64,768]{1,0:T(8,128)(2,1)S(1)}, u32[]{:S(2)}, u32[]{:S(2)}) collective-permute-start(bf16[64,768]{1,0:T(8,128)(2,1)S(1)} %slice_bitcast_fusion.1), channel_id=1, source_target_pairs={{0,4},{4,0},{8,12},{12,8},{16,20},{20,16},{24,28},{28,24},{1,5},{5... | collective-permute-start | bytes 294920 | tf_op jit(solution)/shard_map/ppermute | solution.py:312
  58.5 7.9 %collective-permute-start.6 = (bf16[64,768]{1,0:T(8,128)(2,1)S(1)}, bf16[64,768]{1,0:T(8,128)(2,1)S(1)}, u32[]{:S(2)}, u32[]{:S(2)}) collective-permute-start(bf16[64,768]{1,0:T(8,128)(2,1)S(1)} %get-tuple-element.22), channel_id=1, source_target_pairs={{0,16},{4,20},{8,24},{12,28},{16,0},{20,4},{24,8},{28,12},{1,17},{... | collective-permute-start | bytes 294920 | tf_op jit(solution)/shard_map/ppermute | solution.py:312
  59.1 7.3 %collective-permute-start.7 = (bf16[64,768]{1,0:T(8,128)(2,1)S(1)}, bf16[64,768]{1,0:T(8,128)(2,1)S(1)}, u32[]{:S(2)}, u32[]{:S(2)}) collective-permute-start(bf16[64,768]{1,0:T(8,128)(2,1)S(1)} %get-tuple-element.23), channel_id=1, source_target_pairs={{0,8},{4,12},{8,0},{12,4},{16,24},{20,28},{24,16},{28,20},{1,9},{5... | collective-permute-start | bytes 294920 | tf_op jit(solution)/shard_map/ppermute | solution.py:312
  59.7 8.0 %collective-permute-start.8 = (bf16[64,768]{1,0:T(8,128)(2,1)S(1)}, bf16[64,768]{1,0:T(8,128)(2,1)S(1)}, u32[]{:S(2)}, u32[]{:S(2)}) collective-permute-start(bf16[64,768]{1,0:T(8,128)(2,1)S(1)} %get-tuple-element.24), channel_id=1, source_target_pairs={{0,20},{4,16},{8,28},{12,24},{16,4},{20,0},{24,12},{28,8},{1,21},{... | collective-permute-start | bytes 294920 | tf_op jit(solution)/shard_map/ppermute | solution.py:312
  64.2 4.6 %collective-permute-start.9 = (bf16[64,768]{1,0:T(8,128)(2,1)S(1)}, bf16[64,768]{1,0:T(8,128)(2,1)S(1)}, u32[]{:S(2)}, u32[]{:S(2)}) collective-permute-start(bf16[64,768]{1,0:T(8,128)(2,1)S(1)} %get-tuple-element.25), channel_id=1, source_target_pairs={{0,12},{4,8},{8,4},{12,0},{16,28},{20,24},{24,20},{28,16},{1,13},{... | collective-permute-start | bytes 294920 | tf_op jit(solution)/shard_map/ppermute | solution.py:312
  64.4 4.4 %collective-permute-start.5 = (bf16[64,768]{1,0:T(8,128)(2,1)S(1)}, bf16[64,768]{1,0:T(8,128)(2,1)S(1)}, u32[]{:S(2)}, u32[]{:S(2)}) collective-permute-start(bf16[64,768]{1,0:T(8,128)(2,1)S(1)} %slice_bitcast_fusion), channel_id=1, source_target_pairs={{0,4},{4,0},{8,12},{12,8},{16,20},{20,16},{24,28},{28,24},{1,5},{5... | collective-permute-start | bytes 294920 | tf_op jit(solution)/shard_map/ppermute | solution.py:312

commit v5 on v4

--- a/solution.py
+++ b/solution.py
@@ -58,14 +58,15 @@
 
 
 def table_kernel(_, *out_refs, **sizes):
-    rows = out_refs[0].shape[0]
-    leave_space, enter_time, leave_time = orders(rows, **sizes)
+    some, rows = out_refs[0].shape[0], out_refs[1].shape[0]
+    leave_space, _, _ = orders(some, **sizes)
+    _, enter_time, leave_time = orders(rows, **sizes)
     me = lax.axis_index("tm")
-    row = lax.broadcasted_iota(jnp.int32, (rows, 1), 0)
-    place = lax.broadcasted_iota(jnp.int32, (rows, rows), 1)
-    wanted = [leave_space(row), enter_time(row), leave_time(row, me)]
-    for out_ref, source in zip(out_refs, wanted):
-        out_ref[...] = jnp.where(place == source, 1.0, 0.0).astype(BF16)
+    for out_ref, source in zip(out_refs, (leave_space, enter_time, lambda r: leave_time(r, me))):
+        shape = out_ref.shape
+        wanted = source(lax.broadcasted_iota(jnp.int32, (shape[0], 1), 0))
+        place = lax.broadcasted_iota(jnp.int32, shape, 1)
+        out_ref[...] = jnp.where(place == wanted, 1.0, 0.0).astype(BF16)
 
 
 def group_of(width):
@@ -124,37 +125,42 @@
         out_ref[j] = out.reshape(len(clip_refs), frames, toks, width)
 
 
-def space_kernel(*refs, distances, groups):
+def space_kernel(*refs, distances, late, groups, first):
     count = len(distances)
     clip_refs, refs = refs[:count], refs[count:]
-    *qkv_refs, w_ref, order_ref, out_ref, mix_ref, last_ref = refs
-    project(clip_refs[count - last_ref.shape[1] :], w_ref, last_ref)
-    qkv_refs = [*qkv_refs, last_ref]
-    frames, toks, width = clip_refs[0].shape[1:]
+    *refs, w_ref, order_ref, out_ref, mix_ref, last_ref = refs
+    qkv_refs, before = (refs[:-1], refs[-1]) if first else (refs, None)
+    project(clip_refs[count - late :], w_ref, last_ref)
+    frames, toks, width = last_ref.shape[2:]
     rows = count * toks
     share = toks // groups
-    block = frames * share
     masks = halves(rows)
     group = group_of(width)
 
     def part(j, f, cols):
-        return jnp.concatenate(
-            [ref[j, s, f, :, cols] for ref in qkv_refs for s in range(ref.shape[1])], axis=0
-        )
+        early = [ref[j, s, first + f, :, cols] for ref in qkv_refs for s in range(ref.shape[1])]
+        return jnp.concatenate(early + [last_ref[j, s, f, :, cols] for s in range(late)], axis=0)
 
     for f in range(frames):
         for p in range(0, width, group):
             cols = pl.ds(p, group)
             mixed = attend(part(0, f, cols), part(1, f, cols), part(2, f, cols), masks, None)
             mix_ref[pl.ds(f * rows, rows), cols] = mixed
-    clip = jnp.concatenate(
-        [own_or_whole(c, f) for f in range(frames) for c in clip_refs], axis=0
-    )
-    after = (dot(mix_ref[...], w_ref[3]) + clip.astype(F32)).astype(BF16)
-    after = dot(order_ref[...], after).astype(BF16).reshape(count, groups, block, width)
+    clip = [
+        own_or_whole(c, f if i >= count - late else first + f)
+        for f in range(frames)
+        for i, c in enumerate(clip_refs)
+    ]
+    after = dot(mix_ref[...], w_ref[3]) + jnp.concatenate(clip, axis=0).astype(F32)
+    after = dot(order_ref[...], after.astype(BF16)).astype(BF16)
+    after = after.reshape(count, groups, frames * share, width)
     me = lax.axis_index("space")
     for i, k in enumerate(distances):
-        out_ref[pl.ds((me ^ k) * groups, groups)] = after[i]
+        at = pl.ds((me ^ k) * groups, groups)
+        if before is None:
+            out_ref[at] = after[i]
+        else:
+            out_ref[at] = jnp.concatenate([before[at], after[i]], axis=1)
 
 
 def time_kernel(x_ref, w_ref, order_ref, *refs, toks, both, direct):
@@ -228,14 +234,6 @@
     )(*args)
 
 
-def exchange(pieces, axis, order, unit=1):
-    count = lax.axis_size(axis)
-    got = {0: pieces[0]}
-    for k in order:
-        got[k] = lax.ppermute(pieces[k], axis, [(i, i ^ (k * unit)) for i in range(count)])
-    return [got[k] for k in range(len(pieces))]
-
-
 def on_device(clip, w_spatial, w_temporal):
     frames, toks, width = clip.shape
     rows = frames * toks
@@ -248,15 +246,25 @@
 
     blocks = clip.reshape(space, *piece)
     me = lax.axis_index("space")
-    near = sorted(range(1, space), key=lambda k: (k == 1, k))
+    early = [0, 2, 1] if space > 3 else [0]
+    late = [k for k in range(space) if k not in early]
+    chunks = 2 if per % 2 == 0 and late else 1
+    step = per // chunks
     parts = {0: blocks}
     held = blocks
-    for k in near:
+    for k in early[1:] + late:
         parts[k] = lax.dynamic_index_in_dim(held, me ^ k, 0, keepdims=False)
         held = lax.optimization_barrier((blocks, parts[k]))[0]
-    parts = [parts[k] for k in range(space)]
-    parts = exchange(parts, "space", sorted(range(1, space), key=lambda k: (k == 1, k)))
-    groups = [[0], [2], [1], [*range(3, space)]] if space > 3 else [[*range(space)]]
+
+    def over_space(part, distance):
+        return lax.ppermute(part, "space", [(i, i ^ distance) for i in range(space)])
+
+    for k in early[1:]:
+        parts[k] = over_space(parts[k], k)
+    ends = [
+        [over_space(parts[k][c * step : (c + 1) * step], k) for k in late] for c in range(chunks)
+    ]
+    groups = [[k] for k in early]
     qkv = [
         call(
             project_kernel,
@@ -266,30 +274,37 @@
             w_spatial,
             flops=3 * cost * len(group) // space,
         )[0]
-        for group in groups[:-1]
+        for group in groups
     ]
     leave_space, enter_time, leave_time = call(
         functools.partial(
             table_kernel, count=space, groups=tm, share=share
         ),
         "orders",
-        [(rows, rows)] * 3,
-        qkv[0] if qkv else parts[0],
-    )
-    after = call(
-        functools.partial(space_kernel, distances=sum(groups, []), groups=tm),
-        "spatial",
-        [(space * tm, block, width)],
-        *[parts[k] for k in sum(groups, [])],
-        *qkv,
-        w_spatial,
-        leave_space,
-        scratch=[
-            pltpu.VMEM((rows, width), BF16),
-            pltpu.VMEM((3, len(groups[-1]), *piece), BF16),
-        ],
-        flops=2 * cost,
-    )[0]
+        [(rows // chunks, rows // chunks), (rows, rows), (rows, rows)],
+        qkv[0],
+    )
+    before = []
+    for c in range(chunks):
+        before = call(
+            functools.partial(
+                space_kernel, distances=early + late, late=len(late), groups=tm, first=c * step
+            ),
+            "spatial",
+            [(space * tm, (c + 1) * step * share, width)],
+            *[parts[k] for k in early],
+            *ends[c],
+            *qkv,
+            *before,
+            w_spatial,
+            leave_space,
+            scratch=[
+                pltpu.VMEM((rows // chunks, width), BF16),
+                pltpu.VMEM((3, len(late), step, toks, width), BF16),
+            ],
+            flops=2 * cost // chunks,
+        )
+    after = before[0]
     after = lax.all_to_all(after, ("space", "tm"), split_axis=0, concat_axis=0, tiled=True)
     both = [k for k in range(tm // 2) if k.bit_count() != 1]
     direct = [2 * k + s for s in range(2) for k in reversed(range(tm // 2)) if k not in both]

time: 70.4 us -> 69.9 us (level)
  waiting for transfers between devices: 12.4 us -> 6.58 us
  starting transfers between devices: 12.6 us -> 16.5 us
  Pallas kernels: 12 us -> 13.4 us
  local copies, waits for them, and re-layouts: 6.33 us -> 7.44 us
  blocking collectives: 26.6 us -> 25.5 us
    ppermute x3 -> x4, waiting for transfers between devices: 6.53 us -> 0.7 us  [over_space(): lax.ppermute(part, 'space', [(i, i ^ distance) for i in range(space)])]
    ppermute x3 -> x4, starting transfers between devices: 5.75 us -> 9.62 us  [over_space(): lax.ppermute(part, 'space', [(i, i ^ distance) for i in range(space)])]
    pallas_call x7 -> x8, Pallas kernels: 12 us -> 13.4 us  [call(): pl.pallas_call(kernel, out_shape=like, in_specs=[within] * len(args), out...]
    unnamed x12, local copies, waits for them, and re-layouts: 3.49 us -> 4.59 us
    all_to_all x1, blocking collectives: 26.6 us -> 25.5 us  [on_device(): lax.all_to_all(after, ('space', 'tm'), split_axis=0, concat_axis=0, tiled...]
    slice x0 -> x1, local copies, waits for them, and re-layouts: none -> 0.95 us  [on_device(): parts[k][c * step:(c + 1) * step]]
    squeeze x3 -> x2, local copies, waits for them, and re-layouts: 2.82 us -> 1.88 us  [on_device(): parts[k] = lax.dynamic_index_in_dim(held, me ^ k, 0, keepdims=False)]
  transfers between devices with their start and end apart: 10 -> 11, of which waited for: 5 -> 4; matrix products, arithmetic and copies ran while one was open for 3% -> 3% of each run, Pallas kernels for 4% -> 7%
where the time goes in v5:
time: 69.9 us; the launch traced here: 69.6 us
  blocking collectives  25.5 us (36%)
  starting transfers between devices  16.5 us (24%)
  Pallas kernels  13.4 us (19%)
  local copies, waits for them, and re-layouts  7.44 us (11%)
  waiting for transfers between devices  6.58 us (9%)
    all_to_all x1, blocking collectives, on_device(): lax.all_to_all(after, ('space', 'tm'), split_axis=0, concat_axis=0, tiled...  25.5 us
    pallas_call x8, Pallas kernels, call(): pl.pallas_call(kernel, out_shape=like, in_specs=[within] * len(args), out...  13.4 us
    ppermute x4, starting transfers between devices, over_space(): lax.ppermute(part, 'space', [(i, i ^ distance) for i in range(space)])  9.62 us
    ppermute x7, starting transfers between devices, over_tm(): return lax.ppermute(part, 'tm', [(i, i ^ distance) for i in range(tm)])  6.89 us
    ppermute x7, waiting for transfers between devices, over_tm(): return lax.ppermute(part, 'tm', [(i, i ^ distance) for i in range(tm)])  5.88 us
    unnamed x12, local copies, waits for them, and re-layouts  4.59 us
    squeeze x2, local copies, waits for them, and re-layouts, on_device(): parts[k] = lax.dynamic_index_in_dim(held, me ^ k, 0, keepdims=False)  1.88 us
  transfers between devices with their start and end apart: 11, of which 4 were waited for; matrix products, arithmetic and copies ran while one was open for 3% of the time, Pallas kernels for 7%

profile of v5, /device:TPU:0, one launch (start us, length us, event | category | flops | bytes accessed | tf_op | source)
XLA Modules:
  0.0 69.6 jit_solution(13265609610306157078)
XLA Ops:
  0.0 0.9 %dynamic-slice_bitcast_fusion.1 = bf16[4,32,768]{2,1,0:T(8,128)(2,1)S(1)} fusion(bf16[4,4,32,768]{3,2,1,0:T(8,128)(2,1)} %bitcast.14, s32[]{:T(128)S(6)} %select_n.10), kind=kLoop, calls=%fused_computation.1 | loop fusion | bytes 393220 | tf_op jit(solution)/shard_map/jit(dynamic_index_in_dim)/squeeze | solution.py:256
  0.9 4.1 %collective-permute-start = (bf16[4,32,768]{2,1,0:T(8,128)(2,1)S(1)}, bf16[4,32,768]{2,1,0:T(8,128)(2,1)S(1)}, u32[]{:S(2)}, u32[]{:S(2)}) collective-permute-start(bf16[4,32,768]{2,1,0:T(8,128)(2,1)S(1)} %dynamic-slice_bitcast_fusion.1), channel_id=1, source_target_pairs={{0,2},{1,3},{2,0},{3,1},{4,6},{5,7},{6,4},{7,5},{8,10},{9,11},{10,... | collective-permute-start | bytes 589832 | tf_op jit(solution)/shard_map/ppermute | solution.py:260
  5.0 0.9 %dynamic-slice_bitcast_fusion = bf16[4,32,768]{2,1,0:T(8,128)(2,1)S(1)} fusion(bf16[4,4,32,768]{3,2,1,0:T(8,128)(2,1)} %bitcast.15, s32[]{:T(128)S(6)} %select_n.11), kind=kLoop, calls=%fused_computation | loop fusion | bytes 393220 | tf_op jit(solution)/shard_map/jit(dynamic_index_in_dim)/squeeze | solution.py:256
  6.0 1.6 %collective-permute-start.1 = (bf16[4,32,768]{2,1,0:T(8,128)(2,1)S(1)}, bf16[4,32,768]{2,1,0:T(8,128)(2,1)S(1)}, u32[]{:S(2)}, u32[]{:S(2)}) collective-permute-start(bf16[4,32,768]{2,1,0:T(8,128)(2,1)S(1)} %dynamic-slice_bitcast_fusion), channel_id=1, source_target_pairs={{0,1},{1,0},{2,3},{3,2},{4,5},{5,4},{6,7},{7,6},{8,9},{9,8},{10,11... | collective-permute-start | bytes 589832 | tf_op jit(solution)/shard_map/ppermute | solution.py:260
  7.6 1.0 %dynamic-slice_bitcast_fusion.2 = (bf16[2,32,768]{2,1,0:T(8,128)(2,1)S(1)}, bf16[2,32,768]{2,1,0:T(8,128)(2,1)S(1)}) fusion(bf16[4,4,32,768]{3,2,1,0:T(8,128)(2,1)} %bitcast.16, s32[]{:T(128)S(6)} %select_n.12, s32[]{:T(128)S(6)} %add.13), kind=kLoop, calls=%fused_computation.3 | loop fusion | bytes 393224 | tf_op jit(solution)/shard_map/slice | solution.py:265
  8.6 0.1 collective-permute-start.3
  8.7 3.8 %collective-permute-start.2 = (bf16[2,32,768]{2,1,0:T(8,128)(2,1)S(1)}, bf16[2,32,768]{2,1,0:T(8,128)(2,1)S(1)}, u32[]{:S(2)}, u32[]{:S(2)}) collective-permute-start(bf16[2,32,768]{2,1,0:T(8,128)(2,1)S(1)} %get-tuple-element.28), channel_id=1, source_target_pairs={{0,3},{1,2},{2,1},{3,0},{4,7},{5,6},{6,5},{7,4},{8,11},{9,10},{10,... | collective-permute-start | bytes 294920 | tf_op jit(solution)/shard_map/ppermute | solution.py:260
  12.5 2.3 %copy-done = bf16[4,768,768]{2,1,0:T(8,128)(2,1)S(1)} copy-done((bf16[4,768,768]{2,1,0:T(8,128)(2,1)S(1)}, bf16[4,768,768]{2,1,0:T(8,128)(2,1)}, u32[]{:S(2)}) %copy-start) | copy-done | bytes 4718616
  14.8 1.1 %copy-done.2 = bf16[16,32,768]{2,1,0:T(8,128)(2,1)S(1)} copy-done((bf16[16,32,768]{2,1,0:T(8,128)(2,1)S(1)}, bf16[16,32,768]{2,1,0:T(8,128)(2,1)}, u32[]{:S(2)}) %copy-start.2) | copy-done | bytes 786456
  15.9 0.7 %project.3._.refs_4_ = bf16[3,1,4,32,768]{4,3,2,1,0:T(8,128)(2,1)S(1)} custom-call(bf16[4,4,32,768]{3,2,1,0:T(8,128)(2,1)S(1)} %bitcast.17, bf16[4,768,768]{2,1,0:T(8,128)(2,1)S(1)} %copy-done), custom_call_target="tpu_custom_call" | custom-call | flops 452984832 | bytes 6094848 | tf_op jit(solution)/shard_map/project/pallas_call | solution.py:224
  16.7 0.5 orders.1
  17.2 1.1 %copy-done.1 = bf16[4,768,768]{2,1,0:T(8,128)(2,1)S(1)} copy-done((bf16[4,768,768]{2,1,0:T(8,128)(2,1)S(1)}, bf16[4,768,768]{2,1,0:T(8,128)(2,1)}, u32[]{:S(2)}) %copy-start.1) | copy-done | bytes 4718616
  18.3 0.7 %project.4.refs_5_ = bf16[3,1,4,32,768]{4,3,2,1,0:T(8,128)(2,1)S(1)} custom-call(bf16[4,32,768]{2,1,0:T(8,128)(2,1)S(1)} %collective-permute-done.refs_0_.refs_1_, bf16[4,768,768]{2,1,0:T(8,128)(2,1)S(1)} %copy-done.1), custom_call_target="tpu_custom_call" | custom-call | flops 452984832 | bytes 5505024 | tf_op jit(solution)/shard_map/project/pallas_call | solution.py:224
  19.0 0.7 collective-permute-done.1.refs_0_.refs_2_
  19.7 0.7 %project.5.refs_6_ = bf16[3,1,4,32,768]{4,3,2,1,0:T(8,128)(2,1)S(1)} custom-call(bf16[4,32,768]{2,1,0:T(8,128)(2,1)S(1)} %collective-permute-done.1.refs_0_.refs_2_, bf16[4,768,768]{2,1,0:T(8,128)(2,1)S(1)} %copy-done.1), custom_call_target="tpu_custom_call" | custom-call | flops 452984832 | bytes 5505024 | tf_op jit(solution)/shard_map/project/pallas_call | solution.py:224
  20.4 0.0 slice-start
  20.4 2.3 %spatial.2.refs_7_ = bf16[32,8,768]{2,1,0:T(8,128)(2,1)S(1)} custom-call(bf16[4,4,32,768]{3,2,1,0:T(8,128)(2,1)S(1)} %bitcast.18, bf16[4,32,768]{2,1,0:T(8,128)(2,1)S(1)} %collective-permute-done.refs_0_.refs_1_, bf16[4,32,768]{2,1,0:T(8,128)(2,1)S(1)} %collective-permute-done.1.refs_0_.refs_2_, bf16[2,32,768]{2,1,0:T(8,128)(2,1)S(1)} %collective-permute-done.3.refs_3_, ...), custom_call_target="tpu_custom_call" | custom-call | flops 603979776 | bytes 8290304 | tf_op jit(solution)/shard_map/spatial/pallas_call | solution.py:224
  22.7 0.0 slice-start.1
  22.8 2.3 %spatial.3 = bf16[32,16,768]{2,1,0:T(8,128)(2,1)S(1)} custom-call(bf16[4,4,32,768]{3,2,1,0:T(8,128)(2,1)S(1)} %bitcast.19, bf16[4,32,768]{2,1,0:T(8,128)(2,1)S(1)} %collective-permute-done.refs_0_.refs_1_, bf16[4,32,768]{2,1,0:T(8,128)(2,1)S(1)} %collective-permute-done.1.refs_0_.refs_2_, bf16[2,32,768]{2,1,0:T(8,128)(2,1)S(1)} %collective-permute-done.2.refs_3_, ...), custom_call_target="tpu_custom_call" | custom-call | flops 603979776 | bytes 9076736 | tf_op jit(solution)/shard_map/spatial/pallas_call | solution.py:224
  25.1 25.5 %all_to_all.5 = bf16[32,16,768]{2,1,0:T(8,128)(2,1)S(1)} all-to-all(bf16[32,16,768]{2,1,0:T(8,128)(2,1)S(1)} %spatial.3), channel_id=1, replica_groups=mesh['tm'=8,'space'=4] {'space','tm'}, dimensions={0} | all-to-all | bytes 1572864 | tf_op jit(solution)/shard_map/all_to_all | solution.py:308
  50.6 4.9 %temporal.1 = (bf16[2,64,768]{2,1,0:T(8,128)(2,1)S(1)}, bf16[2,64,768]{2,1,0:T(8,128)(2,1)S(1)}, bf16[64,768]{1,0:T(8,128)(2,1)S(1)}, bf16[64,768]{1,0:T(8,128)(...) custom-call(bf16[4,8,16,768]{3,2,1,0:T(8,128)(2,1)S(1)} %bitcast.20, ...), custom_call_target="tpu_custom_call" | custom-call | flops 3019898880 | bytes 6815744 | tf_op jit(solution)/shard_map/temporal/pallas_call | solution.py:224
  55.5 2.5 %collective-permute-start.4 = (bf16[2,64,768]{2,1,0:T(8,128)(2,1)S(1)}, bf16[2,64,768]{2,1,0:T(8,128)(2,1)S(1)}, u32[]{:S(2)}, u32[]{:S(2)}) collective-permute-start(bf16[2,64,768]{2,1,0:T(8,128)(2,1)S(1)} %get-tuple-element.21), channel_id=1, source_target_pairs={{0,24},{4,28},{8,16},{12,20},{16,8},{20,12},{24,0},{28,4},{1,25},{... | collective-permute-start | bytes 589832 | tf_op jit(solution)/shard_map/ppermute | solution.py:327
  58.0 0.1 collective-permute-start.5
  58.0 0.6 collective-permute-start.7
  58.6 0.6 collective-permute-start.8
  59.2 1.0 %collective-permute-start.9 = (bf16[64,768]{1,0:T(8,128)(2,1)S(1)}, bf16[64,768]{1,0:T(8,128)(2,1)S(1)}, u32[]{:S(2)}, u32[]{:S(2)}) collective-permute-start(bf16[64,768]{1,0:T(8,128)(2,1)S(1)} %get-tuple-element.24), channel_id=1, source_target_pairs={{0,20},{4,16},{8,28},{12,24},{16,4},{20,0},{24,12},{28,8},{1,21},{... | collective-permute-start | bytes 294920 | tf_op jit(solution)/shard_map/ppermute | solution.py:327
  60.2 3.5 %collective-permute-done.4.refs_1_ = bf16[2,64,768]{2,1,0:T(8,128)(2,1)S(1)} collective-permute-done((bf16[2,64,768]{2,1,0:T(8,128)(2,1)S(1)}, bf16[2,64,768]{2,1,0:T(8,128)(2,1)S(1)}, u32[]{:S(2)}, u32[]{:S(2)}) %collective-permute-start.4) | collective-permute-done | bytes 196640 | tf_op jit(solution)/shard_map/ppermute | solution.py:327
  63.7 0.2 collective-permute-start.10
  63.9 2.0 %collective-permute-start.6 = (bf16[64,768]{1,0:T(8,128)(2,1)S(1)}, bf16[64,768]{1,0:T(8,128)(2,1)S(1)}, u32[]{:S(2)}, u32[]{:S(2)}) collective-permute-start(bf16[64,768]{1,0:T(8,128)(2,1)S(1)} %slice_bitcast_fusion), channel_id=1, source_target_pairs={{0,4},{4,0},{8,12},{12,8},{16,20},{20,16},{24,28},{28,24},{1,5},{5... | collective-permute-start | bytes 294920 | tf_op jit(solution)/shard_map/ppermute | solution.py:327
  65.9 1.3 %collective-permute-done.9.refs_6_ = bf16[64,768]{1,0:T(8,128)(2,1)S(1)} collective-permute-done((bf16[64,768]{1,0:T(8,128)(2,1)S(1)}, bf16[64,768]{1,0:T(8,128)(2,1)S(1)}, u32[]{:S(2)}, u32[]{:S(2)}) %collective-permute-start.9) | collective-permute-done | bytes 98336 | tf_op jit(solution)/shard_map/ppermute | solution.py:327
  67.2 1.1 %collective-permute-done.10.refs_7_ = bf16[64,768]{1,0:T(8,128)(2,1)S(1)} collective-permute-done((bf16[64,768]{1,0:T(8,128)(2,1)S(1)}, bf16[64,768]{1,0:T(8,128)(2,1)S(1)}, u32[]{:S(2)}, u32[]{:S(2)}) %collective-permute-start.10) | collective-permute-done | bytes 98336 | tf_op jit(solution)/shard_map/ppermute | solution.py:327
  68.3 1.3 %place.1 = bf16[16,32,768]{2,1,0:T(8,128)(2,1)} custom-call(bf16[2,64,768]{2,1,0:T(8,128)(2,1)S(1)} %get-tuple-element.20.refs_0_, bf16[2,64,768]{2,1,0:T(8,128)(2,1)S(1)} %collective-permute-done.4.refs_1_, bf16[64,768]{1,0:T(8,128)(2,1)S(1)} %collective-permute-done.5.refs_2_, bf16[64,768]{1,0:T(8,128)(2,1)S(1)} %collective-permute-done.6.refs_3_, ...), custom_call_target="tpu_custom_call" | custom-call | bytes 2293760 | tf_op jit(solution)/shard_map/place/pallas_call | solution.py:224
  (17 shorter events, 0.0 us)
Async XLA Ops:
  0.9 16.2 %collective-permute-start = (bf16[4,32,768]{2,1,0:T(8,128)(2,1)S(1)}, bf16[4,32,768]{2,1,0:T(8,128)(2,1)S(1)}, u32[]{:S(2)}, u32[]{:S(2)}) collective-permute-start(bf16[4,32,768]{2,1,0:T(8,128)(2,1)S(1)} %dynamic-slice_bitcast_fusion.1), channel_id=1, source_target_pairs={{0,2},{1,3},{2,0},{3,1},{4,6},{5,7},{6,4},{7,5},{8,10},{9,11},{10,... | collective-permute-start | bytes 589832 | tf_op jit(solution)/shard_map/ppermute | solution.py:260
  6.0 13.7 %collective-permute-start.1 = (bf16[4,32,768]{2,1,0:T(8,128)(2,1)S(1)}, bf16[4,32,768]{2,1,0:T(8,128)(2,1)S(1)}, u32[]{:S(2)}, u32[]{:S(2)}) collective-permute-start(bf16[4,32,768]{2,1,0:T(8,128)(2,1)S(1)} %dynamic-slice_bitcast_fusion), channel_id=1, source_target_pairs={{0,1},{1,0},{2,3},{3,2},{4,5},{5,4},{6,7},{7,6},{8,9},{9,8},{10,11... | collective-permute-start | bytes 589832 | tf_op jit(solution)/shard_map/ppermute | solution.py:260
  8.6 11.8 %collective-permute-start.3 = (bf16[2,32,768]{2,1,0:T(8,128)(2,1)S(1)}, bf16[2,32,768]{2,1,0:T(8,128)(2,1)S(1)}, u32[]{:S(2)}, u32[]{:S(2)}) collective-permute-start(bf16[2,32,768]{2,1,0:T(8,128)(2,1)S(1)} %get-tuple-element.27), channel_id=1, source_target_pairs={{0,3},{1,2},{2,1},{3,0},{4,7},{5,6},{6,5},{7,4},{8,11},{9,10},{10,... | collective-permute-start | bytes 294920 | tf_op jit(solution)/shard_map/ppermute | solution.py:260
  8.7 14.1 %collective-permute-start.2 = (bf16[2,32,768]{2,1,0:T(8,128)(2,1)S(1)}, bf16[2,32,768]{2,1,0:T(8,128)(2,1)S(1)}, u32[]{:S(2)}, u32[]{:S(2)}) collective-permute-start(bf16[2,32,768]{2,1,0:T(8,128)(2,1)S(1)} %get-tuple-element.28), channel_id=1, source_target_pairs={{0,3},{1,2},{2,1},{3,0},{4,7},{5,6},{6,5},{7,4},{8,11},{9,10},{10,... | collective-permute-start | bytes 294920 | tf_op jit(solution)/shard_map/ppermute | solution.py:260
  12.5 2.3 %copy-start = (bf16[4,768,768]{2,1,0:T(8,128)(2,1)S(1)}, bf16[4,768,768]{2,1,0:T(8,128)(2,1)}, u32[]{:S(2)}) copy-start(bf16[4,768,768]{2,1,0:T(8,128)(2,1)} %refs_8_.1) | copy-start | bytes 14155780
  14.8 1.1 %copy-start.2 = (bf16[16,32,768]{2,1,0:T(8,128)(2,1)S(1)}, bf16[16,32,768]{2,1,0:T(8,128)(2,1)}, u32[]{:S(2)}) copy-start(bf16[16,32,768]{2,1,0:T(8,128)(2,1)} %param.3) | copy-start | bytes 2359300
  15.9 2.3 %copy-start.1 = (bf16[4,768,768]{2,1,0:T(8,128)(2,1)S(1)}, bf16[4,768,768]{2,1,0:T(8,128)(2,1)}, u32[]{:S(2)}) copy-start(bf16[4,768,768]{2,1,0:T(8,128)(2,1)} %refs_8_.1) | copy-start | bytes 14155780
  17.2 3.2 %copy-start.3 = (bf16[16,32,768]{2,1,0:T(8,128)(2,1)S(1)}, bf16[16,32,768]{2,1,0:T(8,128)(2,1)}, u32[]{:S(2)}) copy-start(bf16[16,32,768]{2,1,0:T(8,128)(2,1)} %param.3) | copy-start | bytes 2359300
  20.4 30.2 %slice-start = ((s8[4718592]{0:T(1024)(128)(4,1)}), s8[4194304]{0:T(1024)(128)(4,1)S(1)}, s32[]{:S(2)}) async-start(s8[4718592]{0:T(1024)(128)(4,1)} %bitcast.21), calls=%async_computation.1 | async-start | bytes 8388608
  22.7 27.9 %slice-start.1 = ((s8[4718592]{0:T(1024)(128)(4,1)}), s8[524288]{0:T(1024)(128)(4,1)S(1)}, s32[]{:S(2)}) async-start(s8[4718592]{0:T(1024)(128)(4,1)} %bitcast.21), calls=%async_computation.2 | async-start | bytes 1048576
  55.5 8.2 %collective-permute-start.4 = (bf16[2,64,768]{2,1,0:T(8,128)(2,1)S(1)}, bf16[2,64,768]{2,1,0:T(8,128)(2,1)S(1)}, u32[]{:S(2)}, u32[]{:S(2)}) collective-permute-start(bf16[2,64,768]{2,1,0:T(8,128)(2,1)S(1)} %get-tuple-element.21), channel_id=1, source_target_pairs={{0,24},{4,28},{8,16},{12,20},{16,8},{20,12},{24,0},{28,4},{1,25},{... | collective-permute-start | bytes 589832 | tf_op jit(solution)/shard_map/ppermute | solution.py:327
  58.0 5.9 %collective-permute-start.5 = (bf16[64,768]{1,0:T(8,128)(2,1)S(1)}, bf16[64,768]{1,0:T(8,128)(2,1)S(1)}, u32[]{:S(2)}, u32[]{:S(2)}) collective-permute-start(bf16[64,768]{1,0:T(8,128)(2,1)S(1)} %slice_bitcast_fusion.1), channel_id=1, source_target_pairs={{0,4},{4,0},{8,12},{12,8},{16,20},{20,16},{24,28},{28,24},{1,5},{5... | collective-permute-start | bytes 294920 | tf_op jit(solution)/shard_map/ppermute | solution.py:327
  58.0 7.9 %collective-permute-start.7 = (bf16[64,768]{1,0:T(8,128)(2,1)S(1)}, bf16[64,768]{1,0:T(8,128)(2,1)S(1)}, u32[]{:S(2)}, u32[]{:S(2)}) collective-permute-start(bf16[64,768]{1,0:T(8,128)(2,1)S(1)} %get-tuple-element.22), channel_id=1, source_target_pairs={{0,16},{4,20},{8,24},{12,28},{16,0},{20,4},{24,8},{28,12},{1,17},{... | collective-permute-start | bytes 294920 | tf_op jit(solution)/shard_map/ppermute | solution.py:327
  58.6 7.3 %collective-permute-start.8 = (bf16[64,768]{1,0:T(8,128)(2,1)S(1)}, bf16[64,768]{1,0:T(8,128)(2,1)S(1)}, u32[]{:S(2)}, u32[]{:S(2)}) collective-permute-start(bf16[64,768]{1,0:T(8,128)(2,1)S(1)} %get-tuple-element.23), channel_id=1, source_target_pairs={{0,8},{4,12},{8,0},{12,4},{16,24},{20,28},{24,16},{28,20},{1,9},{5... | collective-permute-start | bytes 294920 | tf_op jit(solution)/shard_map/ppermute | solution.py:327
  59.2 8.0 %collective-permute-start.9 = (bf16[64,768]{1,0:T(8,128)(2,1)S(1)}, bf16[64,768]{1,0:T(8,128)(2,1)S(1)}, u32[]{:S(2)}, u32[]{:S(2)}) collective-permute-start(bf16[64,768]{1,0:T(8,128)(2,1)S(1)} %get-tuple-element.24), channel_id=1, source_target_pairs={{0,20},{4,16},{8,28},{12,24},{16,4},{20,0},{24,12},{28,8},{1,21},{... | collective-permute-start | bytes 294920 | tf_op jit(solution)/shard_map/ppermute | solution.py:327
  63.7 4.6 %collective-permute-start.10 = (bf16[64,768]{1,0:T(8,128)(2,1)S(1)}, bf16[64,768]{1,0:T(8,128)(2,1)S(1)}, u32[]{:S(2)}, u32[]{:S(2)}) collective-permute-start(bf16[64,768]{1,0:T(8,128)(2,1)S(1)} %get-tuple-element.25), channel_id=1, source_target_pairs={{0,12},{4,8},{8,4},{12,0},{16,28},{20,24},{24,20},{28,16},{1,13},{... | collective-permute-start | bytes 294920 | tf_op jit(solution)/shard_map/ppermute | solution.py:327
  63.9 4.4 %collective-permute-start.6 = (bf16[64,768]{1,0:T(8,128)(2,1)S(1)}, bf16[64,768]{1,0:T(8,128)(2,1)S(1)}, u32[]{:S(2)}, u32[]{:S(2)}) collective-permute-start(bf16[64,768]{1,0:T(8,128)(2,1)S(1)} %slice_bitcast_fusion), channel_id=1, source_target_pairs={{0,4},{4,0},{8,12},{12,8},{16,20},{20,16},{24,28},{28,24},{1,5},{5... | collective-permute-start | bytes 294920 | tf_op jit(solution)/shard_map/ppermute | solution.py:327

commit v6 on v5

--- a/solution.py
+++ b/solution.py
@@ -202,6 +202,7 @@
     frames, toks, width = out_ref.shape
     parts = {2 * k: in_refs[i].at[0] for i, k in enumerate(both)}
     parts |= {2 * k + 1: in_refs[len(both) + i] for i, k in enumerate(both)}
+    parts[1] = parts[1].at[1 - lax.axis_index("tm") % 2]
     parts |= {k: in_refs[2 * len(both) + i] for i, k in enumerate(direct)}
     rows = jnp.concatenate([parts[k][...] for k in range(len(parts))], axis=0)
     steps = sems.shape[0]
@@ -327,7 +328,9 @@
         return lax.ppermute(part, "tm", [(i, i ^ distance) for i in range(tm)])
 
     whole = [over_tm(part, 2 * k) if k else part for k, part in zip(both, result)]
-    beside = [over_tm(part[1], 1) for part in whole]
+    pairs = [[i, i + 1] for i in range(0, tm, 2)]
+    beside = [lax.all_gather(whole[0][1], "tm", axis_index_groups=pairs)]
+    beside += [over_tm(part[1], 1) for part in whole[1:]]
     near = [over_tm(part, k) for k, part in zip(direct, result[len(both) :])]
     steps = 4 if frames % 4 == 0 else 1
     return call(

time: 69.9 us -> 68.8 us (0.984)
  waiting for transfers between devices: 6.58 us -> 3.95 us
  blocking collectives: 25.5 us -> 27.6 us
    ppermute x7 -> x6, waiting for transfers between devices: 5.88 us -> 3.25 us  [over_tm(): return lax.ppermute(part, 'tm', [(i, i ^ distance) for i in range(tm)])]
    all_gather x0 -> x1, blocking collectives: none -> 2.07 us  [on_device(): beside = [lax.all_gather(whole[0][1], 'tm', axis_index_groups=pairs)]]
    ppermute x7 -> x6, starting transfers between devices: 6.89 us -> 6.3 us  [over_tm(): return lax.ppermute(part, 'tm', [(i, i ^ distance) for i in range(tm)])]
  transfers between devices with their start and end apart: 11 -> 10, of which waited for: 4 -> 3; matrix products, arithmetic and copies ran while one was open for 3% -> 3% of each run, Pallas kernels for 7% -> 7%
where the time goes in v6:
time: 68.8 us; the launch traced here: 68.5 us
  blocking collectives  27.6 us (40%)
  starting transfers between devices  15.9 us (23%)
  Pallas kernels  13.4 us (19%)
  local copies, waits for them, and re-layouts  7.44 us (11%)
  waiting for transfers between devices  3.95 us (6%)
    all_to_all x1, blocking collectives, on_device(): lax.all_to_all(after, ('space', 'tm'), split_axis=0, concat_axis=0, tiled...  25.5 us
    pallas_call x8, Pallas kernels, call(): pl.pallas_call(kernel, out_shape=like, in_specs=[within] * len(args), out...  13.4 us
    ppermute x4, starting transfers between devices, over_space(): lax.ppermute(part, 'space', [(i, i ^ distance) for i in range(space)])  9.62 us
    ppermute x6, starting transfers between devices, over_tm(): return lax.ppermute(part, 'tm', [(i, i ^ distance) for i in range(tm)])  6.3 us
    unnamed x12, local copies, waits for them, and re-layouts  4.59 us
    ppermute x6, waiting for transfers between devices, over_tm(): return lax.ppermute(part, 'tm', [(i, i ^ distance) for i in range(tm)])  3.25 us
    all_gather x1, blocking collectives, on_device(): beside = [lax.all_gather(whole[0][1], 'tm', axis_index_groups=pairs)]  2.07 us
    squeeze x2, local copies, waits for them, and re-layouts, on_device(): parts[k] = lax.dynamic_index_in_dim(held, me ^ k, 0, keepdims=False)  1.88 us
  transfers between devices with their start and end apart: 10, of which 3 were waited for; matrix products, arithmetic and copies ran while one was open for 3% of the time, Pallas kernels for 7%

profile of v6, /device:TPU:0, one launch (start us, length us, event | category | flops | bytes accessed | tf_op | source)
XLA Modules:
  0.0 68.5 jit_solution(5742426837144740757)
XLA Ops:
  0.0 0.9 %dynamic-slice_bitcast_fusion.1 = bf16[4,32,768]{2,1,0:T(8,128)(2,1)S(1)} fusion(bf16[4,4,32,768]{3,2,1,0:T(8,128)(2,1)} %bitcast.12, s32[]{:T(128)S(6)} %select_n.10), kind=kLoop, calls=%fused_computation.1 | loop fusion | bytes 393220 | tf_op jit(solution)/shard_map/jit(dynamic_index_in_dim)/squeeze | solution.py:257
  0.9 4.1 %collective-permute-start = (bf16[4,32,768]{2,1,0:T(8,128)(2,1)S(1)}, bf16[4,32,768]{2,1,0:T(8,128)(2,1)S(1)}, u32[]{:S(2)}, u32[]{:S(2)}) collective-permute-start(bf16[4,32,768]{2,1,0:T(8,128)(2,1)S(1)} %dynamic-slice_bitcast_fusion.1), channel_id=1, source_target_pairs={{0,2},{1,3},{2,0},{3,1},{4,6},{5,7},{6,4},{7,5},{8,10},{9,11},{10,... | collective-permute-start | bytes 589832 | tf_op jit(solution)/shard_map/ppermute | solution.py:261
  5.0 0.9 %dynamic-slice_bitcast_fusion = bf16[4,32,768]{2,1,0:T(8,128)(2,1)S(1)} fusion(bf16[4,4,32,768]{3,2,1,0:T(8,128)(2,1)} %bitcast.13, s32[]{:T(128)S(6)} %select_n.11), kind=kLoop, calls=%fused_computation | loop fusion | bytes 393220 | tf_op jit(solution)/shard_map/jit(dynamic_index_in_dim)/squeeze | solution.py:257
  6.0 1.6 %collective-permute-start.1 = (bf16[4,32,768]{2,1,0:T(8,128)(2,1)S(1)}, bf16[4,32,768]{2,1,0:T(8,128)(2,1)S(1)}, u32[]{:S(2)}, u32[]{:S(2)}) collective-permute-start(bf16[4,32,768]{2,1,0:T(8,128)(2,1)S(1)} %dynamic-slice_bitcast_fusion), channel_id=1, source_target_pairs={{0,1},{1,0},{2,3},{3,2},{4,5},{5,4},{6,7},{7,6},{8,9},{9,8},{10,11... | collective-permute-start | bytes 589832 | tf_op jit(solution)/shard_map/ppermute | solution.py:261
  7.6 1.0 %dynamic-slice_bitcast_fusion.2 = (bf16[2,32,768]{2,1,0:T(8,128)(2,1)S(1)}, bf16[2,32,768]{2,1,0:T(8,128)(2,1)S(1)}) fusion(bf16[4,4,32,768]{3,2,1,0:T(8,128)(2,1)} %bitcast.14, s32[]{:T(128)S(6)} %select_n.12, s32[]{:T(128)S(6)} %add.13), kind=kLoop, calls=%fused_computation.3 | loop fusion | bytes 393224 | tf_op jit(solution)/shard_map/slice | solution.py:266
  8.6 0.1 collective-permute-start.3
  8.7 3.8 %collective-permute-start.2 = (bf16[2,32,768]{2,1,0:T(8,128)(2,1)S(1)}, bf16[2,32,768]{2,1,0:T(8,128)(2,1)S(1)}, u32[]{:S(2)}, u32[]{:S(2)}) collective-permute-start(bf16[2,32,768]{2,1,0:T(8,128)(2,1)S(1)} %get-tuple-element.28), channel_id=1, source_target_pairs={{0,3},{1,2},{2,1},{3,0},{4,7},{5,6},{6,5},{7,4},{8,11},{9,10},{10,... | collective-permute-start | bytes 294920 | tf_op jit(solution)/shard_map/ppermute | solution.py:261
  12.5 2.3 %copy-done = bf16[4,768,768]{2,1,0:T(8,128)(2,1)S(1)} copy-done((bf16[4,768,768]{2,1,0:T(8,128)(2,1)S(1)}, bf16[4,768,768]{2,1,0:T(8,128)(2,1)}, u32[]{:S(2)}) %copy-start) | copy-done | bytes 4718616
  14.8 1.1 %copy-done.2 = bf16[16,32,768]{2,1,0:T(8,128)(2,1)S(1)} copy-done((bf16[16,32,768]{2,1,0:T(8,128)(2,1)S(1)}, bf16[16,32,768]{2,1,0:T(8,128)(2,1)}, u32[]{:S(2)}) %copy-start.2) | copy-done | bytes 786456
  15.9 0.7 %project.3._.refs_4_ = bf16[3,1,4,32,768]{4,3,2,1,0:T(8,128)(2,1)S(1)} custom-call(bf16[4,4,32,768]{3,2,1,0:T(8,128)(2,1)S(1)} %bitcast.15, bf16[4,768,768]{2,1,0:T(8,128)(2,1)S(1)} %copy-done), custom_call_target="tpu_custom_call" | custom-call | flops 452984832 | bytes 6094848 | tf_op jit(solution)/shard_map/project/pallas_call | solution.py:225
  16.7 0.5 orders.1
  17.2 0.0 copy-start.3
  17.2 1.1 %copy-done.1 = bf16[4,768,768]{2,1,0:T(8,128)(2,1)S(1)} copy-done((bf16[4,768,768]{2,1,0:T(8,128)(2,1)S(1)}, bf16[4,768,768]{2,1,0:T(8,128)(2,1)}, u32[]{:S(2)}) %copy-start.1) | copy-done | bytes 4718616
  18.3 0.7 %project.4.refs_5_ = bf16[3,1,4,32,768]{4,3,2,1,0:T(8,128)(2,1)S(1)} custom-call(bf16[4,32,768]{2,1,0:T(8,128)(2,1)S(1)} %collective-permute-done.refs_0_.refs_1_, bf16[4,768,768]{2,1,0:T(8,128)(2,1)S(1)} %copy-done.1), custom_call_target="tpu_custom_call" | custom-call | flops 452984832 | bytes 5505024 | tf_op jit(solution)/shard_map/project/pallas_call | solution.py:225
  19.0 0.7 %collective-permute-done.1.refs_0_.refs_2_ = bf16[4,32,768]{2,1,0:T(8,128)(2,1)S(1)} collective-permute-done((bf16[4,32,768]{2,1,0:T(8,128)(2,1)S(1)}, bf16[4,32,768]{2,1,0:T(8,128)(2,1)S(1)}, u32[]{:S(2)}, u32[]{:S(2)}) %collective-permute-start.1) | collective-permute-done | bytes 196640 | tf_op jit(solution)/shard_map/ppermute | solution.py:261
  19.7 0.7 %project.5.refs_6_ = bf16[3,1,4,32,768]{4,3,2,1,0:T(8,128)(2,1)S(1)} custom-call(bf16[4,32,768]{2,1,0:T(8,128)(2,1)S(1)} %collective-permute-done.1.refs_0_.refs_2_, bf16[4,768,768]{2,1,0:T(8,128)(2,1)S(1)} %copy-done.1), custom_call_target="tpu_custom_call" | custom-call | flops 452984832 | bytes 5505024 | tf_op jit(solution)/shard_map/project/pallas_call | solution.py:225
  20.4 0.0 slice-start
  20.4 2.3 %spatial.2.refs_7_ = bf16[32,8,768]{2,1,0:T(8,128)(2,1)S(1)} custom-call(bf16[4,4,32,768]{3,2,1,0:T(8,128)(2,1)S(1)} %bitcast.16, bf16[4,32,768]{2,1,0:T(8,128)(2,1)S(1)} %collective-permute-done.refs_0_.refs_1_, bf16[4,32,768]{2,1,0:T(8,128)(2,1)S(1)} %collective-permute-done.1.refs_0_.refs_2_, bf16[2,32,768]{2,1,0:T(8,128)(2,1)S(1)} %collective-permute-done.3.refs_3_, ...), custom_call_target="tpu_custom_call" | custom-call | flops 603979776 | bytes 8290304 | tf_op jit(solution)/shard_map/spatial/pallas_call | solution.py:225
  22.7 0.0 slice-start.1
  22.8 2.3 %spatial.3 = bf16[32,16,768]{2,1,0:T(8,128)(2,1)S(1)} custom-call(bf16[4,4,32,768]{3,2,1,0:T(8,128)(2,1)S(1)} %bitcast.17, bf16[4,32,768]{2,1,0:T(8,128)(2,1)S(1)} %collective-permute-done.refs_0_.refs_1_, bf16[4,32,768]{2,1,0:T(8,128)(2,1)S(1)} %collective-permute-done.1.refs_0_.refs_2_, bf16[2,32,768]{2,1,0:T(8,128)(2,1)S(1)} %collective-permute-done.2.refs_3_, ...), custom_call_target="tpu_custom_call" | custom-call | flops 603979776 | bytes 9076736 | tf_op jit(solution)/shard_map/spatial/pallas_call | solution.py:225
  25.1 25.5 %all_to_all.5 = bf16[32,16,768]{2,1,0:T(8,128)(2,1)S(1)} all-to-all(bf16[32,16,768]{2,1,0:T(8,128)(2,1)S(1)} %spatial.3), channel_id=1, replica_groups=mesh['tm'=8,'space'=4] {'space','tm'}, dimensions={0} | all-to-all | bytes 1572864 | tf_op jit(solution)/shard_map/all_to_all | solution.py:309
  50.6 4.9 %temporal.1 = (bf16[2,64,768]{2,1,0:T(8,128)(2,1)S(1)}, bf16[2,64,768]{2,1,0:T(8,128)(2,1)S(1)}, bf16[64,768]{1,0:T(8,128)(2,1)S(1)}, bf16[64,768]{1,0:T(8,128)(...) custom-call(bf16[4,8,16,768]{3,2,1,0:T(8,128)(2,1)S(1)} %bitcast.18, ...), custom_call_target="tpu_custom_call" | custom-call | flops 3019898880 | bytes 6815744 | tf_op jit(solution)/shard_map/temporal/pallas_call | solution.py:225
  55.5 2.5 %collective-permute-start.4 = (bf16[2,64,768]{2,1,0:T(8,128)(2,1)S(1)}, bf16[2,64,768]{2,1,0:T(8,128)(2,1)S(1)}, u32[]{:S(2)}, u32[]{:S(2)}) collective-permute-start(bf16[2,64,768]{2,1,0:T(8,128)(2,1)S(1)} %get-tuple-element.21), channel_id=1, source_target_pairs={{0,24},{4,28},{8,16},{12,20},{16,8},{20,12},{24,0},{28,4},{1,25},{... | collective-permute-start | bytes 589832 | tf_op jit(solution)/shard_map/ppermute | solution.py:328
  58.0 0.5 collective-permute-start.6
  58.5 0.6 collective-permute-start.7
  59.1 0.1 collective-permute-start.8
  59.1 2.6 %collective-permute-start.9 = (bf16[64,768]{1,0:T(8,128)(2,1)S(1)}, bf16[64,768]{1,0:T(8,128)(2,1)S(1)}, u32[]{:S(2)}, u32[]{:S(2)}) collective-permute-start(bf16[64,768]{1,0:T(8,128)(2,1)S(1)} %get-tuple-element.25), channel_id=1, source_target_pairs={{0,12},{4,8},{8,4},{12,0},{16,28},{20,24},{24,20},{28,16},{1,13},{... | collective-permute-start | bytes 294920 | tf_op jit(solution)/shard_map/ppermute | solution.py:328
  61.7 2.6 %collective-permute-done.4.refs_1_ = bf16[2,64,768]{2,1,0:T(8,128)(2,1)S(1)} collective-permute-done((bf16[2,64,768]{2,1,0:T(8,128)(2,1)S(1)}, bf16[2,64,768]{2,1,0:T(8,128)(2,1)S(1)}, u32[]{:S(2)}, u32[]{:S(2)}) %collective-permute-start.4) | collective-permute-done | bytes 196640 | tf_op jit(solution)/shard_map/ppermute | solution.py:328
  64.3 0.1 collective-permute-start.5
  64.4 2.1 %all_gather.3.refs_2_ = bf16[2,64,768]{2,1,0:T(8,128)(2,1)S(1)} all-gather(bf16[1,64,768]{2,1,0:T(8,128)(2,1)S(1)} %slice.22), channel_id=1, replica_groups={{0,4},{8,12},{16,20},{24,28},{1,5},{9,13},{17,21},{25,29},{2,6},{10,14}..., dimensions={0}, use_global_device_ids=true | all-gather | bytes 294912 | tf_op jit(solution)/shard_map/all_gather | solution.py:332
  66.5 0.7 collective-permute-done.8.refs_6_
  67.2 1.3 %place.1 = bf16[16,32,768]{2,1,0:T(8,128)(2,1)} custom-call(bf16[2,64,768]{2,1,0:T(8,128)(2,1)S(1)} %get-tuple-element.20.refs_0_, bf16[2,64,768]{2,1,0:T(8,128)(2,1)S(1)} %collective-permute-done.4.refs_1_, bf16[2,64,768]{2,1,0:T(8,128)(2,1)S(1)} %all_gather.3.refs_2_, bf16[64,768]{1,0:T(8,128)(2,1)S(1)} %collective-permute-done.5.refs_3_, ...), custom_call_target="tpu_custom_call" | custom-call | bytes 2392064 | tf_op jit(solution)/shard_map/place/pallas_call | solution.py:225
  (16 shorter events, 0.0 us)
Async XLA Ops:
  0.9 16.2 %collective-permute-start = (bf16[4,32,768]{2,1,0:T(8,128)(2,1)S(1)}, bf16[4,32,768]{2,1,0:T(8,128)(2,1)S(1)}, u32[]{:S(2)}, u32[]{:S(2)}) collective-permute-start(bf16[4,32,768]{2,1,0:T(8,128)(2,1)S(1)} %dynamic-slice_bitcast_fusion.1), channel_id=1, source_target_pairs={{0,2},{1,3},{2,0},{3,1},{4,6},{5,7},{6,4},{7,5},{8,10},{9,11},{10,... | collective-permute-start | bytes 589832 | tf_op jit(solution)/shard_map/ppermute | solution.py:261
  6.0 13.7 %collective-permute-start.1 = (bf16[4,32,768]{2,1,0:T(8,128)(2,1)S(1)}, bf16[4,32,768]{2,1,0:T(8,128)(2,1)S(1)}, u32[]{:S(2)}, u32[]{:S(2)}) collective-permute-start(bf16[4,32,768]{2,1,0:T(8,128)(2,1)S(1)} %dynamic-slice_bitcast_fusion), channel_id=1, source_target_pairs={{0,1},{1,0},{2,3},{3,2},{4,5},{5,4},{6,7},{7,6},{8,9},{9,8},{10,11... | collective-permute-start | bytes 589832 | tf_op jit(solution)/shard_map/ppermute | solution.py:261
  8.6 11.8 %collective-permute-start.3 = (bf16[2,32,768]{2,1,0:T(8,128)(2,1)S(1)}, bf16[2,32,768]{2,1,0:T(8,128)(2,1)S(1)}, u32[]{:S(2)}, u32[]{:S(2)}) collective-permute-start(bf16[2,32,768]{2,1,0:T(8,128)(2,1)S(1)} %get-tuple-element.27), channel_id=1, source_target_pairs={{0,3},{1,2},{2,1},{3,0},{4,7},{5,6},{6,5},{7,4},{8,11},{9,10},{10,... | collective-permute-start | bytes 294920 | tf_op jit(solution)/shard_map/ppermute | solution.py:261
  8.7 14.1 %collective-permute-start.2 = (bf16[2,32,768]{2,1,0:T(8,128)(2,1)S(1)}, bf16[2,32,768]{2,1,0:T(8,128)(2,1)S(1)}, u32[]{:S(2)}, u32[]{:S(2)}) collective-permute-start(bf16[2,32,768]{2,1,0:T(8,128)(2,1)S(1)} %get-tuple-element.28), channel_id=1, source_target_pairs={{0,3},{1,2},{2,1},{3,0},{4,7},{5,6},{6,5},{7,4},{8,11},{9,10},{10,... | collective-permute-start | bytes 294920 | tf_op jit(solution)/shard_map/ppermute | solution.py:261
  12.5 2.3 %copy-start = (bf16[4,768,768]{2,1,0:T(8,128)(2,1)S(1)}, bf16[4,768,768]{2,1,0:T(8,128)(2,1)}, u32[]{:S(2)}) copy-start(bf16[4,768,768]{2,1,0:T(8,128)(2,1)} %refs_8_.1) | copy-start | bytes 14155780
  14.8 1.1 %copy-start.2 = (bf16[16,32,768]{2,1,0:T(8,128)(2,1)S(1)}, bf16[16,32,768]{2,1,0:T(8,128)(2,1)}, u32[]{:S(2)}) copy-start(bf16[16,32,768]{2,1,0:T(8,128)(2,1)} %param.3) | copy-start | bytes 2359300
  15.9 2.3 %copy-start.1 = (bf16[4,768,768]{2,1,0:T(8,128)(2,1)S(1)}, bf16[4,768,768]{2,1,0:T(8,128)(2,1)}, u32[]{:S(2)}) copy-start(bf16[4,768,768]{2,1,0:T(8,128)(2,1)} %refs_8_.1) | copy-start | bytes 14155780
  17.2 3.2 %copy-start.3 = (bf16[16,32,768]{2,1,0:T(8,128)(2,1)S(1)}, bf16[16,32,768]{2,1,0:T(8,128)(2,1)}, u32[]{:S(2)}) copy-start(bf16[16,32,768]{2,1,0:T(8,128)(2,1)} %param.3) | copy-start | bytes 2359300
  20.4 30.2 %slice-start = ((s8[4718592]{0:T(1024)(128)(4,1)}), s8[4194304]{0:T(1024)(128)(4,1)S(1)}, s32[]{:S(2)}) async-start(s8[4718592]{0:T(1024)(128)(4,1)} %bitcast.19), calls=%async_computation.1 | async-start | bytes 8388608
  22.7 27.9 %slice-start.1 = ((s8[4718592]{0:T(1024)(128)(4,1)}), s8[524288]{0:T(1024)(128)(4,1)S(1)}, s32[]{:S(2)}) async-start(s8[4718592]{0:T(1024)(128)(4,1)} %bitcast.19), calls=%async_computation.2 | async-start | bytes 1048576
  55.5 8.8 %collective-permute-start.4 = (bf16[2,64,768]{2,1,0:T(8,128)(2,1)S(1)}, bf16[2,64,768]{2,1,0:T(8,128)(2,1)S(1)}, u32[]{:S(2)}, u32[]{:S(2)}) collective-permute-start(bf16[2,64,768]{2,1,0:T(8,128)(2,1)S(1)} %get-tuple-element.21), channel_id=1, source_target_pairs={{0,24},{4,28},{8,16},{12,20},{16,8},{20,12},{24,0},{28,4},{1,25},{... | collective-permute-start | bytes 589832 | tf_op jit(solution)/shard_map/ppermute | solution.py:328
  58.0 8.5 %collective-permute-start.6 = (bf16[64,768]{1,0:T(8,128)(2,1)S(1)}, bf16[64,768]{1,0:T(8,128)(2,1)S(1)}, u32[]{:S(2)}, u32[]{:S(2)}) collective-permute-start(bf16[64,768]{1,0:T(8,128)(2,1)S(1)} %get-tuple-element.22), channel_id=1, source_target_pairs={{0,16},{4,20},{8,24},{12,28},{16,0},{20,4},{24,8},{28,12},{1,17},{... | collective-permute-start | bytes 294920 | tf_op jit(solution)/shard_map/ppermute | solution.py:328
  58.5 8.0 %collective-permute-start.7 = (bf16[64,768]{1,0:T(8,128)(2,1)S(1)}, bf16[64,768]{1,0:T(8,128)(2,1)S(1)}, u32[]{:S(2)}, u32[]{:S(2)}) collective-permute-start(bf16[64,768]{1,0:T(8,128)(2,1)S(1)} %get-tuple-element.23), channel_id=1, source_target_pairs={{0,8},{4,12},{8,0},{12,4},{16,24},{20,28},{24,16},{28,20},{1,9},{5... | collective-permute-start | bytes 294920 | tf_op jit(solution)/shard_map/ppermute | solution.py:328
  59.1 8.1 %collective-permute-start.8 = (bf16[64,768]{1,0:T(8,128)(2,1)S(1)}, bf16[64,768]{1,0:T(8,128)(2,1)S(1)}, u32[]{:S(2)}, u32[]{:S(2)}) collective-permute-start(bf16[64,768]{1,0:T(8,128)(2,1)S(1)} %get-tuple-element.24), channel_id=1, source_target_pairs={{0,20},{4,16},{8,28},{12,24},{16,4},{20,0},{24,12},{28,8},{1,21},{... | collective-permute-start | bytes 294920 | tf_op jit(solution)/shard_map/ppermute | solution.py:328
  59.1 8.0 %collective-permute-start.9 = (bf16[64,768]{1,0:T(8,128)(2,1)S(1)}, bf16[64,768]{1,0:T(8,128)(2,1)S(1)}, u32[]{:S(2)}, u32[]{:S(2)}) collective-permute-start(bf16[64,768]{1,0:T(8,128)(2,1)S(1)} %get-tuple-element.25), channel_id=1, source_target_pairs={{0,12},{4,8},{8,4},{12,0},{16,28},{20,24},{24,20},{28,16},{1,13},{... | collective-permute-start | bytes 294920 | tf_op jit(solution)/shard_map/ppermute | solution.py:328
  64.3 2.9 %collective-permute-start.5 = (bf16[64,768]{1,0:T(8,128)(2,1)S(1)}, bf16[64,768]{1,0:T(8,128)(2,1)S(1)}, u32[]{:S(2)}, u32[]{:S(2)}) collective-permute-start(bf16[64,768]{1,0:T(8,128)(2,1)S(1)} %slice_bitcast_fusion), channel_id=1, source_target_pairs={{0,4},{4,0},{8,12},{12,8},{16,20},{20,16},{24,28},{28,24},{1,5},{5... | collective-permute-start | bytes 294920 | tf_op jit(solution)/shard_map/ppermute | solution.py:328

commit v7 on v6

--- a/solution.py
+++ b/solution.py
@@ -308,7 +308,7 @@
     after = before[0]
     after = lax.all_to_all(after, ("space", "tm"), split_axis=0, concat_axis=0, tiled=True)
     both = [k for k in range(tm // 2) if k.bit_count() != 1]
-    direct = [2 * k + s for s in range(2) for k in reversed(range(tm // 2)) if k not in both]
+    direct = [2 * k + s for s in range(2) for k in range(tm // 2) if k not in both]
     result = call(
         functools.partial(time_kernel, toks=share, both=both, direct=direct),
         "temporal",

time: 68.8 us -> 68.8 us (level)
  no operation moved by 1% of the time
where the time goes in v7:
time: 68.8 us; the launch traced here: 68.4 us
  blocking collectives  27.6 us (40%)
  starting transfers between devices  15.9 us (23%)
  Pallas kernels  13.4 us (19%)
  local copies, waits for them, and re-layouts  7.44 us (11%)
  waiting for transfers between devices  3.9 us (6%)
    all_to_all x1, blocking collectives, on_device(): lax.all_to_all(after, ('space', 'tm'), split_axis=0, concat_axis=0, tiled...  25.5 us
    pallas_call x8, Pallas kernels, call(): pl.pallas_call(kernel, out_shape=like, in_specs=[within] * len(args), out...  13.4 us
    ppermute x4, starting transfers between devices, over_space(): lax.ppermute(part, 'space', [(i, i ^ distance) for i in range(space)])  9.62 us
    ppermute x6, starting transfers between devices, over_tm(): return lax.ppermute(part, 'tm', [(i, i ^ distance) for i in range(tm)])  6.3 us
    unnamed x12, local copies, waits for them, and re-layouts  4.59 us
    ppermute x6, waiting for transfers between devices, over_tm(): return lax.ppermute(part, 'tm', [(i, i ^ distance) for i in range(tm)])  3.21 us
    all_gather x1, blocking collectives, on_device(): beside = [lax.all_gather(whole[0][1], 'tm', axis_index_groups=pairs)]  2.07 us
    squeeze x2, local copies, waits for them, and re-layouts, on_device(): parts[k] = lax.dynamic_index_in_dim(held, me ^ k, 0, keepdims=False)  1.88 us
  transfers between devices with their start and end apart: 10, of which 3 were waited for; matrix products, arithmetic and copies ran while one was open for 3% of the time, Pallas kernels for 7%

profile of v7, /device:TPU:0, one launch (start us, length us, event | category | flops | bytes accessed | tf_op | source)
XLA Modules:
  0.0 68.4 jit_solution(13030927496400608492)
XLA Ops:
  0.0 0.9 %dynamic-slice_bitcast_fusion.1 = bf16[4,32,768]{2,1,0:T(8,128)(2,1)S(1)} fusion(bf16[4,4,32,768]{3,2,1,0:T(8,128)(2,1)} %bitcast.12, s32[]{:T(128)S(6)} %select_n.10), kind=kLoop, calls=%fused_computation.1 | loop fusion | bytes 393220 | tf_op jit(solution)/shard_map/jit(dynamic_index_in_dim)/squeeze | solution.py:257
  0.9 4.1 %collective-permute-start = (bf16[4,32,768]{2,1,0:T(8,128)(2,1)S(1)}, bf16[4,32,768]{2,1,0:T(8,128)(2,1)S(1)}, u32[]{:S(2)}, u32[]{:S(2)}) collective-permute-start(bf16[4,32,768]{2,1,0:T(8,128)(2,1)S(1)} %dynamic-slice_bitcast_fusion.1), channel_id=1, source_target_pairs={{0,2},{1,3},{2,0},{3,1},{4,6},{5,7},{6,4},{7,5},{8,10},{9,11},{10,... | collective-permute-start | bytes 589832 | tf_op jit(solution)/shard_map/ppermute | solution.py:261
  5.0 0.9 %dynamic-slice_bitcast_fusion = bf16[4,32,768]{2,1,0:T(8,128)(2,1)S(1)} fusion(bf16[4,4,32,768]{3,2,1,0:T(8,128)(2,1)} %bitcast.13, s32[]{:T(128)S(6)} %select_n.11), kind=kLoop, calls=%fused_computation | loop fusion | bytes 393220 | tf_op jit(solution)/shard_map/jit(dynamic_index_in_dim)/squeeze | solution.py:257
  6.0 1.6 %collective-permute-start.1 = (bf16[4,32,768]{2,1,0:T(8,128)(2,1)S(1)}, bf16[4,32,768]{2,1,0:T(8,128)(2,1)S(1)}, u32[]{:S(2)}, u32[]{:S(2)}) collective-permute-start(bf16[4,32,768]{2,1,0:T(8,128)(2,1)S(1)} %dynamic-slice_bitcast_fusion), channel_id=1, source_target_pairs={{0,1},{1,0},{2,3},{3,2},{4,5},{5,4},{6,7},{7,6},{8,9},{9,8},{10,11... | collective-permute-start | bytes 589832 | tf_op jit(solution)/shard_map/ppermute | solution.py:261
  7.6 1.0 %dynamic-slice_bitcast_fusion.2 = (bf16[2,32,768]{2,1,0:T(8,128)(2,1)S(1)}, bf16[2,32,768]{2,1,0:T(8,128)(2,1)S(1)}) fusion(bf16[4,4,32,768]{3,2,1,0:T(8,128)(2,1)} %bitcast.14, s32[]{:T(128)S(6)} %select_n.12, s32[]{:T(128)S(6)} %add.13), kind=kLoop, calls=%fused_computation.3 | loop fusion | bytes 393224 | tf_op jit(solution)/shard_map/slice | solution.py:266
  8.6 0.1 collective-permute-start.3
  8.7 3.8 %collective-permute-start.2 = (bf16[2,32,768]{2,1,0:T(8,128)(2,1)S(1)}, bf16[2,32,768]{2,1,0:T(8,128)(2,1)S(1)}, u32[]{:S(2)}, u32[]{:S(2)}) collective-permute-start(bf16[2,32,768]{2,1,0:T(8,128)(2,1)S(1)} %get-tuple-element.28), channel_id=1, source_target_pairs={{0,3},{1,2},{2,1},{3,0},{4,7},{5,6},{6,5},{7,4},{8,11},{9,10},{10,... | collective-permute-start | bytes 294920 | tf_op jit(solution)/shard_map/ppermute | solution.py:261
  12.5 2.3 %copy-done = bf16[4,768,768]{2,1,0:T(8,128)(2,1)S(1)} copy-done((bf16[4,768,768]{2,1,0:T(8,128)(2,1)S(1)}, bf16[4,768,768]{2,1,0:T(8,128)(2,1)}, u32[]{:S(2)}) %copy-start) | copy-done | bytes 4718616
  14.8 1.1 %copy-done.2 = bf16[16,32,768]{2,1,0:T(8,128)(2,1)S(1)} copy-done((bf16[16,32,768]{2,1,0:T(8,128)(2,1)S(1)}, bf16[16,32,768]{2,1,0:T(8,128)(2,1)}, u32[]{:S(2)}) %copy-start.2) | copy-done | bytes 786456
  15.9 0.7 %project.3._.refs_4_ = bf16[3,1,4,32,768]{4,3,2,1,0:T(8,128)(2,1)S(1)} custom-call(bf16[4,4,32,768]{3,2,1,0:T(8,128)(2,1)S(1)} %bitcast.15, bf16[4,768,768]{2,1,0:T(8,128)(2,1)S(1)} %copy-done), custom_call_target="tpu_custom_call" | custom-call | flops 452984832 | bytes 6094848 | tf_op jit(solution)/shard_map/project/pallas_call | solution.py:225
  16.7 0.5 orders.1
  17.2 0.0 copy-start.3
  17.2 1.1 %copy-done.1 = bf16[4,768,768]{2,1,0:T(8,128)(2,1)S(1)} copy-done((bf16[4,768,768]{2,1,0:T(8,128)(2,1)S(1)}, bf16[4,768,768]{2,1,0:T(8,128)(2,1)}, u32[]{:S(2)}) %copy-start.1) | copy-done | bytes 4718616
  18.3 0.7 %project.4.refs_5_ = bf16[3,1,4,32,768]{4,3,2,1,0:T(8,128)(2,1)S(1)} custom-call(bf16[4,32,768]{2,1,0:T(8,128)(2,1)S(1)} %collective-permute-done.refs_0_.refs_1_, bf16[4,768,768]{2,1,0:T(8,128)(2,1)S(1)} %copy-done.1), custom_call_target="tpu_custom_call" | custom-call | flops 452984832 | bytes 5505024 | tf_op jit(solution)/shard_map/project/pallas_call | solution.py:225
  19.0 0.7 %collective-permute-done.1.refs_0_.refs_2_ = bf16[4,32,768]{2,1,0:T(8,128)(2,1)S(1)} collective-permute-done((bf16[4,32,768]{2,1,0:T(8,128)(2,1)S(1)}, bf16[4,32,768]{2,1,0:T(8,128)(2,1)S(1)}, u32[]{:S(2)}, u32[]{:S(2)}) %collective-permute-start.1) | collective-permute-done | bytes 196640 | tf_op jit(solution)/shard_map/ppermute | solution.py:261
  19.7 0.7 %project.5.refs_6_ = bf16[3,1,4,32,768]{4,3,2,1,0:T(8,128)(2,1)S(1)} custom-call(bf16[4,32,768]{2,1,0:T(8,128)(2,1)S(1)} %collective-permute-done.1.refs_0_.refs_2_, bf16[4,768,768]{2,1,0:T(8,128)(2,1)S(1)} %copy-done.1), custom_call_target="tpu_custom_call" | custom-call | flops 452984832 | bytes 5505024 | tf_op jit(solution)/shard_map/project/pallas_call | solution.py:225
  20.4 0.0 slice-start
  20.4 2.3 %spatial.2.refs_7_ = bf16[32,8,768]{2,1,0:T(8,128)(2,1)S(1)} custom-call(bf16[4,4,32,768]{3,2,1,0:T(8,128)(2,1)S(1)} %bitcast.16, bf16[4,32,768]{2,1,0:T(8,128)(2,1)S(1)} %collective-permute-done.refs_0_.refs_1_, bf16[4,32,768]{2,1,0:T(8,128)(2,1)S(1)} %collective-permute-done.1.refs_0_.refs_2_, bf16[2,32,768]{2,1,0:T(8,128)(2,1)S(1)} %collective-permute-done.3.refs_3_, ...), custom_call_target="tpu_custom_call" | custom-call | flops 603979776 | bytes 8290304 | tf_op jit(solution)/shard_map/spatial/pallas_call | solution.py:225
  22.7 0.0 slice-start.1
  22.8 2.3 %spatial.3 = bf16[32,16,768]{2,1,0:T(8,128)(2,1)S(1)} custom-call(bf16[4,4,32,768]{3,2,1,0:T(8,128)(2,1)S(1)} %bitcast.17, bf16[4,32,768]{2,1,0:T(8,128)(2,1)S(1)} %collective-permute-done.refs_0_.refs_1_, bf16[4,32,768]{2,1,0:T(8,128)(2,1)S(1)} %collective-permute-done.1.refs_0_.refs_2_, bf16[2,32,768]{2,1,0:T(8,128)(2,1)S(1)} %collective-permute-done.2.refs_3_, ...), custom_call_target="tpu_custom_call" | custom-call | flops 603979776 | bytes 9076736 | tf_op jit(solution)/shard_map/spatial/pallas_call | solution.py:225
  25.1 25.5 %all_to_all.5 = bf16[32,16,768]{2,1,0:T(8,128)(2,1)S(1)} all-to-all(bf16[32,16,768]{2,1,0:T(8,128)(2,1)S(1)} %spatial.3), channel_id=1, replica_groups=mesh['tm'=8,'space'=4] {'space','tm'}, dimensions={0} | all-to-all | bytes 1572864 | tf_op jit(solution)/shard_map/all_to_all | solution.py:309
  50.6 4.9 %temporal.1 = (bf16[2,64,768]{2,1,0:T(8,128)(2,1)S(1)}, bf16[2,64,768]{2,1,0:T(8,128)(2,1)S(1)}, bf16[64,768]{1,0:T(8,128)(2,1)S(1)}, bf16[64,768]{1,0:T(8,128)(...) custom-call(bf16[4,8,16,768]{3,2,1,0:T(8,128)(2,1)S(1)} %bitcast.18, ...), custom_call_target="tpu_custom_call" | custom-call | flops 3019898880 | bytes 6815744 | tf_op jit(solution)/shard_map/temporal/pallas_call | solution.py:225
  55.5 2.5 %collective-permute-start.4 = (bf16[2,64,768]{2,1,0:T(8,128)(2,1)S(1)}, bf16[2,64,768]{2,1,0:T(8,128)(2,1)S(1)}, u32[]{:S(2)}, u32[]{:S(2)}) collective-permute-start(bf16[2,64,768]{2,1,0:T(8,128)(2,1)S(1)} %get-tuple-element.21), channel_id=1, source_target_pairs={{0,24},{4,28},{8,16},{12,20},{16,8},{20,12},{24,0},{28,4},{1,25},{... | collective-permute-start | bytes 589832 | tf_op jit(solution)/shard_map/ppermute | solution.py:328
  58.0 0.6 collective-permute-start.6
  58.6 0.5 collective-permute-start.7
  59.1 0.4 collective-permute-start.8
  59.5 2.3 %collective-permute-start.9 = (bf16[64,768]{1,0:T(8,128)(2,1)S(1)}, bf16[64,768]{1,0:T(8,128)(2,1)S(1)}, u32[]{:S(2)}, u32[]{:S(2)}) collective-permute-start(bf16[64,768]{1,0:T(8,128)(2,1)S(1)} %get-tuple-element.25), channel_id=1, source_target_pairs={{0,20},{4,16},{8,28},{12,24},{16,4},{20,0},{24,12},{28,8},{1,21},{... | collective-permute-start | bytes 294920 | tf_op jit(solution)/shard_map/ppermute | solution.py:328
  61.7 2.5 %collective-permute-done.4.refs_1_ = bf16[2,64,768]{2,1,0:T(8,128)(2,1)S(1)} collective-permute-done((bf16[2,64,768]{2,1,0:T(8,128)(2,1)S(1)}, bf16[2,64,768]{2,1,0:T(8,128)(2,1)S(1)}, u32[]{:S(2)}, u32[]{:S(2)}) %collective-permute-start.4) | collective-permute-done | bytes 196640 | tf_op jit(solution)/shard_map/ppermute | solution.py:328
  64.3 0.1 collective-permute-start.5
  64.4 2.1 %all_gather.3.refs_2_ = bf16[2,64,768]{2,1,0:T(8,128)(2,1)S(1)} all-gather(bf16[1,64,768]{2,1,0:T(8,128)(2,1)S(1)} %slice.22), channel_id=1, replica_groups={{0,4},{8,12},{16,20},{24,28},{1,5},{9,13},{17,21},{25,29},{2,6},{10,14}..., dimensions={0}, use_global_device_ids=true | all-gather | bytes 294912 | tf_op jit(solution)/shard_map/all_gather | solution.py:332
  66.5 0.7 collective-permute-done.9.refs_7_
  67.1 1.3 %place.1 = bf16[16,32,768]{2,1,0:T(8,128)(2,1)} custom-call(bf16[2,64,768]{2,1,0:T(8,128)(2,1)S(1)} %get-tuple-element.20.refs_0_, bf16[2,64,768]{2,1,0:T(8,128)(2,1)S(1)} %collective-permute-done.4.refs_1_, bf16[2,64,768]{2,1,0:T(8,128)(2,1)S(1)} %all_gather.3.refs_2_, bf16[64,768]{1,0:T(8,128)(2,1)S(1)} %collective-permute-done.5.refs_3_, ...), custom_call_target="tpu_custom_call" | custom-call | bytes 2392064 | tf_op jit(solution)/shard_map/place/pallas_call | solution.py:225
  (16 shorter events, 0.0 us)
Async XLA Ops:
  0.9 16.2 %collective-permute-start = (bf16[4,32,768]{2,1,0:T(8,128)(2,1)S(1)}, bf16[4,32,768]{2,1,0:T(8,128)(2,1)S(1)}, u32[]{:S(2)}, u32[]{:S(2)}) collective-permute-start(bf16[4,32,768]{2,1,0:T(8,128)(2,1)S(1)} %dynamic-slice_bitcast_fusion.1), channel_id=1, source_target_pairs={{0,2},{1,3},{2,0},{3,1},{4,6},{5,7},{6,4},{7,5},{8,10},{9,11},{10,... | collective-permute-start | bytes 589832 | tf_op jit(solution)/shard_map/ppermute | solution.py:261
  6.0 13.7 %collective-permute-start.1 = (bf16[4,32,768]{2,1,0:T(8,128)(2,1)S(1)}, bf16[4,32,768]{2,1,0:T(8,128)(2,1)S(1)}, u32[]{:S(2)}, u32[]{:S(2)}) collective-permute-start(bf16[4,32,768]{2,1,0:T(8,128)(2,1)S(1)} %dynamic-slice_bitcast_fusion), channel_id=1, source_target_pairs={{0,1},{1,0},{2,3},{3,2},{4,5},{5,4},{6,7},{7,6},{8,9},{9,8},{10,11... | collective-permute-start | bytes 589832 | tf_op jit(solution)/shard_map/ppermute | solution.py:261
  8.6 11.8 %collective-permute-start.3 = (bf16[2,32,768]{2,1,0:T(8,128)(2,1)S(1)}, bf16[2,32,768]{2,1,0:T(8,128)(2,1)S(1)}, u32[]{:S(2)}, u32[]{:S(2)}) collective-permute-start(bf16[2,32,768]{2,1,0:T(8,128)(2,1)S(1)} %get-tuple-element.27), channel_id=1, source_target_pairs={{0,3},{1,2},{2,1},{3,0},{4,7},{5,6},{6,5},{7,4},{8,11},{9,10},{10,... | collective-permute-start | bytes 294920 | tf_op jit(solution)/shard_map/ppermute | solution.py:261
  8.7 14.1 %collective-permute-start.2 = (bf16[2,32,768]{2,1,0:T(8,128)(2,1)S(1)}, bf16[2,32,768]{2,1,0:T(8,128)(2,1)S(1)}, u32[]{:S(2)}, u32[]{:S(2)}) collective-permute-start(bf16[2,32,768]{2,1,0:T(8,128)(2,1)S(1)} %get-tuple-element.28), channel_id=1, source_target_pairs={{0,3},{1,2},{2,1},{3,0},{4,7},{5,6},{6,5},{7,4},{8,11},{9,10},{10,... | collective-permute-start | bytes 294920 | tf_op jit(solution)/shard_map/ppermute | solution.py:261
  12.5 2.3 %copy-start = (bf16[4,768,768]{2,1,0:T(8,128)(2,1)S(1)}, bf16[4,768,768]{2,1,0:T(8,128)(2,1)}, u32[]{:S(2)}) copy-start(bf16[4,768,768]{2,1,0:T(8,128)(2,1)} %refs_8_.1) | copy-start | bytes 14155780
  14.8 1.1 %copy-start.2 = (bf16[16,32,768]{2,1,0:T(8,128)(2,1)S(1)}, bf16[16,32,768]{2,1,0:T(8,128)(2,1)}, u32[]{:S(2)}) copy-start(bf16[16,32,768]{2,1,0:T(8,128)(2,1)} %param.3) | copy-start | bytes 2359300
  15.9 2.3 %copy-start.1 = (bf16[4,768,768]{2,1,0:T(8,128)(2,1)S(1)}, bf16[4,768,768]{2,1,0:T(8,128)(2,1)}, u32[]{:S(2)}) copy-start(bf16[4,768,768]{2,1,0:T(8,128)(2,1)} %refs_8_.1) | copy-start | bytes 14155780
  17.2 3.2 %copy-start.3 = (bf16[16,32,768]{2,1,0:T(8,128)(2,1)S(1)}, bf16[16,32,768]{2,1,0:T(8,128)(2,1)}, u32[]{:S(2)}) copy-start(bf16[16,32,768]{2,1,0:T(8,128)(2,1)} %param.3) | copy-start | bytes 2359300
  20.4 30.2 %slice-start = ((s8[4718592]{0:T(1024)(128)(4,1)}), s8[4194304]{0:T(1024)(128)(4,1)S(1)}, s32[]{:S(2)}) async-start(s8[4718592]{0:T(1024)(128)(4,1)} %bitcast.19), calls=%async_computation.1 | async-start | bytes 8388608
  22.7 27.9 %slice-start.1 = ((s8[4718592]{0:T(1024)(128)(4,1)}), s8[524288]{0:T(1024)(128)(4,1)S(1)}, s32[]{:S(2)}) async-start(s8[4718592]{0:T(1024)(128)(4,1)} %bitcast.19), calls=%async_computation.2 | async-start | bytes 1048576
  55.5 8.8 %collective-permute-start.4 = (bf16[2,64,768]{2,1,0:T(8,128)(2,1)S(1)}, bf16[2,64,768]{2,1,0:T(8,128)(2,1)S(1)}, u32[]{:S(2)}, u32[]{:S(2)}) collective-permute-start(bf16[2,64,768]{2,1,0:T(8,128)(2,1)S(1)} %get-tuple-element.21), channel_id=1, source_target_pairs={{0,24},{4,28},{8,16},{12,20},{16,8},{20,12},{24,0},{28,4},{1,25},{... | collective-permute-start | bytes 589832 | tf_op jit(solution)/shard_map/ppermute | solution.py:328
  58.0 8.5 %collective-permute-start.6 = (bf16[64,768]{1,0:T(8,128)(2,1)S(1)}, bf16[64,768]{1,0:T(8,128)(2,1)S(1)}, u32[]{:S(2)}, u32[]{:S(2)}) collective-permute-start(bf16[64,768]{1,0:T(8,128)(2,1)S(1)} %get-tuple-element.22), channel_id=1, source_target_pairs={{0,8},{4,12},{8,0},{12,4},{16,24},{20,28},{24,16},{28,20},{1,9},{5... | collective-permute-start | bytes 294920 | tf_op jit(solution)/shard_map/ppermute | solution.py:328
  58.6 7.9 %collective-permute-start.7 = (bf16[64,768]{1,0:T(8,128)(2,1)S(1)}, bf16[64,768]{1,0:T(8,128)(2,1)S(1)}, u32[]{:S(2)}, u32[]{:S(2)}) collective-permute-start(bf16[64,768]{1,0:T(8,128)(2,1)S(1)} %get-tuple-element.23), channel_id=1, source_target_pairs={{0,16},{4,20},{8,24},{12,28},{16,0},{20,4},{24,8},{28,12},{1,17},{... | collective-permute-start | bytes 294920 | tf_op jit(solution)/shard_map/ppermute | solution.py:328
  59.1 7.4 %collective-permute-start.8 = (bf16[64,768]{1,0:T(8,128)(2,1)S(1)}, bf16[64,768]{1,0:T(8,128)(2,1)S(1)}, u32[]{:S(2)}, u32[]{:S(2)}) collective-permute-start(bf16[64,768]{1,0:T(8,128)(2,1)S(1)} %get-tuple-element.24), channel_id=1, source_target_pairs={{0,12},{4,8},{8,4},{12,0},{16,28},{20,24},{24,20},{28,16},{1,13},{... | collective-permute-start | bytes 294920 | tf_op jit(solution)/shard_map/ppermute | solution.py:328
  59.5 7.7 %collective-permute-start.9 = (bf16[64,768]{1,0:T(8,128)(2,1)S(1)}, bf16[64,768]{1,0:T(8,128)(2,1)S(1)}, u32[]{:S(2)}, u32[]{:S(2)}) collective-permute-start(bf16[64,768]{1,0:T(8,128)(2,1)S(1)} %get-tuple-element.25), channel_id=1, source_target_pairs={{0,20},{4,16},{8,28},{12,24},{16,4},{20,0},{24,12},{28,8},{1,21},{... | collective-permute-start | bytes 294920 | tf_op jit(solution)/shard_map/ppermute | solution.py:328
  64.3 2.9 %collective-permute-start.5 = (bf16[64,768]{1,0:T(8,128)(2,1)S(1)}, bf16[64,768]{1,0:T(8,128)(2,1)S(1)}, u32[]{:S(2)}, u32[]{:S(2)}) collective-permute-start(bf16[64,768]{1,0:T(8,128)(2,1)S(1)} %slice_bitcast_fusion), channel_id=1, source_target_pairs={{0,4},{4,0},{8,12},{12,8},{16,20},{20,16},{24,28},{28,24},{1,5},{5... | collective-permute-start | bytes 294920 | tf_op jit(solution)/shard_map/ppermute | solution.py:328

commit v8 on v6

--- a/solution.py
+++ b/solution.py
@@ -58,9 +58,7 @@
 
 
 def table_kernel(_, *out_refs, **sizes):
-    some, rows = out_refs[0].shape[0], out_refs[1].shape[0]
-    leave_space, _, _ = orders(some, **sizes)
-    _, enter_time, leave_time = orders(rows, **sizes)
+    leave_space, enter_time, leave_time = orders(out_refs[0].shape[0], **sizes)
     me = lax.axis_index("tm")
     for out_ref, source in zip(out_refs, (leave_space, enter_time, lambda r: leave_time(r, me))):
         shape = out_ref.shape
@@ -152,15 +150,16 @@
         for i, c in enumerate(clip_refs)
     ]
     after = dot(mix_ref[...], w_ref[3]) + jnp.concatenate(clip, axis=0).astype(F32)
-    after = dot(order_ref[...], after.astype(BF16)).astype(BF16)
-    after = after.reshape(count, groups, frames * share, width)
+    after = after.astype(BF16)
+    if len(out_ref.shape) == 2:
+        out_ref[...] = after
+        return
+    if before is not None:
+        after = jnp.concatenate([before[...], after], axis=0)
+    after = dot(order_ref[...], after).astype(BF16).reshape(count, groups, -1, width)
     me = lax.axis_index("space")
     for i, k in enumerate(distances):
-        at = pl.ds((me ^ k) * groups, groups)
-        if before is None:
-            out_ref[at] = after[i]
-        else:
-            out_ref[at] = jnp.concatenate([before[at], after[i]], axis=1)
+        out_ref[pl.ds((me ^ k) * groups, groups)] = after[i]
 
 
 def time_kernel(x_ref, w_ref, order_ref, *refs, toks, both, direct):
@@ -282,7 +281,7 @@
             table_kernel, count=space, groups=tm, share=share
         ),
         "orders",
-        [(rows // chunks, rows // chunks), (rows, rows), (rows, rows)],
+        [(rows, rows)] * 3,
         qkv[0],
     )
     before = []
@@ -292,7 +291,7 @@
                 space_kernel, distances=early + late, late=len(late), groups=tm, first=c * step
             ),
             "spatial",
-            [(space * tm, (c + 1) * step * share, width)],
+            [(rows // chunks, width) if c < chunks - 1 else (space * tm, block, width)],
             *[parts[k] for k in early],
             *ends[c],
             *qkv,

time: 68.8 us -> 68.9 us (level)
  no operation moved by 1% of the time
where the time goes in v8:
time: 68.9 us; the launch traced here: 68.5 us
  blocking collectives  27.6 us (40%)
  starting transfers between devices  15.9 us (23%)
  Pallas kernels  13.6 us (20%)
  local copies, waits for them, and re-layouts  7.33 us (11%)
  waiting for transfers between devices  3.95 us (6%)
    all_to_all x1, blocking collectives, on_device(): lax.all_to_all(after, ('space', 'tm'), split_axis=0, concat_axis=0, tiled...  25.5 us
    pallas_call x8, Pallas kernels, call(): pl.pallas_call(kernel, out_shape=like, in_specs=[within] * len(args), out...  13.6 us
    ppermute x4, starting transfers between devices, over_space(): lax.ppermute(part, 'space', [(i, i ^ distance) for i in range(space)])  9.62 us
    ppermute x6, starting transfers between devices, over_tm(): return lax.ppermute(part, 'tm', [(i, i ^ distance) for i in range(tm)])  6.3 us
    unnamed x12, local copies, waits for them, and re-layouts  4.48 us
    ppermute x6, waiting for transfers between devices, over_tm(): return lax.ppermute(part, 'tm', [(i, i ^ distance) for i in range(tm)])  3.26 us
    all_gather x1, blocking collectives, on_device(): beside = [lax.all_gather(whole[0][1], 'tm', axis_index_groups=pairs)]  2.07 us
    squeeze x2, local copies, waits for them, and re-layouts, on_device(): parts[k] = lax.dynamic_index_in_dim(held, me ^ k, 0, keepdims=False)  1.88 us
  transfers between devices with their start and end apart: 10, of which 3 were waited for; matrix products, arithmetic and copies ran while one was open for 3% of the time, Pallas kernels for 7%

profile of v8, /device:TPU:0, one launch (start us, length us, event | category | flops | bytes accessed | tf_op | source)
XLA Modules:
  0.0 68.5 jit_solution(4216104902834095072)
XLA Ops:
  0.0 0.9 %dynamic-slice_bitcast_fusion.1 = bf16[4,32,768]{2,1,0:T(8,128)(2,1)S(1)} fusion(bf16[4,4,32,768]{3,2,1,0:T(8,128)(2,1)} %bitcast.12, s32[]{:T(128)S(6)} %select_n.10), kind=kLoop, calls=%fused_computation.1 | loop fusion | bytes 393220 | tf_op jit(solution)/shard_map/jit(dynamic_index_in_dim)/squeeze | solution.py:256
  0.9 4.1 %collective-permute-start = (bf16[4,32,768]{2,1,0:T(8,128)(2,1)S(1)}, bf16[4,32,768]{2,1,0:T(8,128)(2,1)S(1)}, u32[]{:S(2)}, u32[]{:S(2)}) collective-permute-start(bf16[4,32,768]{2,1,0:T(8,128)(2,1)S(1)} %dynamic-slice_bitcast_fusion.1), channel_id=1, source_target_pairs={{0,2},{1,3},{2,0},{3,1},{4,6},{5,7},{6,4},{7,5},{8,10},{9,11},{10,... | collective-permute-start | bytes 589832 | tf_op jit(solution)/shard_map/ppermute | solution.py:260
  5.0 0.9 %dynamic-slice_bitcast_fusion = bf16[4,32,768]{2,1,0:T(8,128)(2,1)S(1)} fusion(bf16[4,4,32,768]{3,2,1,0:T(8,128)(2,1)} %bitcast.13, s32[]{:T(128)S(6)} %select_n.11), kind=kLoop, calls=%fused_computation | loop fusion | bytes 393220 | tf_op jit(solution)/shard_map/jit(dynamic_index_in_dim)/squeeze | solution.py:256
  6.0 1.6 %collective-permute-start.1 = (bf16[4,32,768]{2,1,0:T(8,128)(2,1)S(1)}, bf16[4,32,768]{2,1,0:T(8,128)(2,1)S(1)}, u32[]{:S(2)}, u32[]{:S(2)}) collective-permute-start(bf16[4,32,768]{2,1,0:T(8,128)(2,1)S(1)} %dynamic-slice_bitcast_fusion), channel_id=1, source_target_pairs={{0,1},{1,0},{2,3},{3,2},{4,5},{5,4},{6,7},{7,6},{8,9},{9,8},{10,11... | collective-permute-start | bytes 589832 | tf_op jit(solution)/shard_map/ppermute | solution.py:260
  7.6 1.0 %dynamic-slice_bitcast_fusion.2 = (bf16[2,32,768]{2,1,0:T(8,128)(2,1)S(1)}, bf16[2,32,768]{2,1,0:T(8,128)(2,1)S(1)}) fusion(bf16[4,4,32,768]{3,2,1,0:T(8,128)(2,1)} %bitcast.14, s32[]{:T(128)S(6)} %select_n.12, s32[]{:T(128)S(6)} %add.13), kind=kLoop, calls=%fused_computation.3 | loop fusion | bytes 393224 | tf_op jit(solution)/shard_map/slice | solution.py:265
  8.6 0.1 collective-permute-start.3
  8.7 3.8 %collective-permute-start.2 = (bf16[2,32,768]{2,1,0:T(8,128)(2,1)S(1)}, bf16[2,32,768]{2,1,0:T(8,128)(2,1)S(1)}, u32[]{:S(2)}, u32[]{:S(2)}) collective-permute-start(bf16[2,32,768]{2,1,0:T(8,128)(2,1)S(1)} %get-tuple-element.28), channel_id=1, source_target_pairs={{0,3},{1,2},{2,1},{3,0},{4,7},{5,6},{6,5},{7,4},{8,11},{9,10},{10,... | collective-permute-start | bytes 294920 | tf_op jit(solution)/shard_map/ppermute | solution.py:260
  12.5 2.3 %copy-done = bf16[4,768,768]{2,1,0:T(8,128)(2,1)S(1)} copy-done((bf16[4,768,768]{2,1,0:T(8,128)(2,1)S(1)}, bf16[4,768,768]{2,1,0:T(8,128)(2,1)}, u32[]{:S(2)}) %copy-start) | copy-done | bytes 4718616
  14.8 1.1 %copy-done.2 = bf16[16,32,768]{2,1,0:T(8,128)(2,1)S(1)} copy-done((bf16[16,32,768]{2,1,0:T(8,128)(2,1)S(1)}, bf16[16,32,768]{2,1,0:T(8,128)(2,1)}, u32[]{:S(2)}) %copy-start.2) | copy-done | bytes 786456
  15.9 0.7 %project.3._.refs_4_ = bf16[3,1,4,32,768]{4,3,2,1,0:T(8,128)(2,1)S(1)} custom-call(bf16[4,4,32,768]{3,2,1,0:T(8,128)(2,1)S(1)} %bitcast.15, bf16[4,768,768]{2,1,0:T(8,128)(2,1)S(1)} %copy-done), custom_call_target="tpu_custom_call" | custom-call | flops 452984832 | bytes 6094848 | tf_op jit(solution)/shard_map/project/pallas_call | solution.py:224
  16.7 0.6 orders.1
  17.3 0.0 copy-start.3
  17.3 1.0 %copy-done.1 = bf16[4,768,768]{2,1,0:T(8,128)(2,1)S(1)} copy-done((bf16[4,768,768]{2,1,0:T(8,128)(2,1)S(1)}, bf16[4,768,768]{2,1,0:T(8,128)(2,1)}, u32[]{:S(2)}) %copy-start.1) | copy-done | bytes 4718616
  18.3 0.7 %project.4.refs_5_ = bf16[3,1,4,32,768]{4,3,2,1,0:T(8,128)(2,1)S(1)} custom-call(bf16[4,32,768]{2,1,0:T(8,128)(2,1)S(1)} %collective-permute-done.refs_0_.refs_1_, bf16[4,768,768]{2,1,0:T(8,128)(2,1)S(1)} %copy-done.1), custom_call_target="tpu_custom_call" | custom-call | flops 452984832 | bytes 5505024 | tf_op jit(solution)/shard_map/project/pallas_call | solution.py:224
  19.0 0.7 %collective-permute-done.1.refs_0_.refs_2_ = bf16[4,32,768]{2,1,0:T(8,128)(2,1)S(1)} collective-permute-done((bf16[4,32,768]{2,1,0:T(8,128)(2,1)S(1)}, bf16[4,32,768]{2,1,0:T(8,128)(2,1)S(1)}, u32[]{:S(2)}, u32[]{:S(2)}) %collective-permute-start.1) | collective-permute-done | bytes 196640 | tf_op jit(solution)/shard_map/ppermute | solution.py:260
  19.7 0.7 %project.5.refs_6_ = bf16[3,1,4,32,768]{4,3,2,1,0:T(8,128)(2,1)S(1)} custom-call(bf16[4,32,768]{2,1,0:T(8,128)(2,1)S(1)} %collective-permute-done.1.refs_0_.refs_2_, bf16[4,768,768]{2,1,0:T(8,128)(2,1)S(1)} %copy-done.1), custom_call_target="tpu_custom_call" | custom-call | flops 452984832 | bytes 5505024 | tf_op jit(solution)/shard_map/project/pallas_call | solution.py:224
  20.4 0.0 slice-start
  20.4 2.2 %spatial.2.refs_7_ = bf16[256,768]{1,0:T(8,128)(2,1)S(1)} custom-call(bf16[4,4,32,768]{3,2,1,0:T(8,128)(2,1)S(1)} %bitcast.16, bf16[4,32,768]{2,1,0:T(8,128)(2,1)S(1)} %collective-permute-done.refs_0_.refs_1_, bf16[4,32,768]{2,1,0:T(8,128)(2,1)S(1)} %collective-permute-done.1.refs_0_.refs_2_, bf16[2,32,768]{2,1,0:T(8,128)(2,1)S(1)} %collective-permute-done.3.refs_3_, ...), custom_call_target="tpu_custom_call" | custom-call | flops 603979776 | bytes 8683520 | tf_op jit(solution)/shard_map/spatial/pallas_call | solution.py:224
  22.6 0.0 slice-start.1
  22.7 2.4 %spatial.3 = bf16[32,16,768]{2,1,0:T(8,128)(2,1)S(1)} custom-call(bf16[4,4,32,768]{3,2,1,0:T(8,128)(2,1)S(1)} %bitcast.17, bf16[4,32,768]{2,1,0:T(8,128)(2,1)S(1)} %collective-permute-done.refs_0_.refs_1_, bf16[4,32,768]{2,1,0:T(8,128)(2,1)S(1)} %collective-permute-done.1.refs_0_.refs_2_, bf16[2,32,768]{2,1,0:T(8,128)(2,1)S(1)} %collective-permute-done.2.refs_3_, ...), custom_call_target="tpu_custom_call" | custom-call | flops 603979776 | bytes 9469952 | tf_op jit(solution)/shard_map/spatial/pallas_call | solution.py:224
  25.1 25.5 %all_to_all.5 = bf16[32,16,768]{2,1,0:T(8,128)(2,1)S(1)} all-to-all(bf16[32,16,768]{2,1,0:T(8,128)(2,1)S(1)} %spatial.3), channel_id=1, replica_groups=mesh['tm'=8,'space'=4] {'space','tm'}, dimensions={0} | all-to-all | bytes 1572864 | tf_op jit(solution)/shard_map/all_to_all | solution.py:308
  50.6 4.9 %temporal.1 = (bf16[2,64,768]{2,1,0:T(8,128)(2,1)S(1)}, bf16[2,64,768]{2,1,0:T(8,128)(2,1)S(1)}, bf16[64,768]{1,0:T(8,128)(2,1)S(1)}, bf16[64,768]{1,0:T(8,128)(...) custom-call(bf16[4,8,16,768]{3,2,1,0:T(8,128)(2,1)S(1)} %bitcast.18, ...), custom_call_target="tpu_custom_call" | custom-call | flops 3019898880 | bytes 6815744 | tf_op jit(solution)/shard_map/temporal/pallas_call | solution.py:224
  55.6 2.5 %collective-permute-start.4 = (bf16[2,64,768]{2,1,0:T(8,128)(2,1)S(1)}, bf16[2,64,768]{2,1,0:T(8,128)(2,1)S(1)}, u32[]{:S(2)}, u32[]{:S(2)}) collective-permute-start(bf16[2,64,768]{2,1,0:T(8,128)(2,1)S(1)} %get-tuple-element.21), channel_id=1, source_target_pairs={{0,24},{4,28},{8,16},{12,20},{16,8},{20,12},{24,0},{28,4},{1,25},{... | collective-permute-start | bytes 589832 | tf_op jit(solution)/shard_map/ppermute | solution.py:327
  58.0 0.5 collective-permute-start.6
  58.5 0.6 collective-permute-start.7
  59.1 0.1 collective-permute-start.8
  59.2 2.6 %collective-permute-start.9 = (bf16[64,768]{1,0:T(8,128)(2,1)S(1)}, bf16[64,768]{1,0:T(8,128)(2,1)S(1)}, u32[]{:S(2)}, u32[]{:S(2)}) collective-permute-start(bf16[64,768]{1,0:T(8,128)(2,1)S(1)} %get-tuple-element.25), channel_id=1, source_target_pairs={{0,12},{4,8},{8,4},{12,0},{16,28},{20,24},{24,20},{28,16},{1,13},{... | collective-permute-start | bytes 294920 | tf_op jit(solution)/shard_map/ppermute | solution.py:327
  61.8 2.6 %collective-permute-done.4.refs_1_ = bf16[2,64,768]{2,1,0:T(8,128)(2,1)S(1)} collective-permute-done((bf16[2,64,768]{2,1,0:T(8,128)(2,1)S(1)}, bf16[2,64,768]{2,1,0:T(8,128)(2,1)S(1)}, u32[]{:S(2)}, u32[]{:S(2)}) %collective-permute-start.4) | collective-permute-done | bytes 196640 | tf_op jit(solution)/shard_map/ppermute | solution.py:327
  64.4 0.1 collective-permute-start.5
  64.5 2.1 %all_gather.3.refs_2_ = bf16[2,64,768]{2,1,0:T(8,128)(2,1)S(1)} all-gather(bf16[1,64,768]{2,1,0:T(8,128)(2,1)S(1)} %slice.22), channel_id=1, replica_groups={{0,4},{8,12},{16,20},{24,28},{1,5},{9,13},{17,21},{25,29},{2,6},{10,14}..., dimensions={0}, use_global_device_ids=true | all-gather | bytes 294912 | tf_op jit(solution)/shard_map/all_gather | solution.py:331
  66.5 0.7 collective-permute-done.8.refs_6_
  67.2 1.3 %place.1 = bf16[16,32,768]{2,1,0:T(8,128)(2,1)} custom-call(bf16[2,64,768]{2,1,0:T(8,128)(2,1)S(1)} %get-tuple-element.20.refs_0_, bf16[2,64,768]{2,1,0:T(8,128)(2,1)S(1)} %collective-permute-done.4.refs_1_, bf16[2,64,768]{2,1,0:T(8,128)(2,1)S(1)} %all_gather.3.refs_2_, bf16[64,768]{1,0:T(8,128)(2,1)S(1)} %collective-permute-done.5.refs_3_, ...), custom_call_target="tpu_custom_call" | custom-call | bytes 2392064 | tf_op jit(solution)/shard_map/place/pallas_call | solution.py:224
  (16 shorter events, 0.0 us)
Async XLA Ops:
  0.9 16.3 %collective-permute-start = (bf16[4,32,768]{2,1,0:T(8,128)(2,1)S(1)}, bf16[4,32,768]{2,1,0:T(8,128)(2,1)S(1)}, u32[]{:S(2)}, u32[]{:S(2)}) collective-permute-start(bf16[4,32,768]{2,1,0:T(8,128)(2,1)S(1)} %dynamic-slice_bitcast_fusion.1), channel_id=1, source_target_pairs={{0,2},{1,3},{2,0},{3,1},{4,6},{5,7},{6,4},{7,5},{8,10},{9,11},{10,... | collective-permute-start | bytes 589832 | tf_op jit(solution)/shard_map/ppermute | solution.py:260
  6.0 13.7 %collective-permute-start.1 = (bf16[4,32,768]{2,1,0:T(8,128)(2,1)S(1)}, bf16[4,32,768]{2,1,0:T(8,128)(2,1)S(1)}, u32[]{:S(2)}, u32[]{:S(2)}) collective-permute-start(bf16[4,32,768]{2,1,0:T(8,128)(2,1)S(1)} %dynamic-slice_bitcast_fusion), channel_id=1, source_target_pairs={{0,1},{1,0},{2,3},{3,2},{4,5},{5,4},{6,7},{7,6},{8,9},{9,8},{10,11... | collective-permute-start | bytes 589832 | tf_op jit(solution)/shard_map/ppermute | solution.py:260
  8.6 11.8 %collective-permute-start.3 = (bf16[2,32,768]{2,1,0:T(8,128)(2,1)S(1)}, bf16[2,32,768]{2,1,0:T(8,128)(2,1)S(1)}, u32[]{:S(2)}, u32[]{:S(2)}) collective-permute-start(bf16[2,32,768]{2,1,0:T(8,128)(2,1)S(1)} %get-tuple-element.27), channel_id=1, source_target_pairs={{0,3},{1,2},{2,1},{3,0},{4,7},{5,6},{6,5},{7,4},{8,11},{9,10},{10,... | collective-permute-start | bytes 294920 | tf_op jit(solution)/shard_map/ppermute | solution.py:260
  8.7 14.0 %collective-permute-start.2 = (bf16[2,32,768]{2,1,0:T(8,128)(2,1)S(1)}, bf16[2,32,768]{2,1,0:T(8,128)(2,1)S(1)}, u32[]{:S(2)}, u32[]{:S(2)}) collective-permute-start(bf16[2,32,768]{2,1,0:T(8,128)(2,1)S(1)} %get-tuple-element.28), channel_id=1, source_target_pairs={{0,3},{1,2},{2,1},{3,0},{4,7},{5,6},{6,5},{7,4},{8,11},{9,10},{10,... | collective-permute-start | bytes 294920 | tf_op jit(solution)/shard_map/ppermute | solution.py:260
  12.5 2.3 %copy-start = (bf16[4,768,768]{2,1,0:T(8,128)(2,1)S(1)}, bf16[4,768,768]{2,1,0:T(8,128)(2,1)}, u32[]{:S(2)}) copy-start(bf16[4,768,768]{2,1,0:T(8,128)(2,1)} %refs_8_.1) | copy-start | bytes 14155780
  14.8 1.1 %copy-start.2 = (bf16[16,32,768]{2,1,0:T(8,128)(2,1)S(1)}, bf16[16,32,768]{2,1,0:T(8,128)(2,1)}, u32[]{:S(2)}) copy-start(bf16[16,32,768]{2,1,0:T(8,128)(2,1)} %param.3) | copy-start | bytes 2359300
  15.9 2.3 %copy-start.1 = (bf16[4,768,768]{2,1,0:T(8,128)(2,1)S(1)}, bf16[4,768,768]{2,1,0:T(8,128)(2,1)}, u32[]{:S(2)}) copy-start(bf16[4,768,768]{2,1,0:T(8,128)(2,1)} %refs_8_.1) | copy-start | bytes 14155780
  17.3 3.1 %copy-start.3 = (bf16[16,32,768]{2,1,0:T(8,128)(2,1)S(1)}, bf16[16,32,768]{2,1,0:T(8,128)(2,1)}, u32[]{:S(2)}) copy-start(bf16[16,32,768]{2,1,0:T(8,128)(2,1)} %param.3) | copy-start | bytes 2359300
  20.4 30.2 %slice-start = ((s8[4718592]{0:T(1024)(128)(4,1)}), s8[4194304]{0:T(1024)(128)(4,1)S(1)}, s32[]{:S(2)}) async-start(s8[4718592]{0:T(1024)(128)(4,1)} %bitcast.19), calls=%async_computation.1 | async-start | bytes 8388608
  22.6 28.0 %slice-start.1 = ((s8[4718592]{0:T(1024)(128)(4,1)}), s8[524288]{0:T(1024)(128)(4,1)S(1)}, s32[]{:S(2)}) async-start(s8[4718592]{0:T(1024)(128)(4,1)} %bitcast.19), calls=%async_computation.2 | async-start | bytes 1048576
  55.6 8.8 %collective-permute-start.4 = (bf16[2,64,768]{2,1,0:T(8,128)(2,1)S(1)}, bf16[2,64,768]{2,1,0:T(8,128)(2,1)S(1)}, u32[]{:S(2)}, u32[]{:S(2)}) collective-permute-start(bf16[2,64,768]{2,1,0:T(8,128)(2,1)S(1)} %get-tuple-element.21), channel_id=1, source_target_pairs={{0,24},{4,28},{8,16},{12,20},{16,8},{20,12},{24,0},{28,4},{1,25},{... | collective-permute-start | bytes 589832 | tf_op jit(solution)/shard_map/ppermute | solution.py:327
  58.0 8.5 %collective-permute-start.6 = (bf16[64,768]{1,0:T(8,128)(2,1)S(1)}, bf16[64,768]{1,0:T(8,128)(2,1)S(1)}, u32[]{:S(2)}, u32[]{:S(2)}) collective-permute-start(bf16[64,768]{1,0:T(8,128)(2,1)S(1)} %get-tuple-element.22), channel_id=1, source_target_pairs={{0,16},{4,20},{8,24},{12,28},{16,0},{20,4},{24,8},{28,12},{1,17},{... | collective-permute-start | bytes 294920 | tf_op jit(solution)/shard_map/ppermute | solution.py:327
  58.5 8.0 %collective-permute-start.7 = (bf16[64,768]{1,0:T(8,128)(2,1)S(1)}, bf16[64,768]{1,0:T(8,128)(2,1)S(1)}, u32[]{:S(2)}, u32[]{:S(2)}) collective-permute-start(bf16[64,768]{1,0:T(8,128)(2,1)S(1)} %get-tuple-element.23), channel_id=1, source_target_pairs={{0,8},{4,12},{8,0},{12,4},{16,24},{20,28},{24,16},{28,20},{1,9},{5... | collective-permute-start | bytes 294920 | tf_op jit(solution)/shard_map/ppermute | solution.py:327
  59.1 8.1 %collective-permute-start.8 = (bf16[64,768]{1,0:T(8,128)(2,1)S(1)}, bf16[64,768]{1,0:T(8,128)(2,1)S(1)}, u32[]{:S(2)}, u32[]{:S(2)}) collective-permute-start(bf16[64,768]{1,0:T(8,128)(2,1)S(1)} %get-tuple-element.24), channel_id=1, source_target_pairs={{0,20},{4,16},{8,28},{12,24},{16,4},{20,0},{24,12},{28,8},{1,21},{... | collective-permute-start | bytes 294920 | tf_op jit(solution)/shard_map/ppermute | solution.py:327
  59.2 8.0 %collective-permute-start.9 = (bf16[64,768]{1,0:T(8,128)(2,1)S(1)}, bf16[64,768]{1,0:T(8,128)(2,1)S(1)}, u32[]{:S(2)}, u32[]{:S(2)}) collective-permute-start(bf16[64,768]{1,0:T(8,128)(2,1)S(1)} %get-tuple-element.25), channel_id=1, source_target_pairs={{0,12},{4,8},{8,4},{12,0},{16,28},{20,24},{24,20},{28,16},{1,13},{... | collective-permute-start | bytes 294920 | tf_op jit(solution)/shard_map/ppermute | solution.py:327
  64.4 2.9 %collective-permute-start.5 = (bf16[64,768]{1,0:T(8,128)(2,1)S(1)}, bf16[64,768]{1,0:T(8,128)(2,1)S(1)}, u32[]{:S(2)}, u32[]{:S(2)}) collective-permute-start(bf16[64,768]{1,0:T(8,128)(2,1)S(1)} %slice_bitcast_fusion), channel_id=1, source_target_pairs={{0,4},{4,0},{8,12},{12,8},{16,20},{20,16},{24,28},{28,24},{1,5},{5... | collective-permute-start | bytes 294920 | tf_op jit(solution)/shard_map/ppermute | solution.py:327

commit v9 on v8

--- a/solution.py
+++ b/solution.py
@@ -127,7 +127,8 @@
     count = len(distances)
     clip_refs, refs = refs[:count], refs[count:]
     *refs, w_ref, order_ref, out_ref, mix_ref, last_ref = refs
-    qkv_refs, before = (refs[:-1], refs[-1]) if first else (refs, None)
+    before = refs[len(refs) - late - 1 :] if first else []
+    qkv_refs = refs[: len(refs) - len(before)]
     project(clip_refs[count - late :], w_ref, last_ref)
     frames, toks, width = last_ref.shape[2:]
     rows = count * toks
@@ -144,18 +145,23 @@
             cols = pl.ds(p, group)
             mixed = attend(part(0, f, cols), part(1, f, cols), part(2, f, cols), masks, None)
             mix_ref[pl.ds(f * rows, rows), cols] = mixed
-    clip = [
-        own_or_whole(c, f if i >= count - late else first + f)
-        for f in range(frames)
-        for i, c in enumerate(clip_refs)
-    ]
-    after = dot(mix_ref[...], w_ref[3]) + jnp.concatenate(clip, axis=0).astype(F32)
+    if len(out_ref.shape) == 2:
+        out_ref[...] = mix_ref[...]
+        return
+    mix = mix_ref[...]
+    if first:
+        mix = jnp.concatenate([before[0][...], mix], axis=0)
+
+    def block_of(i, f):
+        if i < count - late:
+            return own_or_whole(clip_refs[i], f)
+        if f < first:
+            return before[1 + i - count + late][f]
+        return clip_refs[i][f - first]
+
+    clip = [block_of(i, f) for f in range(first + frames) for i in range(count)]
+    after = dot(mix, w_ref[3]) + jnp.concatenate(clip, axis=0).astype(F32)
     after = after.astype(BF16)
-    if len(out_ref.shape) == 2:
-        out_ref[...] = after
-        return
-    if before is not None:
-        after = jnp.concatenate([before[...], after], axis=0)
     after = dot(order_ref[...], after).astype(BF16).reshape(count, groups, -1, width)
     me = lax.axis_index("space")
     for i, k in enumerate(distances):
@@ -296,6 +302,7 @@
             *ends[c],
             *qkv,
             *before,
+            *(ends[0] if c else []),
             w_spatial,
             leave_space,
             scratch=[

time: 68.9 us -> 69 us (level)
  transfers between devices with their start and end apart: 10 -> 10, of which waited for: 3 -> 3; matrix products, arithmetic and copies ran while one was open for 3% -> 3% of each run, Pallas kernels for 7% -> 6%
where the time goes in v9:
time: 69 us; the launch traced here: 68.6 us
  blocking collectives  27.9 us (40%)
  starting transfers between devices  15.9 us (23%)
  Pallas kernels  13.4 us (19%)
  local copies, waits for them, and re-layouts  7.33 us (11%)
  waiting for transfers between devices  3.95 us (6%)
    all_to_all x1, blocking collectives, on_device(): lax.all_to_all(after, ('space', 'tm'), split_axis=0, concat_axis=0, tiled...  25.8 us
    pallas_call x8, Pallas kernels, call(): pl.pallas_call(kernel, out_shape=like, in_specs=[within] * len(args), out...  13.4 us
    ppermute x4, starting transfers between devices, over_space(): lax.ppermute(part, 'space', [(i, i ^ distance) for i in range(space)])  9.62 us
    ppermute x6, starting transfers between devices, over_tm(): return lax.ppermute(part, 'tm', [(i, i ^ distance) for i in range(tm)])  6.3 us
    unnamed x12, local copies, waits for them, and re-layouts  4.48 us
    ppermute x6, waiting for transfers between devices, over_tm(): return lax.ppermute(part, 'tm', [(i, i ^ distance) for i in range(tm)])  3.26 us
    all_gather x1, blocking collectives, on_device(): beside = [lax.all_gather(whole[0][1], 'tm', axis_index_groups=pairs)]  2.07 us
    squeeze x2, local copies, waits for them, and re-layouts, on_device(): parts[k] = lax.dynamic_index_in_dim(held, me ^ k, 0, keepdims=False)  1.88 us
  transfers between devices with their start and end apart: 10, of which 3 were waited for; matrix products, arithmetic and copies ran while one was open for 3% of the time, Pallas kernels for 6%

profile of v9, /device:TPU:0, one launch (start us, length us, event | category | flops | bytes accessed | tf_op | source)
XLA Modules:
  0.0 68.6 jit_solution(7859822041364727393)
XLA Ops:
  0.0 0.9 %dynamic-slice_bitcast_fusion.1 = bf16[4,32,768]{2,1,0:T(8,128)(2,1)S(1)} fusion(bf16[4,4,32,768]{3,2,1,0:T(8,128)(2,1)} %bitcast.12, s32[]{:T(128)S(6)} %select_n.10), kind=kLoop, calls=%fused_computation.1 | loop fusion | bytes 393220 | tf_op jit(solution)/shard_map/jit(dynamic_index_in_dim)/squeeze | solution.py:262
  0.9 4.1 %collective-permute-start = (bf16[4,32,768]{2,1,0:T(8,128)(2,1)S(1)}, bf16[4,32,768]{2,1,0:T(8,128)(2,1)S(1)}, u32[]{:S(2)}, u32[]{:S(2)}) collective-permute-start(bf16[4,32,768]{2,1,0:T(8,128)(2,1)S(1)} %dynamic-slice_bitcast_fusion.1), channel_id=1, source_target_pairs={{0,2},{1,3},{2,0},{3,1},{4,6},{5,7},{6,4},{7,5},{8,10},{9,11},{10,... | collective-permute-start | bytes 589832 | tf_op jit(solution)/shard_map/ppermute | solution.py:266
  5.0 0.9 %dynamic-slice_bitcast_fusion = bf16[4,32,768]{2,1,0:T(8,128)(2,1)S(1)} fusion(bf16[4,4,32,768]{3,2,1,0:T(8,128)(2,1)} %bitcast.13, s32[]{:T(128)S(6)} %select_n.11), kind=kLoop, calls=%fused_computation | loop fusion | bytes 393220 | tf_op jit(solution)/shard_map/jit(dynamic_index_in_dim)/squeeze | solution.py:262
  6.0 1.6 %collective-permute-start.1 = (bf16[4,32,768]{2,1,0:T(8,128)(2,1)S(1)}, bf16[4,32,768]{2,1,0:T(8,128)(2,1)S(1)}, u32[]{:S(2)}, u32[]{:S(2)}) collective-permute-start(bf16[4,32,768]{2,1,0:T(8,128)(2,1)S(1)} %dynamic-slice_bitcast_fusion), channel_id=1, source_target_pairs={{0,1},{1,0},{2,3},{3,2},{4,5},{5,4},{6,7},{7,6},{8,9},{9,8},{10,11... | collective-permute-start | bytes 589832 | tf_op jit(solution)/shard_map/ppermute | solution.py:266
  7.6 1.0 %dynamic-slice_bitcast_fusion.2 = (bf16[2,32,768]{2,1,0:T(8,128)(2,1)S(1)}, bf16[2,32,768]{2,1,0:T(8,128)(2,1)S(1)}) fusion(bf16[4,4,32,768]{3,2,1,0:T(8,128)(2,1)} %bitcast.14, s32[]{:T(128)S(6)} %select_n.12, s32[]{:T(128)S(6)} %add.13), kind=kLoop, calls=%fused_computation.3 | loop fusion | bytes 393224 | tf_op jit(solution)/shard_map/slice | solution.py:271
  8.6 0.1 collective-permute-start.3
  8.7 3.8 %collective-permute-start.2 = (bf16[2,32,768]{2,1,0:T(8,128)(2,1)S(1)}, bf16[2,32,768]{2,1,0:T(8,128)(2,1)S(1)}, u32[]{:S(2)}, u32[]{:S(2)}) collective-permute-start(bf16[2,32,768]{2,1,0:T(8,128)(2,1)S(1)} %get-tuple-element.28), channel_id=1, source_target_pairs={{0,3},{1,2},{2,1},{3,0},{4,7},{5,6},{6,5},{7,4},{8,11},{9,10},{10,... | collective-permute-start | bytes 294920 | tf_op jit(solution)/shard_map/ppermute | solution.py:266
  12.5 2.3 %copy-done = bf16[4,768,768]{2,1,0:T(8,128)(2,1)S(1)} copy-done((bf16[4,768,768]{2,1,0:T(8,128)(2,1)S(1)}, bf16[4,768,768]{2,1,0:T(8,128)(2,1)}, u32[]{:S(2)}) %copy-start) | copy-done | bytes 4718616
  14.8 1.1 %copy-done.2 = bf16[16,32,768]{2,1,0:T(8,128)(2,1)S(1)} copy-done((bf16[16,32,768]{2,1,0:T(8,128)(2,1)S(1)}, bf16[16,32,768]{2,1,0:T(8,128)(2,1)}, u32[]{:S(2)}) %copy-start.2) | copy-done | bytes 786456
  15.9 0.7 %project.3._.refs_4_ = bf16[3,1,4,32,768]{4,3,2,1,0:T(8,128)(2,1)S(1)} custom-call(bf16[4,4,32,768]{3,2,1,0:T(8,128)(2,1)S(1)} %bitcast.15, bf16[4,768,768]{2,1,0:T(8,128)(2,1)S(1)} %copy-done), custom_call_target="tpu_custom_call" | custom-call | flops 452984832 | bytes 6094848 | tf_op jit(solution)/shard_map/project/pallas_call | solution.py:230
  16.7 0.6 orders.1
  17.3 0.0 copy-start.3
  17.3 1.0 %copy-done.1 = bf16[4,768,768]{2,1,0:T(8,128)(2,1)S(1)} copy-done((bf16[4,768,768]{2,1,0:T(8,128)(2,1)S(1)}, bf16[4,768,768]{2,1,0:T(8,128)(2,1)}, u32[]{:S(2)}) %copy-start.1) | copy-done | bytes 4718616
  18.3 0.7 %project.4.refs_5_ = bf16[3,1,4,32,768]{4,3,2,1,0:T(8,128)(2,1)S(1)} custom-call(bf16[4,32,768]{2,1,0:T(8,128)(2,1)S(1)} %collective-permute-done.refs_0_.refs_1_, bf16[4,768,768]{2,1,0:T(8,128)(2,1)S(1)} %copy-done.1), custom_call_target="tpu_custom_call" | custom-call | flops 452984832 | bytes 5505024 | tf_op jit(solution)/shard_map/project/pallas_call | solution.py:230
  19.0 0.7 %collective-permute-done.1.refs_0_.refs_2_ = bf16[4,32,768]{2,1,0:T(8,128)(2,1)S(1)} collective-permute-done((bf16[4,32,768]{2,1,0:T(8,128)(2,1)S(1)}, bf16[4,32,768]{2,1,0:T(8,128)(2,1)S(1)}, u32[]{:S(2)}, u32[]{:S(2)}) %collective-permute-start.1) | collective-permute-done | bytes 196640 | tf_op jit(solution)/shard_map/ppermute | solution.py:266
  19.7 0.7 %project.5.refs_6_ = bf16[3,1,4,32,768]{4,3,2,1,0:T(8,128)(2,1)S(1)} custom-call(bf16[4,32,768]{2,1,0:T(8,128)(2,1)S(1)} %collective-permute-done.1.refs_0_.refs_2_, bf16[4,768,768]{2,1,0:T(8,128)(2,1)S(1)} %copy-done.1), custom_call_target="tpu_custom_call" | custom-call | flops 452984832 | bytes 5505024 | tf_op jit(solution)/shard_map/project/pallas_call | solution.py:230
  20.4 0.0 slice-start
  20.4 1.7 %spatial.2.refs_7_ = bf16[256,768]{1,0:T(8,128)(2,1)S(1)} custom-call(bf16[4,4,32,768]{3,2,1,0:T(8,128)(2,1)S(1)} %bitcast.16, bf16[4,32,768]{2,1,0:T(8,128)(2,1)S(1)} %collective-permute-done.refs_0_.refs_1_, bf16[4,32,768]{2,1,0:T(8,128)(2,1)S(1)} %collective-permute-done.1.refs_0_.refs_2_, bf16[2,32,768]{2,1,0:T(8,128)(2,1)S(1)} %collective-permute-done.3.refs_3_.refs_8_, ...), custom_call_target="tpu_custom_call" | custom-call | flops 603979776 | bytes 8683520 | tf_op jit(solution)/shard_map/spatial/pallas_call | solution.py:230
  22.1 0.0 slice-start.1
  22.2 2.8 %spatial.3 = bf16[32,16,768]{2,1,0:T(8,128)(2,1)S(1)} custom-call(bf16[4,4,32,768]{3,2,1,0:T(8,128)(2,1)S(1)} %bitcast.17, bf16[4,32,768]{2,1,0:T(8,128)(2,1)S(1)} %collective-permute-done.refs_0_.refs_1_, bf16[4,32,768]{2,1,0:T(8,128)(2,1)S(1)} %collective-permute-done.1.refs_0_.refs_2_, bf16[2,32,768]{2,1,0:T(8,128)(2,1)S(1)} %collective-permute-done.2.refs_3_, ...), custom_call_target="tpu_custom_call" | custom-call | flops 603979776 | bytes 9568256 | tf_op jit(solution)/shard_map/spatial/pallas_call | solution.py:230
  25.0 25.8 %all_to_all.5 = bf16[32,16,768]{2,1,0:T(8,128)(2,1)S(1)} all-to-all(bf16[32,16,768]{2,1,0:T(8,128)(2,1)S(1)} %spatial.3), channel_id=1, replica_groups=mesh['tm'=8,'space'=4] {'space','tm'}, dimensions={0} | all-to-all | bytes 1572864 | tf_op jit(solution)/shard_map/all_to_all | solution.py:315
  50.8 4.9 %temporal.1 = (bf16[2,64,768]{2,1,0:T(8,128)(2,1)S(1)}, bf16[2,64,768]{2,1,0:T(8,128)(2,1)S(1)}, bf16[64,768]{1,0:T(8,128)(2,1)S(1)}, bf16[64,768]{1,0:T(8,128)(...) custom-call(bf16[4,8,16,768]{3,2,1,0:T(8,128)(2,1)S(1)} %bitcast.18, ...), custom_call_target="tpu_custom_call" | custom-call | flops 3019898880 | bytes 6815744 | tf_op jit(solution)/shard_map/temporal/pallas_call | solution.py:230
  55.7 2.5 %collective-permute-start.4 = (bf16[2,64,768]{2,1,0:T(8,128)(2,1)S(1)}, bf16[2,64,768]{2,1,0:T(8,128)(2,1)S(1)}, u32[]{:S(2)}, u32[]{:S(2)}) collective-permute-start(bf16[2,64,768]{2,1,0:T(8,128)(2,1)S(1)} %get-tuple-element.21), channel_id=1, source_target_pairs={{0,24},{4,28},{8,16},{12,20},{16,8},{20,12},{24,0},{28,4},{1,25},{... | collective-permute-start | bytes 589832 | tf_op jit(solution)/shard_map/ppermute | solution.py:334
  58.1 0.5 collective-permute-start.6
  58.7 0.6 collective-permute-start.7
  59.2 0.1 collective-permute-start.8
  59.3 2.6 %collective-permute-start.9 = (bf16[64,768]{1,0:T(8,128)(2,1)S(1)}, bf16[64,768]{1,0:T(8,128)(2,1)S(1)}, u32[]{:S(2)}, u32[]{:S(2)}) collective-permute-start(bf16[64,768]{1,0:T(8,128)(2,1)S(1)} %get-tuple-element.25), channel_id=1, source_target_pairs={{0,12},{4,8},{8,4},{12,0},{16,28},{20,24},{24,20},{28,16},{1,13},{... | collective-permute-start | bytes 294920 | tf_op jit(solution)/shard_map/ppermute | solution.py:334
  61.9 2.6 %collective-permute-done.4.refs_1_ = bf16[2,64,768]{2,1,0:T(8,128)(2,1)S(1)} collective-permute-done((bf16[2,64,768]{2,1,0:T(8,128)(2,1)S(1)}, bf16[2,64,768]{2,1,0:T(8,128)(2,1)S(1)}, u32[]{:S(2)}, u32[]{:S(2)}) %collective-permute-start.4) | collective-permute-done | bytes 196640 | tf_op jit(solution)/shard_map/ppermute | solution.py:334
  64.5 0.1 collective-permute-start.5
  64.6 2.1 %all_gather.3.refs_2_ = bf16[2,64,768]{2,1,0:T(8,128)(2,1)S(1)} all-gather(bf16[1,64,768]{2,1,0:T(8,128)(2,1)S(1)} %slice.22), channel_id=1, replica_groups={{0,4},{8,12},{16,20},{24,28},{1,5},{9,13},{17,21},{25,29},{2,6},{10,14}..., dimensions={0}, use_global_device_ids=true | all-gather | bytes 294912 | tf_op jit(solution)/shard_map/all_gather | solution.py:338
  66.7 0.7 collective-permute-done.8.refs_6_
  67.3 1.3 %place.1 = bf16[16,32,768]{2,1,0:T(8,128)(2,1)} custom-call(bf16[2,64,768]{2,1,0:T(8,128)(2,1)S(1)} %get-tuple-element.20.refs_0_, bf16[2,64,768]{2,1,0:T(8,128)(2,1)S(1)} %collective-permute-done.4.refs_1_, bf16[2,64,768]{2,1,0:T(8,128)(2,1)S(1)} %all_gather.3.refs_2_, bf16[64,768]{1,0:T(8,128)(2,1)S(1)} %collective-permute-done.5.refs_3_, ...), custom_call_target="tpu_custom_call" | custom-call | bytes 2392064 | tf_op jit(solution)/shard_map/place/pallas_call | solution.py:230
  (16 shorter events, 0.0 us)
Async XLA Ops:
  0.9 16.3 %collective-permute-start = (bf16[4,32,768]{2,1,0:T(8,128)(2,1)S(1)}, bf16[4,32,768]{2,1,0:T(8,128)(2,1)S(1)}, u32[]{:S(2)}, u32[]{:S(2)}) collective-permute-start(bf16[4,32,768]{2,1,0:T(8,128)(2,1)S(1)} %dynamic-slice_bitcast_fusion.1), channel_id=1, source_target_pairs={{0,2},{1,3},{2,0},{3,1},{4,6},{5,7},{6,4},{7,5},{8,10},{9,11},{10,... | collective-permute-start | bytes 589832 | tf_op jit(solution)/shard_map/ppermute | solution.py:266
  6.0 13.7 %collective-permute-start.1 = (bf16[4,32,768]{2,1,0:T(8,128)(2,1)S(1)}, bf16[4,32,768]{2,1,0:T(8,128)(2,1)S(1)}, u32[]{:S(2)}, u32[]{:S(2)}) collective-permute-start(bf16[4,32,768]{2,1,0:T(8,128)(2,1)S(1)} %dynamic-slice_bitcast_fusion), channel_id=1, source_target_pairs={{0,1},{1,0},{2,3},{3,2},{4,5},{5,4},{6,7},{7,6},{8,9},{9,8},{10,11... | collective-permute-start | bytes 589832 | tf_op jit(solution)/shard_map/ppermute | solution.py:266
  8.6 11.8 %collective-permute-start.3 = (bf16[2,32,768]{2,1,0:T(8,128)(2,1)S(1)}, bf16[2,32,768]{2,1,0:T(8,128)(2,1)S(1)}, u32[]{:S(2)}, u32[]{:S(2)}) collective-permute-start(bf16[2,32,768]{2,1,0:T(8,128)(2,1)S(1)} %get-tuple-element.27), channel_id=1, source_target_pairs={{0,3},{1,2},{2,1},{3,0},{4,7},{5,6},{6,5},{7,4},{8,11},{9,10},{10,... | collective-permute-start | bytes 294920 | tf_op jit(solution)/shard_map/ppermute | solution.py:266
  8.7 13.5 %collective-permute-start.2 = (bf16[2,32,768]{2,1,0:T(8,128)(2,1)S(1)}, bf16[2,32,768]{2,1,0:T(8,128)(2,1)S(1)}, u32[]{:S(2)}, u32[]{:S(2)}) collective-permute-start(bf16[2,32,768]{2,1,0:T(8,128)(2,1)S(1)} %get-tuple-element.28), channel_id=1, source_target_pairs={{0,3},{1,2},{2,1},{3,0},{4,7},{5,6},{6,5},{7,4},{8,11},{9,10},{10,... | collective-permute-start | bytes 294920 | tf_op jit(solution)/shard_map/ppermute | solution.py:266
  12.5 2.3 %copy-start = (bf16[4,768,768]{2,1,0:T(8,128)(2,1)S(1)}, bf16[4,768,768]{2,1,0:T(8,128)(2,1)}, u32[]{:S(2)}) copy-start(bf16[4,768,768]{2,1,0:T(8,128)(2,1)} %refs_9_.1) | copy-start | bytes 14155780
  14.8 1.1 %copy-start.2 = (bf16[16,32,768]{2,1,0:T(8,128)(2,1)S(1)}, bf16[16,32,768]{2,1,0:T(8,128)(2,1)}, u32[]{:S(2)}) copy-start(bf16[16,32,768]{2,1,0:T(8,128)(2,1)} %param.3) | copy-start | bytes 2359300
  15.9 2.3 %copy-start.1 = (bf16[4,768,768]{2,1,0:T(8,128)(2,1)S(1)}, bf16[4,768,768]{2,1,0:T(8,128)(2,1)}, u32[]{:S(2)}) copy-start(bf16[4,768,768]{2,1,0:T(8,128)(2,1)} %refs_9_.1) | copy-start | bytes 14155780
  17.3 3.1 %copy-start.3 = (bf16[16,32,768]{2,1,0:T(8,128)(2,1)S(1)}, bf16[16,32,768]{2,1,0:T(8,128)(2,1)}, u32[]{:S(2)}) copy-start(bf16[16,32,768]{2,1,0:T(8,128)(2,1)} %param.3) | copy-start | bytes 2359300
  20.4 30.4 %slice-start = ((s8[4718592]{0:T(1024)(128)(4,1)}), s8[4194304]{0:T(1024)(128)(4,1)S(1)}, s32[]{:S(2)}) async-start(s8[4718592]{0:T(1024)(128)(4,1)} %bitcast.19), calls=%async_computation.1 | async-start | bytes 8388608
  22.1 28.6 %slice-start.1 = ((s8[4718592]{0:T(1024)(128)(4,1)}), s8[524288]{0:T(1024)(128)(4,1)S(1)}, s32[]{:S(2)}) async-start(s8[4718592]{0:T(1024)(128)(4,1)} %bitcast.19), calls=%async_computation.2 | async-start | bytes 1048576
  55.7 8.8 %collective-permute-start.4 = (bf16[2,64,768]{2,1,0:T(8,128)(2,1)S(1)}, bf16[2,64,768]{2,1,0:T(8,128)(2,1)S(1)}, u32[]{:S(2)}, u32[]{:S(2)}) collective-permute-start(bf16[2,64,768]{2,1,0:T(8,128)(2,1)S(1)} %get-tuple-element.21), channel_id=1, source_target_pairs={{0,24},{4,28},{8,16},{12,20},{16,8},{20,12},{24,0},{28,4},{1,25},{... | collective-permute-start | bytes 589832 | tf_op jit(solution)/shard_map/ppermute | solution.py:334
  58.1 8.5 %collective-permute-start.6 = (bf16[64,768]{1,0:T(8,128)(2,1)S(1)}, bf16[64,768]{1,0:T(8,128)(2,1)S(1)}, u32[]{:S(2)}, u32[]{:S(2)}) collective-permute-start(bf16[64,768]{1,0:T(8,128)(2,1)S(1)} %get-tuple-element.22), channel_id=1, source_target_pairs={{0,16},{4,20},{8,24},{12,28},{16,0},{20,4},{24,8},{28,12},{1,17},{... | collective-permute-start | bytes 294920 | tf_op jit(solution)/shard_map/ppermute | solution.py:334
  58.7 8.0 %collective-permute-start.7 = (bf16[64,768]{1,0:T(8,128)(2,1)S(1)}, bf16[64,768]{1,0:T(8,128)(2,1)S(1)}, u32[]{:S(2)}, u32[]{:S(2)}) collective-permute-start(bf16[64,768]{1,0:T(8,128)(2,1)S(1)} %get-tuple-element.23), channel_id=1, source_target_pairs={{0,8},{4,12},{8,0},{12,4},{16,24},{20,28},{24,16},{28,20},{1,9},{5... | collective-permute-start | bytes 294920 | tf_op jit(solution)/shard_map/ppermute | solution.py:334
  59.2 8.1 %collective-permute-start.8 = (bf16[64,768]{1,0:T(8,128)(2,1)S(1)}, bf16[64,768]{1,0:T(8,128)(2,1)S(1)}, u32[]{:S(2)}, u32[]{:S(2)}) collective-permute-start(bf16[64,768]{1,0:T(8,128)(2,1)S(1)} %get-tuple-element.24), channel_id=1, source_target_pairs={{0,20},{4,16},{8,28},{12,24},{16,4},{20,0},{24,12},{28,8},{1,21},{... | collective-permute-start | bytes 294920 | tf_op jit(solution)/shard_map/ppermute | solution.py:334
  59.3 8.0 %collective-permute-start.9 = (bf16[64,768]{1,0:T(8,128)(2,1)S(1)}, bf16[64,768]{1,0:T(8,128)(2,1)S(1)}, u32[]{:S(2)}, u32[]{:S(2)}) collective-permute-start(bf16[64,768]{1,0:T(8,128)(2,1)S(1)} %get-tuple-element.25), channel_id=1, source_target_pairs={{0,12},{4,8},{8,4},{12,0},{16,28},{20,24},{24,20},{28,16},{1,13},{... | collective-permute-start | bytes 294920 | tf_op jit(solution)/shard_map/ppermute | solution.py:334
  64.5 2.9 %collective-permute-start.5 = (bf16[64,768]{1,0:T(8,128)(2,1)S(1)}, bf16[64,768]{1,0:T(8,128)(2,1)S(1)}, u32[]{:S(2)}, u32[]{:S(2)}) collective-permute-start(bf16[64,768]{1,0:T(8,128)(2,1)S(1)} %slice_bitcast_fusion), channel_id=1, source_target_pairs={{0,4},{4,0},{8,12},{12,8},{16,20},{20,16},{24,28},{28,24},{1,5},{5... | collective-permute-start | bytes 294920 | tf_op jit(solution)/shard_map/ppermute | solution.py:334

commit v10 on v8

--- a/solution.py
+++ b/solution.py
@@ -200,9 +200,9 @@
     *in_refs, order_ref, out_ref, done_ref, sems = refs
     frames, toks, width = out_ref.shape
     parts = {2 * k: in_refs[i].at[0] for i, k in enumerate(both)}
-    parts |= {2 * k + 1: in_refs[len(both) + i] for i, k in enumerate(both)}
-    parts[1] = parts[1].at[1 - lax.axis_index("tm") % 2]
-    parts |= {k: in_refs[2 * len(both) + i] for i, k in enumerate(direct)}
+    other = in_refs[len(both)].at[1 - lax.axis_index("tm") % 2]
+    parts |= {2 * k + 1: other.at[i] for i, k in enumerate(both)}
+    parts |= {k: in_refs[len(both) + 1 + i] for i, k in enumerate(direct)}
     rows = jnp.concatenate([parts[k][...] for k in range(len(parts))], axis=0)
     steps = sems.shape[0]
     some = frames // steps
@@ -328,10 +328,10 @@
 
     whole = [over_tm(part, 2 * k) if k else part for k, part in zip(both, result)]
     pairs = [[i, i + 1] for i in range(0, tm, 2)]
-    beside = [lax.all_gather(whole[0][1], "tm", axis_index_groups=pairs)]
-    beside += [over_tm(part[1], 1) for part in whole[1:]]
+    beside = jnp.stack([part[1] for part in whole])
+    beside = [lax.all_gather(beside, "tm", axis_index_groups=pairs)]
     near = [over_tm(part, k) for k, part in zip(direct, result[len(both) :])]
-    steps = 4 if frames % 4 == 0 else 1
+    steps = 2 if frames % 2 == 0 else 1
     return call(
         functools.partial(place_kernel, both=both, direct=direct),
         "place",

time: 68.9 us -> 68.9 us (level)
    ppermute x6 -> x5, waiting for transfers between devices: 3.26 us -> 3.24 us  [over_tm(): return lax.ppermute(part, 'tm', [(i, i ^ distance) for i in range(tm)])]
    ppermute x6 -> x5, starting transfers between devices: 6.3 us -> 6.29 us  [over_tm(): return lax.ppermute(part, 'tm', [(i, i ^ distance) for i in range(tm)])]
  transfers between devices with their start and end apart: 10 -> 9, of which waited for: 3 -> 3; matrix products, arithmetic and copies ran while one was open for 3% -> 3% of each run, Pallas kernels for 7% -> 7%
where the time goes in v10:
time: 68.9 us; the launch traced here: 68.6 us
  blocking collectives  27.6 us (40%)
  starting transfers between devices  15.9 us (23%)
  Pallas kernels  13.6 us (20%)
  local copies, waits for them, and re-layouts  7.33 us (11%)
  waiting for transfers between devices  3.93 us (6%)
    all_to_all x1, blocking collectives, on_device(): lax.all_to_all(after, ('space', 'tm'), split_axis=0, concat_axis=0, tiled...  25.5 us
    pallas_call x8, Pallas kernels, call(): pl.pallas_call(kernel, out_shape=like, in_specs=[within] * len(args), out...  13.6 us
    ppermute x4, starting transfers between devices, over_space(): lax.ppermute(part, 'space', [(i, i ^ distance) for i in range(space)])  9.62 us
    ppermute x5, starting transfers between devices, over_tm(): return lax.ppermute(part, 'tm', [(i, i ^ distance) for i in range(tm)])  6.29 us
    unnamed x12, local copies, waits for them, and re-layouts  4.48 us
    ppermute x5, waiting for transfers between devices, over_tm(): return lax.ppermute(part, 'tm', [(i, i ^ distance) for i in range(tm)])  3.24 us
    all_gather x1, blocking collectives, on_device(): beside = [lax.all_gather(beside, 'tm', axis_index_groups=pairs)]  2.09 us
    squeeze x2, local copies, waits for them, and re-layouts, on_device(): parts[k] = lax.dynamic_index_in_dim(held, me ^ k, 0, keepdims=False)  1.88 us
  transfers between devices with their start and end apart: 9, of which 3 were waited for; matrix products, arithmetic and copies ran while one was open for 3% of the time, Pallas kernels for 7%

profile of v10, /device:TPU:0, one launch (start us, length us, event | category | flops | bytes accessed | tf_op | source)
XLA Modules:
  0.0 68.6 jit_solution(2195372721122718894)
XLA Ops:
  0.0 0.9 %dynamic-slice_bitcast_fusion.1 = bf16[4,32,768]{2,1,0:T(8,128)(2,1)S(1)} fusion(bf16[4,4,32,768]{3,2,1,0:T(8,128)(2,1)} %bitcast.11, s32[]{:T(128)S(6)} %select_n.10), kind=kLoop, calls=%fused_computation.2 | loop fusion | bytes 393220 | tf_op jit(solution)/shard_map/jit(dynamic_index_in_dim)/squeeze | solution.py:256
  0.9 4.1 %collective-permute-start = (bf16[4,32,768]{2,1,0:T(8,128)(2,1)S(1)}, bf16[4,32,768]{2,1,0:T(8,128)(2,1)S(1)}, u32[]{:S(2)}, u32[]{:S(2)}) collective-permute-start(bf16[4,32,768]{2,1,0:T(8,128)(2,1)S(1)} %dynamic-slice_bitcast_fusion.1), channel_id=1, source_target_pairs={{0,2},{1,3},{2,0},{3,1},{4,6},{5,7},{6,4},{7,5},{8,10},{9,11},{10,... | collective-permute-start | bytes 589832 | tf_op jit(solution)/shard_map/ppermute | solution.py:260
  5.0 0.9 %dynamic-slice_bitcast_fusion = bf16[4,32,768]{2,1,0:T(8,128)(2,1)S(1)} fusion(bf16[4,4,32,768]{3,2,1,0:T(8,128)(2,1)} %bitcast.12, s32[]{:T(128)S(6)} %select_n.11), kind=kLoop, calls=%fused_computation.1 | loop fusion | bytes 393220 | tf_op jit(solution)/shard_map/jit(dynamic_index_in_dim)/squeeze | solution.py:256
  6.0 1.6 %collective-permute-start.1 = (bf16[4,32,768]{2,1,0:T(8,128)(2,1)S(1)}, bf16[4,32,768]{2,1,0:T(8,128)(2,1)S(1)}, u32[]{:S(2)}, u32[]{:S(2)}) collective-permute-start(bf16[4,32,768]{2,1,0:T(8,128)(2,1)S(1)} %dynamic-slice_bitcast_fusion), channel_id=1, source_target_pairs={{0,1},{1,0},{2,3},{3,2},{4,5},{5,4},{6,7},{7,6},{8,9},{9,8},{10,11... | collective-permute-start | bytes 589832 | tf_op jit(solution)/shard_map/ppermute | solution.py:260
  7.6 1.0 %dynamic-slice_bitcast_fusion.2 = (bf16[2,32,768]{2,1,0:T(8,128)(2,1)S(1)}, bf16[2,32,768]{2,1,0:T(8,128)(2,1)S(1)}) fusion(bf16[4,4,32,768]{3,2,1,0:T(8,128)(2,1)} %bitcast.13, s32[]{:T(128)S(6)} %select_n.12, s32[]{:T(128)S(6)} %add.13), kind=kLoop, calls=%fused_computation.3 | loop fusion | bytes 393224 | tf_op jit(solution)/shard_map/slice | solution.py:265
  8.6 0.1 collective-permute-start.3
  8.7 3.8 %collective-permute-start.2 = (bf16[2,32,768]{2,1,0:T(8,128)(2,1)S(1)}, bf16[2,32,768]{2,1,0:T(8,128)(2,1)S(1)}, u32[]{:S(2)}, u32[]{:S(2)}) collective-permute-start(bf16[2,32,768]{2,1,0:T(8,128)(2,1)S(1)} %get-tuple-element.28), channel_id=1, source_target_pairs={{0,3},{1,2},{2,1},{3,0},{4,7},{5,6},{6,5},{7,4},{8,11},{9,10},{10,... | collective-permute-start | bytes 294920 | tf_op jit(solution)/shard_map/ppermute | solution.py:260
  12.5 2.3 %copy-done = bf16[4,768,768]{2,1,0:T(8,128)(2,1)S(1)} copy-done((bf16[4,768,768]{2,1,0:T(8,128)(2,1)S(1)}, bf16[4,768,768]{2,1,0:T(8,128)(2,1)}, u32[]{:S(2)}) %copy-start) | copy-done | bytes 4718616
  14.8 1.1 %copy-done.2 = bf16[16,32,768]{2,1,0:T(8,128)(2,1)S(1)} copy-done((bf16[16,32,768]{2,1,0:T(8,128)(2,1)S(1)}, bf16[16,32,768]{2,1,0:T(8,128)(2,1)}, u32[]{:S(2)}) %copy-start.2) | copy-done | bytes 786456
  15.9 0.7 %project.3._.refs_4_ = bf16[3,1,4,32,768]{4,3,2,1,0:T(8,128)(2,1)S(1)} custom-call(bf16[4,4,32,768]{3,2,1,0:T(8,128)(2,1)S(1)} %bitcast.14, bf16[4,768,768]{2,1,0:T(8,128)(2,1)S(1)} %copy-done), custom_call_target="tpu_custom_call" | custom-call | flops 452984832 | bytes 6094848 | tf_op jit(solution)/shard_map/project/pallas_call | solution.py:224
  16.7 0.6 orders.1
  17.3 0.0 copy-start.3
  17.3 0.0 collective-permute-done.refs_0_.refs_1_
  17.3 1.0 %copy-done.1 = bf16[4,768,768]{2,1,0:T(8,128)(2,1)S(1)} copy-done((bf16[4,768,768]{2,1,0:T(8,128)(2,1)S(1)}, bf16[4,768,768]{2,1,0:T(8,128)(2,1)}, u32[]{:S(2)}) %copy-start.1) | copy-done | bytes 4718616
  18.3 0.7 %project.4.refs_5_ = bf16[3,1,4,32,768]{4,3,2,1,0:T(8,128)(2,1)S(1)} custom-call(bf16[4,32,768]{2,1,0:T(8,128)(2,1)S(1)} %collective-permute-done.refs_0_.refs_1_, bf16[4,768,768]{2,1,0:T(8,128)(2,1)S(1)} %copy-done.1), custom_call_target="tpu_custom_call" | custom-call | flops 452984832 | bytes 5505024 | tf_op jit(solution)/shard_map/project/pallas_call | solution.py:224
  19.0 0.7 %collective-permute-done.1.refs_0_.refs_2_ = bf16[4,32,768]{2,1,0:T(8,128)(2,1)S(1)} collective-permute-done((bf16[4,32,768]{2,1,0:T(8,128)(2,1)S(1)}, bf16[4,32,768]{2,1,0:T(8,128)(2,1)S(1)}, u32[]{:S(2)}, u32[]{:S(2)}) %collective-permute-start.1) | collective-permute-done | bytes 196640 | tf_op jit(solution)/shard_map/ppermute | solution.py:260
  19.7 0.7 %project.5.refs_6_ = bf16[3,1,4,32,768]{4,3,2,1,0:T(8,128)(2,1)S(1)} custom-call(bf16[4,32,768]{2,1,0:T(8,128)(2,1)S(1)} %collective-permute-done.1.refs_0_.refs_2_, bf16[4,768,768]{2,1,0:T(8,128)(2,1)S(1)} %copy-done.1), custom_call_target="tpu_custom_call" | custom-call | flops 452984832 | bytes 5505024 | tf_op jit(solution)/shard_map/project/pallas_call | solution.py:224
  20.4 0.0 slice-start
  20.4 2.2 %spatial.2.refs_7_ = bf16[256,768]{1,0:T(8,128)(2,1)S(1)} custom-call(bf16[4,4,32,768]{3,2,1,0:T(8,128)(2,1)S(1)} %bitcast.15, bf16[4,32,768]{2,1,0:T(8,128)(2,1)S(1)} %collective-permute-done.refs_0_.refs_1_, bf16[4,32,768]{2,1,0:T(8,128)(2,1)S(1)} %collective-permute-done.1.refs_0_.refs_2_, bf16[2,32,768]{2,1,0:T(8,128)(2,1)S(1)} %collective-permute-done.3.refs_3_, ...), custom_call_target="tpu_custom_call" | custom-call | flops 603979776 | bytes 8683520 | tf_op jit(solution)/shard_map/spatial/pallas_call | solution.py:224
  22.6 0.0 slice-start.1
  22.7 2.4 %spatial.3 = bf16[32,16,768]{2,1,0:T(8,128)(2,1)S(1)} custom-call(bf16[4,4,32,768]{3,2,1,0:T(8,128)(2,1)S(1)} %bitcast.16, bf16[4,32,768]{2,1,0:T(8,128)(2,1)S(1)} %collective-permute-done.refs_0_.refs_1_, bf16[4,32,768]{2,1,0:T(8,128)(2,1)S(1)} %collective-permute-done.1.refs_0_.refs_2_, bf16[2,32,768]{2,1,0:T(8,128)(2,1)S(1)} %collective-permute-done.2.refs_3_, ...), custom_call_target="tpu_custom_call" | custom-call | flops 603979776 | bytes 9469952 | tf_op jit(solution)/shard_map/spatial/pallas_call | solution.py:224
  25.1 25.5 %all_to_all.5 = bf16[32,16,768]{2,1,0:T(8,128)(2,1)S(1)} all-to-all(bf16[32,16,768]{2,1,0:T(8,128)(2,1)S(1)} %spatial.3), channel_id=1, replica_groups=mesh['tm'=8,'space'=4] {'space','tm'}, dimensions={0} | all-to-all | bytes 1572864 | tf_op jit(solution)/shard_map/all_to_all | solution.py:308
  50.6 4.9 %temporal.1 = (bf16[2,64,768]{2,1,0:T(8,128)(2,1)S(1)}, bf16[2,64,768]{2,1,0:T(8,128)(2,1)S(1)}, bf16[64,768]{1,0:T(8,128)(2,1)S(1)}, bf16[64,768]{1,0:T(8,128)(...) custom-call(bf16[4,8,16,768]{3,2,1,0:T(8,128)(2,1)S(1)} %bitcast.18, ...), custom_call_target="tpu_custom_call" | custom-call | flops 3019898880 | bytes 6815744 | tf_op jit(solution)/shard_map/temporal/pallas_call | solution.py:224
  55.6 2.5 %collective-permute-start.4 = (bf16[2,64,768]{2,1,0:T(8,128)(2,1)S(1)}, bf16[2,64,768]{2,1,0:T(8,128)(2,1)S(1)}, u32[]{:S(2)}, u32[]{:S(2)}) collective-permute-start(bf16[2,64,768]{2,1,0:T(8,128)(2,1)S(1)} %get-tuple-element.21), channel_id=1, source_target_pairs={{0,24},{4,28},{8,16},{12,20},{16,8},{20,12},{24,0},{28,4},{1,25},{... | collective-permute-start | bytes 589832 | tf_op jit(solution)/shard_map/ppermute | solution.py:327
  58.0 0.6 collective-permute-start.5
  58.6 0.6 collective-permute-start.6
  59.2 0.1 collective-permute-start.7
  59.2 2.6 %collective-permute-start.8 = (bf16[64,768]{1,0:T(8,128)(2,1)S(1)}, bf16[64,768]{1,0:T(8,128)(2,1)S(1)}, u32[]{:S(2)}, u32[]{:S(2)}) collective-permute-start(bf16[64,768]{1,0:T(8,128)(2,1)S(1)} %get-tuple-element.25), channel_id=1, source_target_pairs={{0,12},{4,8},{8,4},{12,0},{16,28},{20,24},{24,20},{28,16},{1,13},{... | collective-permute-start | bytes 294920 | tf_op jit(solution)/shard_map/ppermute | solution.py:327
  61.9 2.5 %collective-permute-done.4.refs_1_ = bf16[2,64,768]{2,1,0:T(8,128)(2,1)S(1)} collective-permute-done((bf16[2,64,768]{2,1,0:T(8,128)(2,1)S(1)}, bf16[2,64,768]{2,1,0:T(8,128)(2,1)S(1)}, u32[]{:S(2)}, u32[]{:S(2)}) %collective-permute-start.4) | collective-permute-done | bytes 196640 | tf_op jit(solution)/shard_map/ppermute | solution.py:327
  64.4 2.1 %all-gather = bf16[4,64,768]{2,1,0:T(8,128)(2,1)S(1)} all-gather(bf16[2,64,768]{2,1,0:T(8,128)(2,1)S(1)} %pad_maximum_fusion), channel_id=2, replica_groups={{0,4},{8,12},{16,20},{24,28},{1,5},{9,13},{17,21},{25,29},{2,6},{10,14}..., dimensions={0}, use_global_device_ids=true | all-gather | bytes 589824 | tf_op jit(solution)/shard_map/all_gather | solution.py:332
  66.5 0.7 %collective-permute-done.7.refs_5_ = bf16[64,768]{1,0:T(8,128)(2,1)S(1)} collective-permute-done((bf16[64,768]{1,0:T(8,128)(2,1)S(1)}, bf16[64,768]{1,0:T(8,128)(2,1)S(1)}, u32[]{:S(2)}, u32[]{:S(2)}) %collective-permute-start.7) | collective-permute-done | bytes 98336 | tf_op jit(solution)/shard_map/ppermute | solution.py:327
  67.2 1.3 %place.1 = bf16[16,32,768]{2,1,0:T(8,128)(2,1)} custom-call(bf16[2,64,768]{2,1,0:T(8,128)(2,1)S(1)} %get-tuple-element.20.refs_0_, bf16[2,64,768]{2,1,0:T(8,128)(2,1)S(1)} %collective-permute-done.4.refs_1_, bf16[2,2,64,768]{3,2,1,0:T(8,128)(2,1)S(1)} %bitcast.17, bf16[64,768]{1,0:T(8,128)(2,1)S(1)} %collective-permute-done.5.refs_3_, ...), custom_call_target="tpu_custom_call" | custom-call | bytes 2490368 | tf_op jit(solution)/shard_map/place/pallas_call | solution.py:224
  (15 shorter events, 0.1 us)
Async XLA Ops:
  0.9 16.3 %collective-permute-start = (bf16[4,32,768]{2,1,0:T(8,128)(2,1)S(1)}, bf16[4,32,768]{2,1,0:T(8,128)(2,1)S(1)}, u32[]{:S(2)}, u32[]{:S(2)}) collective-permute-start(bf16[4,32,768]{2,1,0:T(8,128)(2,1)S(1)} %dynamic-slice_bitcast_fusion.1), channel_id=1, source_target_pairs={{0,2},{1,3},{2,0},{3,1},{4,6},{5,7},{6,4},{7,5},{8,10},{9,11},{10,... | collective-permute-start | bytes 589832 | tf_op jit(solution)/shard_map/ppermute | solution.py:260
  6.0 13.7 %collective-permute-start.1 = (bf16[4,32,768]{2,1,0:T(8,128)(2,1)S(1)}, bf16[4,32,768]{2,1,0:T(8,128)(2,1)S(1)}, u32[]{:S(2)}, u32[]{:S(2)}) collective-permute-start(bf16[4,32,768]{2,1,0:T(8,128)(2,1)S(1)} %dynamic-slice_bitcast_fusion), channel_id=1, source_target_pairs={{0,1},{1,0},{2,3},{3,2},{4,5},{5,4},{6,7},{7,6},{8,9},{9,8},{10,11... | collective-permute-start | bytes 589832 | tf_op jit(solution)/shard_map/ppermute | solution.py:260
  8.6 11.8 %collective-permute-start.3 = (bf16[2,32,768]{2,1,0:T(8,128)(2,1)S(1)}, bf16[2,32,768]{2,1,0:T(8,128)(2,1)S(1)}, u32[]{:S(2)}, u32[]{:S(2)}) collective-permute-start(bf16[2,32,768]{2,1,0:T(8,128)(2,1)S(1)} %get-tuple-element.27), channel_id=1, source_target_pairs={{0,3},{1,2},{2,1},{3,0},{4,7},{5,6},{6,5},{7,4},{8,11},{9,10},{10,... | collective-permute-start | bytes 294920 | tf_op jit(solution)/shard_map/ppermute | solution.py:260
  8.7 14.0 %collective-permute-start.2 = (bf16[2,32,768]{2,1,0:T(8,128)(2,1)S(1)}, bf16[2,32,768]{2,1,0:T(8,128)(2,1)S(1)}, u32[]{:S(2)}, u32[]{:S(2)}) collective-permute-start(bf16[2,32,768]{2,1,0:T(8,128)(2,1)S(1)} %get-tuple-element.28), channel_id=1, source_target_pairs={{0,3},{1,2},{2,1},{3,0},{4,7},{5,6},{6,5},{7,4},{8,11},{9,10},{10,... | collective-permute-start | bytes 294920 | tf_op jit(solution)/shard_map/ppermute | solution.py:260
  12.5 2.3 %copy-start = (bf16[4,768,768]{2,1,0:T(8,128)(2,1)S(1)}, bf16[4,768,768]{2,1,0:T(8,128)(2,1)}, u32[]{:S(2)}) copy-start(bf16[4,768,768]{2,1,0:T(8,128)(2,1)} %refs_8_.1) | copy-start | bytes 14155780
  14.8 1.1 %copy-start.2 = (bf16[16,32,768]{2,1,0:T(8,128)(2,1)S(1)}, bf16[16,32,768]{2,1,0:T(8,128)(2,1)}, u32[]{:S(2)}) copy-start(bf16[16,32,768]{2,1,0:T(8,128)(2,1)} %param.3) | copy-start | bytes 2359300
  15.9 2.3 %copy-start.1 = (bf16[4,768,768]{2,1,0:T(8,128)(2,1)S(1)}, bf16[4,768,768]{2,1,0:T(8,128)(2,1)}, u32[]{:S(2)}) copy-start(bf16[4,768,768]{2,1,0:T(8,128)(2,1)} %refs_8_.1) | copy-start | bytes 14155780
  17.3 3.1 %copy-start.3 = (bf16[16,32,768]{2,1,0:T(8,128)(2,1)S(1)}, bf16[16,32,768]{2,1,0:T(8,128)(2,1)}, u32[]{:S(2)}) copy-start(bf16[16,32,768]{2,1,0:T(8,128)(2,1)} %param.3) | copy-start | bytes 2359300
  20.4 30.2 %slice-start = ((s8[4718592]{0:T(1024)(128)(4,1)}), s8[4194304]{0:T(1024)(128)(4,1)S(1)}, s32[]{:S(2)}) async-start(s8[4718592]{0:T(1024)(128)(4,1)} %bitcast.19), calls=%async_computation.1 | async-start | bytes 8388608
  22.6 28.0 %slice-start.1 = ((s8[4718592]{0:T(1024)(128)(4,1)}), s8[524288]{0:T(1024)(128)(4,1)S(1)}, s32[]{:S(2)}) async-start(s8[4718592]{0:T(1024)(128)(4,1)} %bitcast.19), calls=%async_computation.2 | async-start | bytes 1048576
  55.6 8.8 %collective-permute-start.4 = (bf16[2,64,768]{2,1,0:T(8,128)(2,1)S(1)}, bf16[2,64,768]{2,1,0:T(8,128)(2,1)S(1)}, u32[]{:S(2)}, u32[]{:S(2)}) collective-permute-start(bf16[2,64,768]{2,1,0:T(8,128)(2,1)S(1)} %get-tuple-element.21), channel_id=1, source_target_pairs={{0,24},{4,28},{8,16},{12,20},{16,8},{20,12},{24,0},{28,4},{1,25},{... | collective-permute-start | bytes 589832 | tf_op jit(solution)/shard_map/ppermute | solution.py:327
  58.0 8.5 %collective-permute-start.5 = (bf16[64,768]{1,0:T(8,128)(2,1)S(1)}, bf16[64,768]{1,0:T(8,128)(2,1)S(1)}, u32[]{:S(2)}, u32[]{:S(2)}) collective-permute-start(bf16[64,768]{1,0:T(8,128)(2,1)S(1)} %get-tuple-element.22), channel_id=1, source_target_pairs={{0,16},{4,20},{8,24},{12,28},{16,0},{20,4},{24,8},{28,12},{1,17},{... | collective-permute-start | bytes 294920 | tf_op jit(solution)/shard_map/ppermute | solution.py:327
  58.6 7.9 %collective-permute-start.6 = (bf16[64,768]{1,0:T(8,128)(2,1)S(1)}, bf16[64,768]{1,0:T(8,128)(2,1)S(1)}, u32[]{:S(2)}, u32[]{:S(2)}) collective-permute-start(bf16[64,768]{1,0:T(8,128)(2,1)S(1)} %get-tuple-element.23), channel_id=1, source_target_pairs={{0,8},{4,12},{8,0},{12,4},{16,24},{20,28},{24,16},{28,20},{1,9},{5... | collective-permute-start | bytes 294920 | tf_op jit(solution)/shard_map/ppermute | solution.py:327
  59.2 8.0 %collective-permute-start.7 = (bf16[64,768]{1,0:T(8,128)(2,1)S(1)}, bf16[64,768]{1,0:T(8,128)(2,1)S(1)}, u32[]{:S(2)}, u32[]{:S(2)}) collective-permute-start(bf16[64,768]{1,0:T(8,128)(2,1)S(1)} %get-tuple-element.24), channel_id=1, source_target_pairs={{0,20},{4,16},{8,28},{12,24},{16,4},{20,0},{24,12},{28,8},{1,21},{... | collective-permute-start | bytes 294920 | tf_op jit(solution)/shard_map/ppermute | solution.py:327
  59.2 8.0 %collective-permute-start.8 = (bf16[64,768]{1,0:T(8,128)(2,1)S(1)}, bf16[64,768]{1,0:T(8,128)(2,1)S(1)}, u32[]{:S(2)}, u32[]{:S(2)}) collective-permute-start(bf16[64,768]{1,0:T(8,128)(2,1)S(1)} %get-tuple-element.25), channel_id=1, source_target_pairs={{0,12},{4,8},{8,4},{12,0},{16,28},{20,24},{24,20},{28,16},{1,13},{... | collective-permute-start | bytes 294920 | tf_op jit(solution)/shard_map/ppermute | solution.py:327
